TPU v7x, 256 devices: a whole 4x4x8 slice. The times are simulated.
256 devices in a mesh: dp: 256 (over x, y, z, core).
Axes of the slice: x: 4, y: 4, z: 8, core: 2. Of those that a mesh axis runs over, the one named last changes fastest.
Arguments:
- image_emb: float32 [65536, 1280], P('dp'), may hold values from -50 to 50
- text_emb: float32 [65536, 1280], P('dp'), may hold values from -50 to 50
- logit_scale: float32 [], replicated, may hold values from 2 to 4
Outputs:
- loss: float32 [], replicated
- image_grad: float32 [65536, 1280], P('dp')
- text_grad: float32 [65536, 1280], P('dp')
- scale_grad: float32 [], replicated
All inputs are finite; a program needn't handle non-finite values.
Results may differ from a plain program's by a relative error of at most 0.0003.
Values sent between devices are 32-bit elements; how exact they have to be, the bound alone decides.
No kernel may reach another device: no remote copies, remote signals or barrier semaphores. Data moves between devices by JAX's collectives and lax.ppermute only.
A program may use at most 64 MiB of HBM per device.

v0:
```python
import jax
import jax.numpy as jnp
from jax import lax
from jax.sharding import PartitionSpec as P

WIN = 8


precise = lax.Precision.HIGHEST


def from_behind(value, axis, steps):
    count = lax.axis_size(axis)
    pairs = [(source, (source + steps) % count) for source in range(count)]
    return lax.ppermute(value, axis, pairs)


def absorb(running, logits, reduce_dim):
    top_old, total_old = running
    top_new = jnp.maximum(top_old, jnp.max(logits, axis=reduce_dim))
    widened = jnp.expand_dims(top_new, reduce_dim)
    total_new = total_old * jnp.exp(top_old - top_new) + jnp.sum(
        jnp.exp(logits - widened), axis=reduce_dim
    )
    return (top_new, total_new)


def finish(running):
    return running[0] + jnp.log(running[1])


def on_device(image_emb, text_emb, logit_scale):
    row_count = image_emb.shape[0]
    devices = lax.axis_size("dp")
    lower_reach = WIN // 2 - 1
    upper_reach = WIN // 2
    identity = jnp.eye(row_count, dtype=jnp.float32)
    start_stats = (
        jnp.full((row_count,), -jnp.inf, jnp.float32),
        jnp.zeros((row_count,), jnp.float32),
    )

    def scores(text_block):
        return logit_scale * lax.dot_general(
            image_emb,
            text_block,
            (((1,), (1,)), ((), ())),
            precision=precise,
            preferred_element_type=jnp.float32,
        )

    row_stats = start_stats
    text_block = from_behind(text_emb, "dp", lower_reach)
    column_stats = start_stats
    for visit_index in range(WIN):
        logits = scores(text_block)
        row_stats = absorb(row_stats, logits, 1)
        column_stats = absorb(column_stats, logits, 0)
        if visit_index == lower_reach:
            diagonal = jnp.diagonal(logits)
        if visit_index < WIN - 1:
            text_block, column_top, column_total = from_behind(
                (text_block, column_stats[0], column_stats[1]), "dp", -1
            )
            column_stats = (column_top, column_total)
    column_stats = from_behind((column_stats[0], column_stats[1]), "dp", upper_reach)
    row_lse = finish(row_stats)
    column_lse = finish(column_stats)
    loss_part = jnp.sum(row_lse) + jnp.sum(column_lse) - 2.0 * jnp.sum(diagonal)
    image_acc = jnp.zeros_like(image_emb)
    scale_acc = jnp.zeros((), jnp.float32)
    text_acc = jnp.zeros_like(text_emb)
    text_block, block_lse = from_behind((text_emb, column_lse), "dp", lower_reach)
    for visit_index in range(WIN):
        contribute_logits = scores(text_block)
        weights = jnp.exp(contribute_logits - row_lse[:, None]) + jnp.exp(
            contribute_logits - block_lse[None, :]
        )
        if visit_index == lower_reach:
            weights = weights - 2.0 * identity
        image_part = jnp.dot(
            weights, text_block, precision=precise, preferred_element_type=jnp.float32
        )
        text_part = lax.dot_general(
            weights,
            image_emb,
            (((0,), (0,)), ((), ())),
            precision=precise,
            preferred_element_type=jnp.float32,
        )
        image_part, text_part, scale_part = (
            image_part,
            text_part,
            jnp.sum(weights * contribute_logits),
        )
        image_acc = image_acc + image_part
        text_acc = text_acc + text_part
        scale_acc = scale_acc + scale_part
        if visit_index < WIN - 1:
            text_block, block_lse, text_acc = from_behind(
                (text_block, block_lse, text_acc), "dp", -1
            )
    text_grad = from_behind(text_acc, "dp", upper_reach)
    loss_total, scale_total = lax.psum((loss_part, scale_acc), "dp")
    total_rows = row_count * devices
    half_scale = 0.5 * logit_scale
    loss_value = loss_total / (2.0 * total_rows)
    scale_grad = scale_total / (2.0 * total_rows * logit_scale)
    return (loss_value, half_scale * image_acc, half_scale * text_grad, scale_grad)


def solution(mesh):
    in_specs = (P("dp", None), P("dp", None), P())
    out_specs = (P(), P("dp", None), P("dp", None), P())
    return jax.shard_map(
        on_device, mesh=mesh, in_specs=in_specs, out_specs=out_specs, check_vma=False
    )
```

profile of v0, /device:TPU:8, one launch (start us, length us, event | category | flops | bytes accessed | tf_op | source)
XLA Modules:
  0.0 585.2 jit_solution(10402992076979356957)
XLA Ops:
  2.1 44.9 %collective-permute-done = f32[256,1280]{1,0:T(8,128)S(1)} collective-permute-done((f32[256,1280]{1,0:T(8,128)}, f32[256,1280]{1,0:T(8,128)S(1)}, u32[]{:S(2)}, u32[]{:S(2)}) %collective-permute-start) | collective-permute-done | bytes 1310752 | tf_op jit(solution)/shard_map/ppermute | solution.py:15
  49.1 15.1 %collective-permute-done.1 = f32[256,1280]{1,0:T(8,128)S(1)} collective-permute-done((f32[256,1280]{1,0:T(8,128)S(1)}, f32[256,1280]{1,0:T(8,128)S(1)}, u32[]{:S(2)}, u32[]{:S(2)}) %collective-permute-start.1) | collective-permute-done | bytes 1310752 | tf_op jit(solution)/shard_map/ppermute | solution.py:15
  64.3 4.0 collective-permute-start.2
  68.3 15.1 %collective-permute-done.2 = f32[256,1280]{1,0:T(8,128)S(1)} collective-permute-done((f32[256,1280]{1,0:T(8,128)S(1)}, f32[256,1280]{1,0:T(8,128)S(1)}, u32[]{:S(2)}, u32[]{:S(2)}) %collective-permute-start.2) | collective-permute-done | bytes 1310752 | tf_op jit(solution)/shard_map/ppermute | solution.py:15
  83.4 4.0 collective-permute-start.3
  87.4 15.1 %collective-permute-done.3 = f32[256,1280]{1,0:T(8,128)S(1)} collective-permute-done((f32[256,1280]{1,0:T(8,128)S(1)}, f32[256,1280]{1,0:T(8,128)S(1)}, u32[]{:S(2)}, u32[]{:S(2)}) %collective-permute-start.3) | collective-permute-done | bytes 1310752 | tf_op jit(solution)/shard_map/ppermute | solution.py:15
  102.5 4.0 collective-permute-start.4
  106.6 15.1 %collective-permute-done.4 = f32[256,1280]{1,0:T(8,128)S(1)} collective-permute-done((f32[256,1280]{1,0:T(8,128)S(1)}, f32[256,1280]{1,0:T(8,128)S(1)}, u32[]{:S(2)}, u32[]{:S(2)}) %collective-permute-start.4) | collective-permute-done | bytes 1310752 | tf_op jit(solution)/shard_map/ppermute | solution.py:15
  122.7 4.0 collective-permute-start.5
  126.8 15.1 %collective-permute-done.5 = f32[256,1280]{1,0:T(8,128)} collective-permute-done((f32[256,1280]{1,0:T(8,128)S(1)}, f32[256,1280]{1,0:T(8,128)}, u32[]{:S(2)}, u32[]{:S(2)}) %collective-permute-start.5) | collective-permute-done | bytes 1310752 | tf_op jit(solution)/shard_map/ppermute | solution.py:15
  141.9 4.1 collective-permute-start.6
  149.8 11.7 %collective-permute-done.8 = f32[256]{0:T(256)S(1)} collective-permute-done((f32[256]{0:T(256)S(1)}, f32[256]{0:T(256)S(1)}, u32[]{:S(2)}, u32[]{:S(2)}) %collective-permute-start.8) | collective-permute-done | bytes 1056 | tf_op jit(solution)/shard_map/ppermute | solution.py:15
  161.5 4.0 collective-permute-start.9
  167.2 3.4 collective-permute-start.10
  171.9 9.3 %collective-permute-done.10 = f32[256]{0:T(256)S(1)} collective-permute-done((f32[256]{0:T(256)S(1)}, f32[256]{0:T(256)S(1)}, u32[]{:S(2)}, u32[]{:S(2)}) %collective-permute-start.10) | collective-permute-done | bytes 1056 | tf_op jit(solution)/shard_map/ppermute | solution.py:15
  181.2 4.0 collective-permute-start.11
  186.5 3.8 collective-permute-start.12
  204.0 3.8 collective-permute-start.18
  209.1 3.8 collective-permute-start.19
  214.2 3.8 collective-permute-start.20
  219.3 3.8 collective-permute-start.21
  224.4 3.8 collective-permute-start.22
  229.6 6.6 %collective-permute-done.23 = f32[256]{0:T(256)S(1)} collective-permute-done((f32[256]{0:T(256)S(1)}, f32[256]{0:T(256)S(1)}, u32[]{:S(2)}, u32[]{:S(2)}) %collective-permute-start.23) | collective-permute-done | bytes 1056 | tf_op jit(solution)/shard_map/ppermute | solution.py:15
  237.4 5.4 collective-permute-done.24
  244.1 5.2 collective-permute-start.32
  249.2 4.7 collective-permute-start.25
  253.9 10.5 %collective-permute-done.25 = f32[256]{0:T(256)S(1)} collective-permute-done((f32[256]{0:T(256)S(1)}, f32[256]{0:T(256)S(1)}, u32[]{:S(2)}, u32[]{:S(2)}) %collective-permute-start.25) | collective-permute-done | bytes 1056 | tf_op jit(solution)/shard_map/ppermute | solution.py:15
  265.7 4.3 collective-permute-start.33
  270.0 7.6 %collective-permute-start.26 = (f32[256]{0:T(256)S(1)}, f32[256]{0:T(256)S(1)}, u32[]{:S(2)}, u32[]{:S(2)}) collective-permute-start(f32[256]{0:T(256)S(1)} %collective-permute-done.25), channel_id=1, source_target_pairs={{0,255},{1,0},{2,1},{3,2},{4,3},{5,4},{6,5},{7,6},{8,7},{9,8},{10,... | collective-permute-start | bytes 3080 | tf_op jit(solution)/shard_map/ppermute | solution.py:15
  277.6 7.5 %collective-permute-done.26 = f32[256]{0:T(256)S(1)} collective-permute-done((f32[256]{0:T(256)S(1)}, f32[256]{0:T(256)S(1)}, u32[]{:S(2)}, u32[]{:S(2)}) %collective-permute-start.26) | collective-permute-done | bytes 1056 | tf_op jit(solution)/shard_map/ppermute | solution.py:15
  286.5 4.1 collective-permute-start.34
  290.6 5.5 collective-permute-start.27
  296.1 9.6 %collective-permute-done.27 = f32[256]{0:T(256)S(1)} collective-permute-done((f32[256]{0:T(256)S(1)}, f32[256]{0:T(256)S(1)}, u32[]{:S(2)}, u32[]{:S(2)}) %collective-permute-start.27) | collective-permute-done | bytes 1056 | tf_op jit(solution)/shard_map/ppermute | solution.py:15
  307.1 4.1 collective-permute-start.35
  311.2 3.4 collective-permute-start.28
  314.6 11.8 %collective-permute-done.28 = f32[256]{0:T(256)S(1)} collective-permute-done((f32[256]{0:T(256)S(1)}, f32[256]{0:T(256)S(1)}, u32[]{:S(2)}, u32[]{:S(2)}) %collective-permute-start.28) | collective-permute-done | bytes 1056 | tf_op jit(solution)/shard_map/ppermute | solution.py:15
  327.7 4.1 collective-permute-start.36
  333.1 13.9 %collective-permute-done.29 = f32[256]{0:T(256)S(1)} collective-permute-done((f32[256]{0:T(256)S(1)}, f32[256]{0:T(256)S(1)}, u32[]{:S(2)}, u32[]{:S(2)}) %collective-permute-start.29) | collective-permute-done | bytes 1056 | tf_op jit(solution)/shard_map/ppermute | solution.py:15
  348.4 4.1 collective-permute-start.37
  352.8 14.9 %collective-permute-done.30 = f32[256]{0:T(256)S(1)} collective-permute-done((f32[256]{0:T(256)S(1)}, f32[256]{0:T(256)S(1)}, u32[]{:S(2)}, u32[]{:S(2)}) %collective-permute-start.30) | collective-permute-done | bytes 1056 | tf_op jit(solution)/shard_map/ppermute | solution.py:15
  370.0 4.0 collective-permute-start.38
  379.1 2.7 fusion.2
  385.8 3.7 collective-permute-done.31
  389.5 3.7 convolution_add_fusion
  394.8 3.7 convolution_add_fusion.8
  404.8 4.1 convolution_add_fusion.7
  408.9 165.8 %all-reduce = (f32[]{:T(128)}, f32[]{:T(128)}) all-reduce(f32[]{:T(128)S(6)} %sub.376, f32[]{:T(128)S(6)} %add.235), channel_id=1, replica_groups=mesh['dp'=256] {'dp'}, use_global_device_ids=true, to_apply=%region_35.36 | all-reduce | flops 2 | bytes 16 | tf_op jit(solution)/shard_map/psum | solution.py:104
  576.0 4.1 fusion
  (118 shorter events, 57.7 us)
Async XLA Ops:
  0.6 146.0 %copy-start = (f32[256,1280]{1,0:T(8,128)S(1)}, f32[256,1280]{1,0:T(8,128)}, u32[]{:S(2)}) copy-start(f32[256,1280]{1,0:T(8,128)} %param.3) | copy-start | bytes 3932164
  0.6 46.3 %collective-permute-start = (f32[256,1280]{1,0:T(8,128)}, f32[256,1280]{1,0:T(8,128)S(1)}, u32[]{:S(2)}, u32[]{:S(2)}) collective-permute-start(f32[256,1280]{1,0:T(8,128)} %param.4), channel_id=1, source_target_pairs={{0,3},{1,4},{2,5},{3,6},{4,7},{5,8},{6,9},{7,10},{8,11},{9,12},{10... | collective-permute-start | bytes 3932168 | tf_op jit(solution)/shard_map/ppermute | solution.py:15
  46.9 101.1 %copy-start.2 = (f32[256,1280]{1,0:T(8,128)}, f32[256,1280]{1,0:T(8,128)S(1)}, u32[]{:S(2)}) copy-start(f32[256,1280]{1,0:T(8,128)S(1)} %collective-permute-done) | copy-start | bytes 3932164
  46.9 17.3 %collective-permute-start.1 = (f32[256,1280]{1,0:T(8,128)S(1)}, f32[256,1280]{1,0:T(8,128)S(1)}, u32[]{:S(2)}, u32[]{:S(2)}) collective-permute-start(f32[256,1280]{1,0:T(8,128)S(1)} %collective-permute-done), channel_id=1, source_target_pairs={{0,255},{1,0},{2,1},{3,2},{4,3},{5,4},{6,5},{7,6},{8,7},{9,8},{10,... | collective-permute-start | bytes 3932168 | tf_op jit(solution)/shard_map/ppermute | solution.py:15
  64.3 23.2 %copy-start.6 = (f32[256,1280]{1,0:T(8,128)}, f32[256,1280]{1,0:T(8,128)S(1)}, u32[]{:S(2)}) copy-start(f32[256,1280]{1,0:T(8,128)S(1)} %collective-permute-done.1) | copy-start | bytes 3932164
  64.3 19.1 %collective-permute-start.2 = (f32[256,1280]{1,0:T(8,128)S(1)}, f32[256,1280]{1,0:T(8,128)S(1)}, u32[]{:S(2)}, u32[]{:S(2)}) collective-permute-start(f32[256,1280]{1,0:T(8,128)S(1)} %collective-permute-done.1), channel_id=1, source_target_pairs={{0,255},{1,0},{2,1},{3,2},{4,3},{5,4},{6,5},{7,6},{8,7},{9,8},{10,... | collective-permute-start | bytes 3932168 | tf_op jit(solution)/shard_map/ppermute | solution.py:15
  83.4 58.5 %copy-start.9 = (f32[256,1280]{1,0:T(8,128)}, f32[256,1280]{1,0:T(8,128)S(1)}, u32[]{:S(2)}) copy-start(f32[256,1280]{1,0:T(8,128)S(1)} %collective-permute-done.2) | copy-start | bytes 3932164
  83.4 19.1 %collective-permute-start.3 = (f32[256,1280]{1,0:T(8,128)S(1)}, f32[256,1280]{1,0:T(8,128)S(1)}, u32[]{:S(2)}, u32[]{:S(2)}) collective-permute-start(f32[256,1280]{1,0:T(8,128)S(1)} %collective-permute-done.2), channel_id=1, source_target_pairs={{0,255},{1,0},{2,1},{3,2},{4,3},{5,4},{6,5},{7,6},{8,7},{9,8},{10,... | collective-permute-start | bytes 3932168 | tf_op jit(solution)/shard_map/ppermute | solution.py:15
  102.5 39.4 %copy-start.12 = (f32[256,1280]{1,0:T(8,128)}, f32[256,1280]{1,0:T(8,128)S(1)}, u32[]{:S(2)}) copy-start(f32[256,1280]{1,0:T(8,128)S(1)} %collective-permute-done.3) | copy-start | bytes 3932164
  102.5 19.1 %collective-permute-start.4 = (f32[256,1280]{1,0:T(8,128)S(1)}, f32[256,1280]{1,0:T(8,128)S(1)}, u32[]{:S(2)}, u32[]{:S(2)}) collective-permute-start(f32[256,1280]{1,0:T(8,128)S(1)} %collective-permute-done.3), channel_id=1, source_target_pairs={{0,255},{1,0},{2,1},{3,2},{4,3},{5,4},{6,5},{7,6},{8,7},{9,8},{10,... | collective-permute-start | bytes 3932168 | tf_op jit(solution)/shard_map/ppermute | solution.py:15
  122.7 19.1 %collective-permute-start.5 = (f32[256,1280]{1,0:T(8,128)S(1)}, f32[256,1280]{1,0:T(8,128)}, u32[]{:S(2)}, u32[]{:S(2)}) collective-permute-start(f32[256,1280]{1,0:T(8,128)S(1)} %collective-permute-done.4), channel_id=1, source_target_pairs={{0,255},{1,0},{2,1},{3,2},{4,3},{5,4},{6,5},{7,6},{8,7},{9,8},{10,... | collective-permute-start | bytes 3932168 | tf_op jit(solution)/shard_map/ppermute | solution.py:15
  141.9 23.6 %collective-permute-start.6 = (f32[256,1280]{1,0:T(8,128)}, f32[256,1280]{1,0:T(8,128)}, u32[]{:S(2)}, u32[]{:S(2)}) collective-permute-start(f32[256,1280]{1,0:T(8,128)} %collective-permute-done.5), channel_id=1, source_target_pairs={{0,255},{1,0},{2,1},{3,2},{4,3},{5,4},{6,5},{7,6},{8,7},{9,8},{10,... | collective-permute-start | bytes 3932168 | tf_op jit(solution)/shard_map/ppermute | solution.py:15
  148.0 13.4 %collective-permute-start.8 = (f32[256]{0:T(256)S(1)}, f32[256]{0:T(256)S(1)}, u32[]{:S(2)}, u32[]{:S(2)}) collective-permute-start(f32[256]{0:T(256)S(1)} %get-tuple-element.34), channel_id=1, source_target_pairs={{0,255},{1,0},{2,1},{3,2},{4,3},{5,4},{6,5},{7,6},{8,7},{9,8},{10,... | collective-permute-start | bytes 3080 | tf_op jit(solution)/shard_map/ppermute | solution.py:15
  148.3 17.5 %copy-start.10 = (f32[256,1280]{1,0:T(8,128)S(1)}, f32[256,1280]{1,0:T(8,128)}, u32[]{:S(2)}) copy-start(f32[256,1280]{1,0:T(8,128)} %copy-done.9) | copy-start | bytes 3932164
  148.3 53.7 %collective-permute-start.16 = (f32[256]{0:T(256)S(1)}, f32[256]{0:T(256)S(1)}, u32[]{:S(2)}, u32[]{:S(2)}) collective-permute-start(f32[256]{0:T(256)S(1)} %multiply_add_fusion.7), channel_id=1, source_target_pairs={{0,255},{1,0},{2,1},{3,2},{4,3},{5,4},{6,5},{7,6},{8,7},{9,8},{10,... | collective-permute-start | bytes 3080 | tf_op jit(solution)/shard_map/ppermute | solution.py:15
  161.5 9.1 %copy-start.13 = (f32[256,1280]{1,0:T(8,128)S(1)}, f32[256,1280]{1,0:T(8,128)}, u32[]{:S(2)}) copy-start(f32[256,1280]{1,0:T(8,128)} %copy-done.12) | copy-start | bytes 3932164
  161.5 5.7 collective-permute-start.9
  165.5 35.0 %collective-permute-start.7 = (f32[256,1280]{1,0:T(8,128)}, f32[256,1280]{1,0:T(8,128)S(1)}, u32[]{:S(2)}, u32[]{:S(2)}) collective-permute-start(f32[256,1280]{1,0:T(8,128)} %collective-permute-done.6), channel_id=1, source_target_pairs={{0,255},{1,0},{2,1},{3,2},{4,3},{5,4},{6,5},{7,6},{8,7},{9,8},{10,... | collective-permute-start | bytes 3932168 | tf_op jit(solution)/shard_map/ppermute | solution.py:15
  167.1 18.1 %copy-start.4 = (f32[256,1280]{1,0:T(8,128)S(1)}, f32[256,1280]{1,0:T(8,128)}, u32[]{:S(2)}) copy-start(f32[256,1280]{1,0:T(8,128)} %copy-done.3) | copy-start | bytes 3932164
  167.2 14.1 %collective-permute-start.10 = (f32[256]{0:T(256)S(1)}, f32[256]{0:T(256)S(1)}, u32[]{:S(2)}, u32[]{:S(2)}) collective-permute-start(f32[256]{0:T(256)S(1)} %max.162), channel_id=1, source_target_pairs={{0,255},{1,0},{2,1},{3,2},{4,3},{5,4},{6,5},{7,6},{8,7},{9,8},{10,... | collective-permute-start | bytes 3080 | tf_op jit(solution)/shard_map/ppermute | solution.py:15
  181.2 5.3 collective-permute-start.11
  186.5 6.4 %collective-permute-start.12 = (f32[256]{0:T(256)S(1)}, f32[256]{0:T(256)S(1)}, u32[]{:S(2)}, u32[]{:S(2)}) collective-permute-start(f32[256]{0:T(256)S(1)} %max.164), channel_id=1, source_target_pairs={{0,255},{1,0},{2,1},{3,2},{4,3},{5,4},{6,5},{7,6},{8,7},{9,8},{10,... | collective-permute-start | bytes 3080 | tf_op jit(solution)/shard_map/ppermute | solution.py:15
  193.0 5.1 collective-permute-start.13
  198.1 4.6 collective-permute-start.14
  202.1 1.9 collective-permute-start.17
  202.7 26.9 %collective-permute-start.15 = (f32[256]{0:T(256)S(1)}, f32[256]{0:T(256)S(1)}, u32[]{:S(2)}, u32[]{:S(2)}) collective-permute-start(f32[256]{0:T(256)S(1)} %max.167), channel_id=1, source_target_pairs={{0,4},{1,5},{2,6},{3,7},{4,8},{5,9},{6,10},{7,11},{8,12},{9,13},{1... | collective-permute-start | bytes 3080 | tf_op jit(solution)/shard_map/ppermute | solution.py:15
  204.0 5.1 collective-permute-start.18
  209.1 5.1 collective-permute-start.19
  214.2 5.1 collective-permute-start.20
  219.3 5.1 collective-permute-start.21
  224.4 5.1 collective-permute-start.22
  229.5 6.6 %collective-permute-start.23 = (f32[256]{0:T(256)S(1)}, f32[256]{0:T(256)S(1)}, u32[]{:S(2)}, u32[]{:S(2)}) collective-permute-start(f32[256]{0:T(256)S(1)} %multiply_add_fusion), channel_id=1, source_target_pairs={{0,4},{1,5},{2,6},{3,7},{4,8},{5,9},{6,10},{7,11},{8,12},{9,13},{1... | collective-permute-start | bytes 3080 | tf_op jit(solution)/shard_map/ppermute | solution.py:15
  236.7 6.0 %collective-permute-start.24 = (f32[256]{0:T(256)S(1)}, f32[256]{0:T(256)S(1)}, u32[]{:S(2)}, u32[]{:S(2)}) collective-permute-start(f32[256]{0:T(256)S(1)} %get-tuple-element.47), channel_id=1, source_target_pairs={{0,3},{1,4},{2,5},{3,6},{4,7},{5,8},{6,9},{7,10},{8,11},{9,12},{10... | collective-permute-start | bytes 3080 | tf_op jit(solution)/shard_map/ppermute | solution.py:15
  244.1 20.3 %collective-permute-start.32 = (f32[256,1280]{1,0:T(8,128)S(1)}, f32[256,1280]{1,0:T(8,128)S(1)}, u32[]{:S(2)}, u32[]{:S(2)}) collective-permute-start(f32[256,1280]{1,0:T(8,128)S(1)} %fusion.1), channel_id=1, source_target_pairs={{0,255},{1,0},{2,1},{3,2},{4,3},{5,4},{6,5},{7,6},{8,7},{9,8},{10,... | collective-permute-start | bytes 3932168 | tf_op jit(solution)/shard_map/ppermute | solution.py:15
  249.2 15.2 %collective-permute-start.25 = (f32[256]{0:T(256)S(1)}, f32[256]{0:T(256)S(1)}, u32[]{:S(2)}, u32[]{:S(2)}) collective-permute-start(f32[256]{0:T(256)S(1)} %collective-permute-done.24), channel_id=1, source_target_pairs={{0,255},{1,0},{2,1},{3,2},{4,3},{5,4},{6,5},{7,6},{8,7},{9,8},{10,... | collective-permute-start | bytes 3080 | tf_op jit(solution)/shard_map/ppermute | solution.py:15
  265.7 19.4 %collective-permute-start.33 = (f32[256,1280]{1,0:T(8,128)S(1)}, f32[256,1280]{1,0:T(8,128)S(1)}, u32[]{:S(2)}, u32[]{:S(2)}) collective-permute-start(f32[256,1280]{1,0:T(8,128)S(1)} %convolution_add_fusion.5), channel_id=1, source_target_pairs={{0,255},{1,0},{2,1},{3,2},{4,3},{5,4},{6,5},{7,6},{8,7},{9,8},{10,... | collective-permute-start | bytes 3932168 | tf_op jit(solution)/shard_map/ppermute | solution.py:15
  270.0 15.2 %collective-permute-start.26 = (f32[256]{0:T(256)S(1)}, f32[256]{0:T(256)S(1)}, u32[]{:S(2)}, u32[]{:S(2)}) collective-permute-start(f32[256]{0:T(256)S(1)} %collective-permute-done.25), channel_id=1, source_target_pairs={{0,255},{1,0},{2,1},{3,2},{4,3},{5,4},{6,5},{7,6},{8,7},{9,8},{10,... | collective-permute-start | bytes 3080 | tf_op jit(solution)/shard_map/ppermute | solution.py:15
  286.5 19.3 %collective-permute-start.34 = (f32[256,1280]{1,0:T(8,128)S(1)}, f32[256,1280]{1,0:T(8,128)S(1)}, u32[]{:S(2)}, u32[]{:S(2)}) collective-permute-start(f32[256,1280]{1,0:T(8,128)S(1)} %convolution_add_fusion.4), channel_id=1, source_target_pairs={{0,255},{1,0},{2,1},{3,2},{4,3},{5,4},{6,5},{7,6},{8,7},{9,8},{10,... | collective-permute-start | bytes 3932168 | tf_op jit(solution)/shard_map/ppermute | solution.py:15
  290.6 15.2 %collective-permute-start.27 = (f32[256]{0:T(256)S(1)}, f32[256]{0:T(256)S(1)}, u32[]{:S(2)}, u32[]{:S(2)}) collective-permute-start(f32[256]{0:T(256)S(1)} %collective-permute-done.26), channel_id=1, source_target_pairs={{0,255},{1,0},{2,1},{3,2},{4,3},{5,4},{6,5},{7,6},{8,7},{9,8},{10,... | collective-permute-start | bytes 3080 | tf_op jit(solution)/shard_map/ppermute | solution.py:15
  307.1 19.3 %collective-permute-start.35 = (f32[256,1280]{1,0:T(8,128)S(1)}, f32[256,1280]{1,0:T(8,128)S(1)}, u32[]{:S(2)}, u32[]{:S(2)}) collective-permute-start(f32[256,1280]{1,0:T(8,128)S(1)} %fusion.4), channel_id=1, source_target_pairs={{0,255},{1,0},{2,1},{3,2},{4,3},{5,4},{6,5},{7,6},{8,7},{9,8},{10,... | collective-permute-start | bytes 3932168 | tf_op jit(solution)/shard_map/ppermute | solution.py:15
  311.2 15.2 %collective-permute-start.28 = (f32[256]{0:T(256)S(1)}, f32[256]{0:T(256)S(1)}, u32[]{:S(2)}, u32[]{:S(2)}) collective-permute-start(f32[256]{0:T(256)S(1)} %collective-permute-done.27), channel_id=1, source_target_pairs={{0,255},{1,0},{2,1},{3,2},{4,3},{5,4},{6,5},{7,6},{8,7},{9,8},{10,... | collective-permute-start | bytes 3080 | tf_op jit(solution)/shard_map/ppermute | solution.py:15
  327.7 19.3 %collective-permute-start.36 = (f32[256,1280]{1,0:T(8,128)S(1)}, f32[256,1280]{1,0:T(8,128)S(1)}, u32[]{:S(2)}, u32[]{:S(2)}) collective-permute-start(f32[256,1280]{1,0:T(8,128)S(1)} %convolution_add_fusion.3), channel_id=1, source_target_pairs={{0,255},{1,0},{2,1},{3,2},{4,3},{5,4},{6,5},{7,6},{8,7},{9,8},{10,... | collective-permute-start | bytes 3932168 | tf_op jit(solution)/shard_map/ppermute | solution.py:15
  331.9 15.2 %collective-permute-start.29 = (f32[256]{0:T(256)S(1)}, f32[256]{0:T(256)S(1)}, u32[]{:S(2)}, u32[]{:S(2)}) collective-permute-start(f32[256]{0:T(256)S(1)} %collective-permute-done.28), channel_id=1, source_target_pairs={{0,255},{1,0},{2,1},{3,2},{4,3},{5,4},{6,5},{7,6},{8,7},{9,8},{10,... | collective-permute-start | bytes 3080 | tf_op jit(solution)/shard_map/ppermute | solution.py:15
  348.4 19.3 %collective-permute-start.37 = (f32[256,1280]{1,0:T(8,128)S(1)}, f32[256,1280]{1,0:T(8,128)S(1)}, u32[]{:S(2)}, u32[]{:S(2)}) collective-permute-start(f32[256,1280]{1,0:T(8,128)S(1)} %convolution_add_fusion.2), channel_id=1, source_target_pairs={{0,255},{1,0},{2,1},{3,2},{4,3},{5,4},{6,5},{7,6},{8,7},{9,8},{10,... | collective-permute-start | bytes 3932168 | tf_op jit(solution)/shard_map/ppermute | solution.py:15
  352.5 15.2 %collective-permute-start.30 = (f32[256]{0:T(256)S(1)}, f32[256]{0:T(256)S(1)}, u32[]{:S(2)}, u32[]{:S(2)}) collective-permute-start(f32[256]{0:T(256)S(1)} %collective-permute-done.29), channel_id=1, source_target_pairs={{0,255},{1,0},{2,1},{3,2},{4,3},{5,4},{6,5},{7,6},{8,7},{9,8},{10,... | collective-permute-start | bytes 3080 | tf_op jit(solution)/shard_map/ppermute | solution.py:15
  370.0 19.5 %collective-permute-start.38 = (f32[256,1280]{1,0:T(8,128)}, f32[256,1280]{1,0:T(8,128)}, u32[]{:S(2)}, u32[]{:S(2)}) collective-permute-start(f32[256,1280]{1,0:T(8,128)} %convolution_add_fusion.1), channel_id=1, source_target_pairs={{0,255},{1,0},{2,1},{3,2},{4,3},{5,4},{6,5},{7,6},{8,7},{9,8},{10,... | collective-permute-start | bytes 3932168 | tf_op jit(solution)/shard_map/ppermute | solution.py:15
  384.4 5.1 collective-permute-start.31
  393.2 186.8 %collective-permute-start.39 = (f32[256,1280]{1,0:T(8,128)}, f32[256,1280]{1,0:T(8,128)}, u32[]{:S(2)}, u32[]{:S(2)}) collective-permute-start(f32[256,1280]{1,0:T(8,128)} %convolution_add_fusion), channel_id=1, source_target_pairs={{0,4},{1,5},{2,6},{3,7},{4,8},{5,9},{6,10},{7,11},{8,12},{9,13},{1... | collective-permute-start | bytes 3932168 | tf_op jit(solution)/shard_map/ppermute | solution.py:15
  (7 other events, 17.2 us)
where the time goes:
time: 594 us; the launch traced here: 585 us
  waiting for transfers between devices  232 us (39%)
  blocking collectives  166 us (28%)
  starting transfers between devices  117 us (20%)
  matrix products  47 us (8%)
  between operations  12.7 us (2%)
  other arithmetic  7.32 us (1%)
    ppermute x40, waiting for transfers between devices, from_behind(): return lax.ppermute(value, axis, pairs)  232 us
    psum x1, blocking collectives, on_device(): loss_total, scale_total = lax.psum((loss_part, scale_acc), 'dp')  166 us
    ppermute x40, starting transfers between devices, from_behind(): return lax.ppermute(value, axis, pairs)  117 us
    dot_general x8, matrix products, on_device(): jnp.dot(weights, text_block, precision=precise, preferred_element_type=jn...  19.6 us
    dot_general x8, matrix products, on_device(): lax.dot_general(weights, image_emb, (((0,), (0,)), ((), ())), precision=p...  14.1 us
    dot_general x8, matrix products, scores(): lax.dot_general(image_emb, text_block, (((1,), (1,)), ((), ())), precisio...  13.2 us
  transfers between devices with their start and end apart: 40, of which 23 were waited for; matrix products, arithmetic and copies ran while one was open for 7% of the time, Pallas kernels for 0%

commit v1 on v0

v1 whole, which is shorter than its diff:
```python
import jax
import jax.numpy as jnp
from jax import lax
from jax.sharding import PartitionSpec as P

WIN = 8
BOTH = (0, 1)

highest = lax.Precision.HIGHEST
high = lax.Precision.HIGH


def shift(value, steps, cores=BOTH):
    count = lax.axis_size("dp")
    pairs = [(s, (s + steps) % count) for s in range(count) if s % 2 in cores]
    return lax.ppermute(value, "dp", pairs)


def swap(value):
    count = lax.axis_size("dp")
    return lax.ppermute(value, "dp", [(s, s ^ 1) for s in range(count)])


def scores(rows, block, scale):
    return scale * lax.dot_general(
        rows,
        block,
        (((1,), (1,)), ((), ())),
        precision=highest,
        preferred_element_type=jnp.float32,
    )


def apply(weights, block):
    return jnp.dot(weights, block, precision=high, preferred_element_type=jnp.float32)


def lse(logits, axis):
    top = jnp.max(logits, axis=axis, keepdims=True)
    total = jnp.sum(jnp.exp(logits - top), axis=axis)
    return jnp.squeeze(top, axis) + jnp.log(total)


def merge(parts):
    return lse(jnp.stack(parts), 0)


def on_device(image, text, scale):
    rows = image.shape[0]
    first = lax.axis_index("dp") % 2 == 0
    eye = jnp.eye(rows, dtype=jnp.float32)

    text_p = shift(text, 2)
    text_m = shift(text, -2)
    image_s = swap(image)
    text_mm = shift(text_m, -2)
    text_pp = shift(text_p, 2, (1,))
    text_s = swap(text)
    image_p = shift(image, 2)
    image_m = shift(image, -2)
    image_pp = shift(image_p, 2)
    image_mm = shift(image_m, -2, (0,))

    near_t = {-2: text_p, 0: text, 2: text_m}
    far_own_t = text_mm
    far_sib_t = jnp.where(first, text_mm, text_pp)
    both_i = jnp.concatenate([image, image_s])
    near_l = {b: scores(both_i, t, scale) for b, t in near_t.items()}
    own_l = scores(image, far_own_t, scale)
    sib_l = scores(image_s, far_sib_t, scale)

    row_own = merge([lse(v[:rows], 1) for v in near_l.values()] + [lse(own_l, 1)])
    row_sib = merge([lse(v[rows:], 1) for v in near_l.values()] + [lse(sib_l, 1)])
    got = swap(jnp.stack([row_own, row_sib]))
    row_lse = merge([row_own, got[1]])
    row_lse_s = merge([row_sib, got[0]])

    col_near = {b: lse(v, 0) for b, v in near_l.items()}
    col_own = lse(own_l, 0)
    col_sib = lse(sib_l, 0)
    col_far = jnp.where(first, merge([col_own, col_sib]), col_own)
    from_m = shift(col_near[2], 2)
    from_p = shift(col_near[-2], -2)
    from_mm = shift(col_far, 4)
    from_pp = shift(col_sib, -4, (1,))
    from_pp = jnp.where(first, -jnp.inf, from_pp)
    col_lse = merge([col_near[0], from_m, from_p, from_mm, from_pp])

    diagonal = jnp.diagonal(near_l[0][:rows])
    loss_part = jnp.sum(row_lse) + jnp.sum(col_lse) - 2.0 * jnp.sum(diagonal)

    mine = jnp.stack([row_lse, col_lse])
    at = {0: mine}
    for step in (2, -2, 4, -4):
        at[-step] = shift(mine, step)
    col_lse_s = swap(col_lse)

    row_both = jnp.concatenate([row_lse, row_lse_s])[:, None]
    image_acc = jnp.zeros((2 * rows, image.shape[1]), jnp.float32)
    scale_acc = jnp.zeros((), jnp.float32)
    zero = jnp.zeros_like(eye)
    corner = jnp.concatenate([2.0 * eye, zero])
    for b, t in near_t.items():
        v = near_l[b]
        w = jnp.exp(v - row_both) + jnp.exp(v - at[b][1][None, :])
        if b == 0:
            w = w - corner
        image_acc += apply(w, t)
        scale_acc += jnp.sum(w * v)
    w = jnp.exp(own_l - row_lse[:, None]) + jnp.exp(own_l - at[4][1][None, :])
    scale_acc += jnp.sum(w * own_l)
    image_own = image_acc[:rows] + apply(w, far_own_t)
    col_e = jnp.where(first, at[4][1], at[-4][1])
    w = jnp.exp(sib_l - row_lse_s[:, None]) + jnp.exp(sib_l - col_e[None, :])
    scale_acc += jnp.sum(w * sib_l)
    image_sib = image_acc[rows:] + apply(w, far_sib_t)
    image_grad = 0.5 * scale * (image_own + swap(image_sib))

    near_i = {-2: image_p, 0: image, 2: image_m}
    far_own_i = image_pp
    far_sib_i = jnp.where(first, image_mm, image_pp)
    both_t = jnp.concatenate([text, text_s])
    col_both = jnp.concatenate([col_lse, col_lse_s])[:, None]
    text_acc = jnp.zeros((2 * rows, image.shape[1]), jnp.float32)
    for b, i in near_i.items():
        v = scores(both_t, i, scale)
        w = jnp.exp(v - col_both) + jnp.exp(v - at[b][0][None, :])
        if b == 0:
            w = w - corner
        text_acc += apply(w, i)
    v = scores(text, far_own_i, scale)
    w = jnp.exp(v - col_lse[:, None]) + jnp.exp(v - at[-4][0][None, :])
    text_own = text_acc[:rows] + apply(w, far_own_i)
    v = scores(text_s, far_sib_i, scale)
    row_f = jnp.where(first, at[4][0], at[-4][0])
    w = jnp.exp(v - col_lse_s[:, None]) + jnp.exp(v - row_f[None, :])
    text_sib = text_acc[rows:] + apply(w, far_sib_i)
    text_grad = 0.5 * scale * (text_own + swap(text_sib))

    loss_total, scale_total = lax.psum((loss_part, scale_acc), "dp")
    total_rows = rows * lax.axis_size("dp")
    loss = loss_total / (2.0 * total_rows)
    scale_grad = scale_total / (2.0 * total_rows * scale)
    return (loss, image_grad, text_grad, scale_grad)


def solution(mesh):
    in_specs = (P("dp", None), P("dp", None), P())
    out_specs = (P(), P("dp", None), P("dp", None), P())
    return jax.shard_map(
        on_device, mesh=mesh, in_specs=in_specs, out_specs=out_specs, check_vma=False
    )
```

time: 594 us -> 280 us (0.47)
  the two profiles are of different devices: /device:TPU:8 before, /device:TPU:1 now
where the time goes in v1:
time: 280 us; the launch traced here: 275 us
  blocking collectives  80 us (29%)
  matrix products  61 us (22%)
  waiting for transfers between devices  57.8 us (21%)
  starting transfers between devices  47.1 us (17%)
  between operations  10.9 us (4%)
  other arithmetic  9.33 us (3%)
  local copies, waits for them, and re-layouts  9.01 us (3%)
    psum x1, blocking collectives, on_device(): loss_total, scale_total = lax.psum((loss_part, scale_acc), 'dp')  80 us
    ppermute x16, waiting for transfers between devices, shift(): return lax.ppermute(value, 'dp', pairs)  57.8 us
    ppermute x16, starting transfers between devices, shift(): return lax.ppermute(value, 'dp', pairs)  38.6 us
    dot_general x10, matrix products, scores(): lax.dot_general(rows, block, (((1,), (1,)), ((), ())), precision=highest,...  32.7 us
    dot_general x10, matrix products, apply(): jnp.dot(weights, block, precision=high, preferred_element_type=jnp.float32)  28.4 us
    ppermute x6, starting transfers between devices, swap(): return lax.ppermute(value, 'dp', [(s, s ^ 1) for s in range(count)])  8.51 us
  transfers between devices with their start and end apart: 22, of which 5 were waited for; matrix products, arithmetic and copies ran while one was open for 25% of the time, Pallas kernels for 0%

profile of v1, /device:TPU:1, one launch (start us, length us, event | category | flops | bytes accessed | tf_op | source)
XLA Modules:
  0.0 275.2 jit_solution(963764148463461500)
XLA Ops:
  0.6 3.3 %collective-permute-start = (f32[256,1280]{1,0:T(8,128)}, f32[256,1280]{1,0:T(8,128)}, u32[]{:S(2)}, u32[]{:S(2)}) collective-permute-start(f32[256,1280]{1,0:T(8,128)} %param.3), channel_id=1, source_target_pairs={{0,1},{1,0},{2,3},{3,2},{4,5},{5,4},{6,7},{7,6},{8,9},{9,8},{10,11... | collective-permute-start | bytes 3932168 | tf_op jit(solution)/shard_map/ppermute | solution.py:21
  4.0 8.5 %collective-permute-start.2 = (f32[256,1280]{1,0:T(8,128)}, f32[256,1280]{1,0:T(8,128)}, u32[]{:S(2)}, u32[]{:S(2)}) collective-permute-start(f32[256,1280]{1,0:T(8,128)} %param.4), channel_id=1, source_target_pairs={{0,254},{1,255},{2,0},{3,1},{4,2},{5,3},{6,4},{7,5},{8,6},{9,7},{1... | collective-permute-start | bytes 3932168 | tf_op jit(solution)/shard_map/ppermute | solution.py:16
  12.4 1.5 collective-permute-start.18
  13.9 0.9 collective-permute-start.15
  14.8 0.7 fusion.56
  16.2 1.5 constant_dynamic-update-slice_fusion.1
  18.1 1.2 copy-done
  19.5 1.4 constant_dynamic-update-slice_fusion
  20.9 2.5 fusion.88
  23.5 18.4 %collective-permute-done.1 = f32[256,1280]{1,0:T(8,128)} collective-permute-done((f32[256,1280]{1,0:T(8,128)}, f32[256,1280]{1,0:T(8,128)}, u32[]{:S(2)}, u32[]{:S(2)}) %collective-permute-start.1) | collective-permute-done | bytes 1310752 | tf_op jit(solution)/shard_map/ppermute | solution.py:16
  41.8 3.8 %fusion.86 = (f32[256]{0:T(256)S(1)}, f32[512,256]{0,1:T(8,128)S(1)}) fusion(f32[512,1280]{1,0:T(8,128)S(1)} %constant_dynamic-update-slice_fusion, f32[256,1280]{1,0:T(8,128)} %collective-permute-done.1, f32[]{:T(128)S(6)} %copy.21), kind=kOutput, calls=%fused_computation.178 | convolution fusion | flops 2013527808 | bytes 4457476 | tf_op jit(solution)/shard_map/dot_general | solution.py:25
  46.0 3.8 %fusion.87 = (f32[256]{0:T(256)S(1)}, f32[512,256]{0,1:T(8,128)S(1)}) fusion(f32[512,1280]{1,0:T(8,128)S(1)} %constant_dynamic-update-slice_fusion, f32[256,1280]{1,0:T(8,128)} %collective-permute-done.2, f32[]{:T(128)S(6)} %copy.21), kind=kOutput, calls=%fused_computation.179 | convolution fusion | flops 2013527808 | bytes 4457476 | tf_op jit(solution)/shard_map/dot_general | solution.py:25
  50.5 2.4 collective-permute-start.3
  53.0 1.9 collective-permute-start.4
  55.0 7.2 %collective-permute-start.7 = (f32[256]{0:T(256)S(1)}, f32[256]{0:T(256)S(1)}, u32[]{:S(2)}, u32[]{:S(2)}) collective-permute-start(f32[256]{0:T(256)S(1)} %log_add_fusion.4), channel_id=1, source_target_pairs={{0,254},{1,255},{2,0},{3,1},{4,2},{5,3},{6,4},{7,5},{8,6},{9,7},{1... | collective-permute-start | bytes 3080 | tf_op jit(solution)/shard_map/ppermute | solution.py:16
  62.2 1.4 constant_dynamic-update-slice_fusion.2
  63.6 3.3 %convolution_multiply_fusion.1 = f32[512,256]{0,1:T(8,128)} fusion(f32[512,1280]{1,0:T(8,128)S(1)} %constant_dynamic-update-slice_fusion.2, f32[256,1280]{1,0:T(8,128)S(1)} %copy-done, f32[]{:T(128)S(6)} %copy.21), kind=kOutput, calls=%fused_computation.14 | convolution fusion | flops 2013396992 | bytes 4456452 | tf_op jit(solution)/shard_map/dot_general | solution.py:25
  66.9 1.9 collective-permute-done.18
  68.9 4.6 %convolution_multiply_fusion = f32[512,256]{0,1:T(8,128)} fusion(f32[512,1280]{1,0:T(8,128)S(1)} %constant_dynamic-update-slice_fusion.2, f32[256,1280]{1,0:T(8,128)} %collective-permute-done.18, f32[]{:T(128)S(6)} %copy.21), kind=kOutput, calls=%fused_computation.13 | convolution fusion | flops 2013396992 | bytes 4456452 | tf_op jit(solution)/shard_map/dot_general | solution.py:25
  73.4 1.7 collective-permute-start.20
  75.1 4.6 %convolution_multiply_fusion.2 = f32[512,256]{0,1:T(8,128)} fusion(f32[512,1280]{1,0:T(8,128)S(1)} %constant_dynamic-update-slice_fusion.2, f32[256,1280]{1,0:T(8,128)} %collective-permute-done.16, f32[]{:T(128)S(6)} %copy.21), kind=kOutput, calls=%fused_computation.15 | convolution fusion | flops 2013396992 | bytes 4456452 | tf_op jit(solution)/shard_map/dot_general | solution.py:25
  79.7 17.2 %collective-permute-done.3 = f32[256,1280]{1,0:T(8,128)S(1)} collective-permute-done((f32[256,1280]{1,0:T(8,128)}, f32[256,1280]{1,0:T(8,128)S(1)}, u32[]{:S(2)}, u32[]{:S(2)}) %collective-permute-start.3) | collective-permute-done | bytes 1310752 | tf_op jit(solution)/shard_map/ppermute | solution.py:16
  97.4 3.2 %fusion.79 = (f32[256]{0:T(256)S(1)}, f32[256]{0:T(256)S(1)}, f32[256,256]{1,0:T(8,128)S(1)}) fusion(f32[256,1280]{1,0:T(8,128)} %collective-permute-done, f32[256,1280]{1,0:T(8,128)S(1)} %collective-permute-done.3, f32[256,1280]{1,0:T(8,128)S(1)} %collective-permute-done.4, pred[]{:T(512)S(6)} %eq.8, f32[]{:T(128)S(6)} %copy.21), kind=kOutput, calls=%fused_computation.171 | convolution fusion | flops 1007156736 | bytes 4196357 | tf_op jit(solution)/shard_map/dot_general | solution.py:25
  100.8 1.3 fusion.78
  102.2 0.7 copy-done.17
  103.2 10.6 %collective-permute-start.9 = (f32[256]{0:T(256)S(1)}, f32[256]{0:T(256)S(1)}, u32[]{:S(2)}, u32[]{:S(2)}) collective-permute-start(f32[256]{0:T(256)S(1)} %get-tuple-element.34), channel_id=1, source_target_pairs={{1,253},{3,255},{5,1},{7,3},{9,5},{11,7},{13,9},{15,11},{17,13},{1... | collective-permute-start | bytes 3080 | tf_op jit(solution)/shard_map/ppermute | solution.py:16
  114.1 19.8 %collective-permute-done.8 = f32[256]{0:T(256)S(1)} collective-permute-done((f32[256]{0:T(256)S(1)}, f32[256]{0:T(256)S(1)}, u32[]{:S(2)}, u32[]{:S(2)}) %collective-permute-start.8) | collective-permute-done | bytes 1056 | tf_op jit(solution)/shard_map/ppermute | solution.py:16
  134.5 2.2 collective-permute-start.17
  136.8 3.0 %convolution_multiply_fusion.6 = f32[256,256]{1,0:T(8,128)S(1)} fusion(f32[256,1280]{1,0:T(8,128)} %collective-permute-done.15, f32[256,1280]{1,0:T(8,128)} %collective-permute-done.20, f32[256,1280]{1,0:T(8,128)} %collective-permute-done.19, pred[]{:T(512)S(6)} %eq.8, f32[]{:T(128)S(6)} %copy.21), kind=kOutput, calls=%fused_computation.19 | convolution fusion | flops 1007026176 | bytes 4194309 | tf_op jit(solution)/shard_map/dot_general | solution.py:25
  140.5 1.5 collective-permute-start.10
  142.0 2.5 collective-permute-start.13
  144.6 1.5 fusion.24
  146.1 1.5 fusion.6
  147.6 2.8 %fusion.23 = f32[512,1280]{1,0:T(8,128)S(1)} fusion(f32[256,1280]{1,0:T(8,128)} %collective-permute-done.2, f32[512,256]{0,1:T(8,128)S(1)} %copy-done.7, f32[256]{0:T(256)S(1)} %bitcast.88, f32[512]{0:T(512)S(1)} %pad_maximum_fusion.2), kind=kOutput, calls=%fused_computation.48 | convolution fusion | flops 1007026176 | bytes 4459520 | tf_op jit(solution)/shard_map/dot_general | solution.py:35
  151.0 3.2 %fusion.1 = f32[512,1280]{1,0:T(8,128)S(1)} fusion(f32[512,1280]{1,0:T(8,128)S(1)} %fusion.23, f32[512,1280]{1,0:T(8,128)S(1)} %fusion.24, f32[256,1280]{1,0:T(8,128)} %collective-permute-done.1, f32[512,256]{0,1:T(8,128)S(1)} %copy-done.5, f32[256]{0:T(256)S(1)} %bitcast.90, f32[512]{0:T(512)S(1)} %pad_maximum_fusion.2), kind=kOutput, calls=%fused_computation.4 | convolution fusion | flops 1008336896 | bytes 9702400 | tf_op jit(solution)/shard_map/dot_general | solution.py:35
  154.2 2.0 convolution_add_fusion.4
  156.2 1.8 collective-permute-start.14
  157.9 2.8 %fusion.7 = f32[512,1280]{1,0:T(8,128)S(1)} fusion(f32[256,1280]{1,0:T(8,128)} %collective-permute-done.18, f32[512,256]{0,1:T(8,128)S(1)} %copy-done.19, f32[256]{0:T(256)S(1)} %bitcast.117, f32[512]{0:T(512)S(1)} %pad_maximum_fusion.4), kind=kOutput, calls=%fused_computation.31 | convolution fusion | flops 1007026176 | bytes 4459520 | tf_op jit(solution)/shard_map/dot_general | solution.py:35
  160.8 3.0 %fusion = f32[512,1280]{1,0:T(8,128)S(1)} fusion(f32[512,1280]{1,0:T(8,128)S(1)} %fusion.7, f32[512,1280]{1,0:T(8,128)S(1)} %fusion.6, f32[256,1280]{1,0:T(8,128)} %collective-permute-done.16, f32[512,256]{0,1:T(8,128)S(1)} %copy-done.20, f32[256]{0:T(256)S(1)} %bitcast.118, f32[512]{0:T(512)S(1)} %pad_maximum_fusion.4), kind=kOutput, calls=%fused_computation.2 | convolution fusion | flops 1008336896 | bytes 9702400 | tf_op jit(solution)/shard_map/dot_general | solution.py:35
  163.8 4.2 %convolution_add_fusion.2 = f32[256,1280]{1,0:T(8,128)} fusion(f32[512,1280]{1,0:T(8,128)S(1)} %fusion, f32[256,1280]{1,0:T(8,128)} %collective-permute-done.20, f32[256,1280]{1,0:T(8,128)} %collective-permute-done.19, pred[]{:T(512)S(6)} %eq.8, f32[256,256]{1,0:T(8,128)S(1)} %convolution_multiply_fusion.6, f32[256]{0:T(256)S(1)} %bitcast.130, ...), kind=kOutput, calls=%fused_computation.5 | convolution fusion | flops 504168448 | bytes 5507073 | tf_op jit(solution)/shard_map/dot_general | solution.py:35
  168.2 2.4 gather_fusion
  173.2 2.4 multiply_reduce_fusion
  177.6 1.7 multiply_reduce_fusion.3
  179.9 0.8 fusion.33
  181.3 2.6 convolution_multiply_fusion.7
  184.0 80.0 %all-reduce.1 = (f32[]{:T(128)}, f32[]{:T(128)}) all-reduce(f32[]{:T(128)S(6)} %sub.374, f32[]{:T(128)S(6)} %add.493), channel_id=1, replica_groups=mesh['dp'=256] {'dp'}, use_global_device_ids=true, to_apply=%region_34.35 | all-reduce | flops 2 | bytes 16 | tf_op jit(solution)/shard_map/psum | solution.py:140
  265.3 3.8 %fusion.5 = f32[256,1280]{1,0:T(8,128)} fusion(f32[256,1280]{1,0:T(8,128)} %collective-permute-done.14, f32[256,1280]{1,0:T(8,128)S(1)} %copy-done.3, f32[512,1280]{1,0:T(8,128)} %copy-done.8, f32[]{:T(128)S(6)} %mul.98, f32[256,256]{1,0:T(8,128)S(1)} %copy-done.18, f32[256]{0:T(256)S(1)} %bitcast.114, f32[256]{0:T(256)S(1)} %get-tuple-element.36), kind=kOutput, calls=%fused_computation.12 | convolution fusion | flops 504496128 | bytes 5507076 | tf_op jit(solution)/shard_map/dot_general | solution.py:35
  269.0 3.7 %fusion.3 = f32[256,1280]{1,0:T(8,128)} fusion(f32[256,1280]{1,0:T(8,128)} %collective-permute-done.21, f32[256,1280]{1,0:T(8,128)} %collective-permute-done.19, f32[512,1280]{1,0:T(8,128)S(1)} %copy-done.10, f32[]{:T(128)S(6)} %mul.98, f32[256,256]{1,0:T(8,128)S(1)} %convolution_multiply_fusion.7, f32[256]{0:T(256)S(1)} %bitcast.129, ...), kind=kOutput, calls=%fused_computation.8 | convolution fusion | flops 504496128 | bytes 5507076 | tf_op jit(solution)/shard_map/dot_general | solution.py:35
  (113 shorter events, 5.7 us)
Async XLA Ops:
  0.6 17.4 %collective-permute-start = (f32[256,1280]{1,0:T(8,128)}, f32[256,1280]{1,0:T(8,128)}, u32[]{:S(2)}, u32[]{:S(2)}) collective-permute-start(f32[256,1280]{1,0:T(8,128)} %param.3), channel_id=1, source_target_pairs={{0,1},{1,0},{2,3},{3,2},{4,5},{5,4},{6,7},{7,6},{8,9},{9,8},{10,11... | collective-permute-start | bytes 3932168 | tf_op jit(solution)/shard_map/ppermute | solution.py:21
  4.0 37.9 %collective-permute-start.1 = (f32[256,1280]{1,0:T(8,128)}, f32[256,1280]{1,0:T(8,128)}, u32[]{:S(2)}, u32[]{:S(2)}) collective-permute-start(f32[256,1280]{1,0:T(8,128)} %param.4), channel_id=1, source_target_pairs={{0,2},{1,3},{2,4},{3,5},{4,6},{5,7},{6,8},{7,9},{8,10},{9,11},{10,... | collective-permute-start | bytes 3932168 | tf_op jit(solution)/shard_map/ppermute | solution.py:16
  4.0 42.1 %collective-permute-start.2 = (f32[256,1280]{1,0:T(8,128)}, f32[256,1280]{1,0:T(8,128)}, u32[]{:S(2)}, u32[]{:S(2)}) collective-permute-start(f32[256,1280]{1,0:T(8,128)} %param.4), channel_id=1, source_target_pairs={{0,254},{1,255},{2,0},{3,1},{4,2},{5,3},{6,4},{7,5},{8,6},{9,7},{1... | collective-permute-start | bytes 3932168 | tf_op jit(solution)/shard_map/ppermute | solution.py:16
  12.4 56.4 %collective-permute-start.18 = (f32[256,1280]{1,0:T(8,128)}, f32[256,1280]{1,0:T(8,128)}, u32[]{:S(2)}, u32[]{:S(2)}) collective-permute-start(f32[256,1280]{1,0:T(8,128)} %param.3), channel_id=1, source_target_pairs={{0,254},{1,255},{2,0},{3,1},{4,2},{5,3},{6,4},{7,5},{8,6},{9,7},{1... | collective-permute-start | bytes 3932168 | tf_op jit(solution)/shard_map/ppermute | solution.py:16
  13.9 41.1 %collective-permute-start.15 = (f32[256,1280]{1,0:T(8,128)}, f32[256,1280]{1,0:T(8,128)}, u32[]{:S(2)}, u32[]{:S(2)}) collective-permute-start(f32[256,1280]{1,0:T(8,128)} %param.4), channel_id=1, source_target_pairs={{0,1},{1,0},{2,3},{3,2},{4,5},{5,4},{6,7},{7,6},{8,9},{9,8},{10,11... | collective-permute-start | bytes 3932168 | tf_op jit(solution)/shard_map/ppermute | solution.py:21
  16.2 1.7 copy-start.1
  18.0 1.3 copy-start
  19.3 54.1 %collective-permute-start.16 = (f32[256,1280]{1,0:T(8,128)S(1)}, f32[256,1280]{1,0:T(8,128)}, u32[]{:S(2)}, u32[]{:S(2)}) collective-permute-start(f32[256,1280]{1,0:T(8,128)S(1)} %copy-done), channel_id=1, source_target_pairs={{0,2},{1,3},{2,4},{3,5},{4,6},{5,7},{6,8},{7,9},{8,10},{9,11},{10,... | collective-permute-start | bytes 3932168 | tf_op jit(solution)/shard_map/ppermute | solution.py:16
  45.6 4.2 %copy-start.4 = (f32[512,256]{0,1:T(8,128)}, f32[512,256]{0,1:T(8,128)S(1)}, u32[]{:S(2)}) copy-start(f32[512,256]{0,1:T(8,128)S(1)} %get-tuple-element.65) | copy-start | bytes 1572868
  49.9 5.0 %copy-start.6 = (f32[512,256]{0,1:T(8,128)}, f32[512,256]{0,1:T(8,128)S(1)}, u32[]{:S(2)}) copy-start(f32[512,256]{0,1:T(8,128)S(1)} %get-tuple-element.67) | copy-start | bytes 1572868
  50.5 46.4 %collective-permute-start.3 = (f32[256,1280]{1,0:T(8,128)}, f32[256,1280]{1,0:T(8,128)S(1)}, u32[]{:S(2)}, u32[]{:S(2)}) collective-permute-start(f32[256,1280]{1,0:T(8,128)} %collective-permute-done.2), channel_id=1, source_target_pairs={{0,254},{1,255},{2,0},{3,1},{4,2},{5,3},{6,4},{7,5},{8,6},{9,7},{1... | collective-permute-start | bytes 3932168 | tf_op jit(solution)/shard_map/ppermute | solution.py:16
  53.0 44.4 %collective-permute-start.4 = (f32[256,1280]{1,0:T(8,128)}, f32[256,1280]{1,0:T(8,128)S(1)}, u32[]{:S(2)}, u32[]{:S(2)}) collective-permute-start(f32[256,1280]{1,0:T(8,128)} %collective-permute-done.1), channel_id=1, source_target_pairs={{1,3},{3,5},{5,7},{7,9},{9,11},{11,13},{13,15},{15,17},{17,19},{19... | collective-permute-start | bytes 3932168 | tf_op jit(solution)/shard_map/ppermute | solution.py:16
  55.0 58.8 %collective-permute-start.7 = (f32[256]{0:T(256)S(1)}, f32[256]{0:T(256)S(1)}, u32[]{:S(2)}, u32[]{:S(2)}) collective-permute-start(f32[256]{0:T(256)S(1)} %log_add_fusion.4), channel_id=1, source_target_pairs={{0,254},{1,255},{2,0},{3,1},{4,2},{5,3},{6,4},{7,5},{8,6},{9,7},{1... | collective-permute-start | bytes 3080 | tf_op jit(solution)/shard_map/ppermute | solution.py:16
  68.9 45.1 %collective-permute-start.6 = (f32[256]{0:T(256)S(1)}, f32[256]{0:T(256)S(1)}, u32[]{:S(2)}, u32[]{:S(2)}) collective-permute-start(f32[256]{0:T(256)S(1)} %log_add_fusion.5), channel_id=1, source_target_pairs={{0,2},{1,3},{2,4},{3,5},{4,6},{5,7},{6,8},{7,9},{8,10},{9,11},{10,... | collective-permute-start | bytes 3080 | tf_op jit(solution)/shard_map/ppermute | solution.py:16
  73.4 63.3 %collective-permute-start.20 = (f32[256,1280]{1,0:T(8,128)}, f32[256,1280]{1,0:T(8,128)}, u32[]{:S(2)}, u32[]{:S(2)}) collective-permute-start(f32[256,1280]{1,0:T(8,128)} %collective-permute-done.18), channel_id=1, source_target_pairs={{0,254},{2,0},{4,2},{6,4},{8,6},{10,8},{12,10},{14,12},{16,14},{18... | collective-permute-start | bytes 3932168 | tf_op jit(solution)/shard_map/ppermute | solution.py:16
  96.9 3.9 %copy-start.2 = (f32[256,1280]{1,0:T(8,128)}, f32[256,1280]{1,0:T(8,128)S(1)}, u32[]{:S(2)}) copy-start(f32[256,1280]{1,0:T(8,128)S(1)} %collective-permute-done.3) | copy-start | bytes 3932164
  96.9 39.8 %collective-permute-start.19 = (f32[256,1280]{1,0:T(8,128)}, f32[256,1280]{1,0:T(8,128)}, u32[]{:S(2)}, u32[]{:S(2)}) collective-permute-start(f32[256,1280]{1,0:T(8,128)} %collective-permute-done.16), channel_id=1, source_target_pairs={{0,2},{1,3},{2,4},{3,5},{4,6},{5,7},{6,8},{7,9},{8,10},{9,11},{10,... | collective-permute-start | bytes 3932168 | tf_op jit(solution)/shard_map/ppermute | solution.py:16
  97.4 3.2 %copy-start.11 = (f32[256,1280]{1,0:T(8,128)}, f32[256,1280]{1,0:T(8,128)S(1)}, u32[]{:S(2)}) copy-start(f32[256,1280]{1,0:T(8,128)S(1)} %collective-permute-done.4) | copy-start | bytes 3932164
  100.6 1.5 copy-start.14
  102.1 0.7 copy-start.17
  103.2 30.7 %collective-permute-start.9 = (f32[256]{0:T(256)S(1)}, f32[256]{0:T(256)S(1)}, u32[]{:S(2)}, u32[]{:S(2)}) collective-permute-start(f32[256]{0:T(256)S(1)} %get-tuple-element.34), channel_id=1, source_target_pairs={{1,253},{3,255},{5,1},{7,3},{9,5},{11,7},{13,9},{15,11},{17,13},{1... | collective-permute-start | bytes 3080 | tf_op jit(solution)/shard_map/ppermute | solution.py:16
  113.9 20.0 %collective-permute-start.8 = (f32[256]{0:T(256)S(1)}, f32[256]{0:T(256)S(1)}, u32[]{:S(2)}, u32[]{:S(2)}) collective-permute-start(f32[256]{0:T(256)S(1)} %add_select_fusion), channel_id=1, source_target_pairs={{0,4},{1,5},{2,6},{3,7},{4,8},{5,9},{6,10},{7,11},{8,12},{9,13},{1... | collective-permute-start | bytes 3080 | tf_op jit(solution)/shard_map/ppermute | solution.py:16
  114.0 25.8 %collective-permute-start.5 = (f32[2,256]{1,0:T(2,128)S(1)}, f32[2,256]{1,0:T(2,128)S(1)}, u32[]{:S(2)}, u32[]{:S(2)}) collective-permute-start(f32[2,256]{1,0:T(2,128)S(1)} %pad_maximum_fusion.1), channel_id=1, source_target_pairs={{0,1},{1,0},{2,3},{3,2},{4,5},{5,4},{6,7},{7,6},{8,9},{9,8},{10,11... | collective-permute-start | bytes 6152 | tf_op jit(solution)/shard_map/ppermute | solution.py:21
  134.5 10.0 %copy-start.13 = (f32[256,256]{0,1:T(8,128)S(1)}, f32[256,256]{0,1:T(8,128)}, u32[]{:S(2)}) copy-start(f32[256,256]{0,1:T(8,128)} %fusion.56) | copy-start | bytes 786436
  134.5 5.2 %collective-permute-start.17 = (f32[256]{0:T(256)S(1)}, f32[256]{0:T(256)S(1)}, u32[]{:S(2)}, u32[]{:S(2)}) collective-permute-start(f32[256]{0:T(256)S(1)} %get-tuple-element.28), channel_id=1, source_target_pairs={{0,1},{1,0},{2,3},{3,2},{4,5},{5,4},{6,7},{7,6},{8,9},{9,8},{10,11... | collective-permute-start | bytes 3080 | tf_op jit(solution)/shard_map/ppermute | solution.py:21
  140.5 7.1 %collective-permute-start.11 = (f32[2,256]{1,0:T(2,128)S(1)}, f32[2,256]{1,0:T(2,128)S(1)}, u32[]{:S(2)}, u32[]{:S(2)}) collective-permute-start(f32[2,256]{1,0:T(2,128)S(1)} %pad_maximum_fusion.3), channel_id=1, source_target_pairs={{0,254},{1,255},{2,0},{3,1},{4,2},{5,3},{6,4},{7,5},{8,6},{9,7},{1... | collective-permute-start | bytes 6152 | tf_op jit(solution)/shard_map/ppermute | solution.py:16
  140.5 9.9 %collective-permute-start.10 = (f32[2,256]{1,0:T(2,128)S(1)}, f32[2,256]{1,0:T(2,128)S(1)}, u32[]{:S(2)}, u32[]{:S(2)}) collective-permute-start(f32[2,256]{1,0:T(2,128)S(1)} %pad_maximum_fusion.3), channel_id=1, source_target_pairs={{0,2},{1,3},{2,4},{3,5},{4,6},{5,7},{6,8},{7,9},{8,10},{9,11},{10,... | collective-permute-start | bytes 6152 | tf_op jit(solution)/shard_map/ppermute | solution.py:16
  142.0 8.5 %collective-permute-start.12 = (f32[2,256]{1,0:T(2,128)S(1)}, f32[2,256]{1,0:T(2,128)S(1)}, u32[]{:S(2)}, u32[]{:S(2)}) collective-permute-start(f32[2,256]{1,0:T(2,128)S(1)} %pad_maximum_fusion.3), channel_id=1, source_target_pairs={{0,252},{1,253},{2,254},{3,255},{4,0},{5,1},{6,2},{7,3},{8,4},{9,5... | collective-permute-start | bytes 6152 | tf_op jit(solution)/shard_map/ppermute | solution.py:16
  142.0 8.9 %collective-permute-start.13 = (f32[2,256]{1,0:T(2,128)S(1)}, f32[2,256]{1,0:T(2,128)S(1)}, u32[]{:S(2)}, u32[]{:S(2)}) collective-permute-start(f32[2,256]{1,0:T(2,128)S(1)} %pad_maximum_fusion.3), channel_id=1, source_target_pairs={{0,4},{1,5},{2,6},{3,7},{4,8},{5,9},{6,10},{7,11},{8,12},{9,13},{1... | collective-permute-start | bytes 6152 | tf_op jit(solution)/shard_map/ppermute | solution.py:16
  144.6 1.5 copy-start.21
  146.1 1.5 copy-start.7
  147.6 3.3 %copy-start.5 = (f32[512,256]{0,1:T(8,128)S(1)}, f32[512,256]{0,1:T(8,128)}, u32[]{:S(2)}) copy-start(f32[512,256]{0,1:T(8,128)} %copy-done.4) | copy-start | bytes 1572868
  150.9 3.2 %copy-start.3 = (f32[256,1280]{1,0:T(8,128)S(1)}, f32[256,1280]{1,0:T(8,128)}, u32[]{:S(2)}) copy-start(f32[256,1280]{1,0:T(8,128)} %copy-done.2) | copy-start | bytes 3932164
  150.9 3.2 %copy-start.12 = (f32[256,1280]{1,0:T(8,128)S(1)}, f32[256,1280]{1,0:T(8,128)}, u32[]{:S(2)}) copy-start(f32[256,1280]{1,0:T(8,128)} %copy-done.11) | copy-start | bytes 3932164
  151.0 3.2 %copy-start.15 = (f32[256,256]{1,0:T(8,128)S(1)}, f32[256,256]{1,0:T(8,128)}, u32[]{:S(2)}) copy-start(f32[256,256]{1,0:T(8,128)} %copy-done.14) | copy-start | bytes 786436
  154.1 2.0 copy-start.8
  154.2 3.8 %copy-start.19 = (f32[512,256]{0,1:T(8,128)S(1)}, f32[512,256]{0,1:T(8,128)}, u32[]{:S(2)}) copy-start(f32[512,256]{0,1:T(8,128)} %convolution_multiply_fusion) | copy-start | bytes 1572868
  156.2 109.1 %collective-permute-start.14 = (f32[256,1280]{1,0:T(8,128)}, f32[256,1280]{1,0:T(8,128)}, u32[]{:S(2)}, u32[]{:S(2)}) collective-permute-start(f32[256,1280]{1,0:T(8,128)} %convolution_add_fusion.4), channel_id=1, source_target_pairs={{0,1},{1,0},{2,3},{3,2},{4,5},{5,4},{6,7},{7,6},{8,9},{9,8},{10,11... | collective-permute-start | bytes 3932168 | tf_op jit(solution)/shard_map/ppermute | solution.py:21
  157.9 2.8 %copy-start.20 = (f32[512,256]{0,1:T(8,128)S(1)}, f32[512,256]{0,1:T(8,128)}, u32[]{:S(2)}) copy-start(f32[512,256]{0,1:T(8,128)} %convolution_multiply_fusion.2) | copy-start | bytes 1572868
  163.8 4.2 %copy-start.9 = (f32[512,1280]{1,0:T(8,128)}, f32[512,1280]{1,0:T(8,128)S(1)}, u32[]{:S(2)}) copy-start(f32[512,1280]{1,0:T(8,128)S(1)} %fusion) | copy-start | bytes 7864324
  168.0 101.0 %collective-permute-start.21 = (f32[256,1280]{1,0:T(8,128)}, f32[256,1280]{1,0:T(8,128)}, u32[]{:S(2)}, u32[]{:S(2)}) collective-permute-start(f32[256,1280]{1,0:T(8,128)} %convolution_add_fusion.2), channel_id=1, source_target_pairs={{0,1},{1,0},{2,3},{3,2},{4,5},{5,4},{6,7},{7,6},{8,9},{9,8},{10,11... | collective-permute-start | bytes 3932168 | tf_op jit(solution)/shard_map/ppermute | solution.py:21
  170.6 9.3 %copy-start.16 = (f32[256,256]{1,0:T(8,128)S(1)}, f32[256,256]{1,0:T(8,128)}, u32[]{:S(2)}) copy-start(f32[256,256]{1,0:T(8,128)} %copy-done.14) | copy-start | bytes 786436
  181.3 83.9 %copy-start.18 = (f32[256,256]{1,0:T(8,128)S(1)}, f32[256,256]{1,0:T(8,128)}, u32[]{:S(2)}) copy-start(f32[256,256]{1,0:T(8,128)} %copy-done.17) | copy-start | bytes 786436
  265.2 3.8 %copy-start.10 = (f32[512,1280]{1,0:T(8,128)S(1)}, f32[512,1280]{1,0:T(8,128)}, u32[]{:S(2)}) copy-start(f32[512,1280]{1,0:T(8,128)} %copy-done.9) | copy-start | bytes 7864324

commit v2 on v0

v2 whole, which is shorter than its diff:
```python
import functools

import jax
import jax.numpy as jnp
from jax import lax
from jax.experimental import pallas as pl
from jax.experimental.pallas import tpu as pltpu
from jax.sharding import PartitionSpec as P

WIN = 8
BOTH = (0, 1)
LIMIT = 10 * 1024 * 1024
TILE = 256
F32 = jnp.float32
BF16 = jnp.bfloat16
VMEM = pl.BlockSpec(memory_space=pltpu.VMEM)
SMEM = pl.BlockSpec(memory_space=pltpu.SMEM)
ANY = pl.BlockSpec(memory_space=pl.ANY)


def shift(value, steps, cores=BOTH):
    count = lax.axis_size("dp")
    pairs = [(s, (s + steps) % count) for s in range(count) if s % 2 in cores]
    return lax.ppermute(value, "dp", pairs)


def swap(value, bit=1):
    count = lax.axis_size("dp")
    return lax.ppermute(value, "dp", [(s, s ^ bit) for s in range(count)])


def after(value, *done):
    return lax.optimization_barrier((value, done))[0]


def call(kernel, name, micros, outs, args, scratch=(), out_space=VMEM, alias=None):
    return pl.pallas_call(
        kernel,
        name=name,
        out_shape=[jax.ShapeDtypeStruct(s, d) for s, d in outs],
        in_specs=[SMEM] + [VMEM] * (len(args) - 1),
        out_specs=[out_space] * len(outs),
        scratch_shapes=[
            pltpu.VMEM(*x) if isinstance(x, tuple) else x for x in scratch
        ],
        compiler_params=pltpu.CompilerParams(vmem_limit_bytes=LIMIT),
        input_output_aliases=alias or {},
        cost_estimate=pl.CostEstimate(
            flops=int(micros * 1.15e9), bytes_accessed=1, transcendentals=0
        ),
    )(*args)


def dot_nt(a, b):
    return lax.dot_general(a, b, (((1,), (1,)), ((), ())), preferred_element_type=F32)


def dot_nn(a, b):
    return lax.dot_general(a, b, (((1,), (0,)), ((), ())), preferred_element_type=F32)


def two(x):
    h = x.astype(BF16)
    return h, (x - h.astype(F32)).astype(BF16)


def three(x):
    h = x.astype(BF16)
    r = x - h.astype(F32)
    m = r.astype(BF16)
    return h, m, (r - m.astype(F32)).astype(BF16)


def scores(a, b):
    (ah, am, al), (bh, bm, bl) = a, b
    small = dot_nt(ah, bl) + dot_nt(al, bh) + dot_nt(am, bm)
    return (small + (dot_nt(ah, bm) + dot_nt(am, bh))) + dot_nt(ah, bh)


def put_three(x, h, m, l):
    h[...], m[...], l[...] = three(x)


def take(refs, rows=slice(None)):
    return tuple(r[rows] for r in refs)


def column(v):
    return jnp.transpose(jnp.broadcast_to(v, (8, v.shape[1])))[:, :1]


def row(v):
    return jnp.transpose(jnp.broadcast_to(v, (v.shape[0], 128)))[:1]


def stat(tops, sums, means):
    top = functools.reduce(jnp.maximum, tops)
    total = sum(jnp.exp(t - top) * s for t, s in zip(tops, sums))
    mean = sum(jnp.exp(t - top) * m for t, m in zip(tops, means))
    return top + jnp.log(total), mean / total


def merge(parts):
    return stat([p[0] for p in parts], [1.0] * len(parts), [p[1] for p in parts])


def lse(blocks, axis):
    top = functools.reduce(
        jnp.maximum, [jnp.max(b, axis=axis, keepdims=True) for b in blocks]
    )
    total, mean = 0.0, 0.0
    for b in blocks:
        e = jnp.exp(b - top)
        total += jnp.sum(e, axis=axis, keepdims=True)
        mean += jnp.sum(e * b, axis=axis, keepdims=True)
    return top + jnp.log(total), mean / total


def own_kernel(s, a0, a1, b0, h, m, l, out, bh, bm, bl):
    n = a0.shape[0]
    for k, a in enumerate((a0, a1)):
        r = pl.ds(k * n, n)
        h[r], m[r], l[r] = three(a[...])
    put_three(b0[...], bh, bm, bl)
    out[...] = s[0] * scores(take((h, m, l)), take((bh, bm, bl)))


def near_kernel(s, h, m, l, b0, bp, bm, lp, lm, blocks_h, blocks_l, *parts):
    n = b0.shape[0]
    r = pl.ds(n, n)
    blocks_h[r], blocks_l[r] = two(b0[...])
    for k, (block, out) in enumerate(((bp, lp), (bm, lm))):
        put_three(block[...], *parts)
        r = pl.ds((k + 2) * n, n)
        blocks_h[r], blocks_l[r] = parts[0][...], parts[1][...]
        out[...] = s[0] * scores(take((h, m, l)), take(parts))


def near_stats_kernel(s, l0, lp, lm, top, mean, diag):
    n = l0.shape[1]
    t, m = lse([l0[...], lp[...], lm[...]], 1)
    top[...] = jnp.broadcast_to(t, top.shape)
    mean[...] = jnp.broadcast_to(m, mean.shape)
    i = lax.broadcasted_iota(jnp.int32, (n, n), 0)
    j = lax.broadcasted_iota(jnp.int32, (n, n), 1)
    diag[...] = jnp.sum(jnp.where(i == j, l0[0:n, :], 0.0), axis=0, keepdims=True)


def other_far(s, a, b, text):
    first = s[1] == 0.0
    return jnp.where(first, b[...], a[...]) if text else jnp.where(first, a[...], b[...])


def far_scores(s, parts, a, b, text, top, mean, lf, rows_out, blocks_h, blocks_l, *split):
    n = a.shape[0]
    for k, block in enumerate((a[...], other_far(s, a, b, text))):
        put_three(block, *split)
        r = pl.ds(4 * k * n, n)
        blocks_h[r], blocks_l[r] = split[0][...], split[1][...]
        r = pl.ds(k * n, n)
        lf[r, :] = s[0] * scores(take(parts, r), take(split))
    t, m = merge([(top[:, :1], mean[:, :1]), lse([lf[...]], 1)])
    rows_out[0:1, :] = row(t[:n])
    rows_out[1:2, :] = row(m[:n])
    rows_out[2:3, :] = row(t[n:])
    rows_out[3:4, :] = row(m[n:])


def text_far_kernel(s, xh, xm, xl, a, b, top, mean, old_h, old_l, lf, rows_out, *rest):
    far_scores(s, (xh, xm, xl), a, b, False, top, mean, lf, rows_out, *rest)


def image_far_kernel(s, yh, ym, yl, a, b, top, mean, old_h, old_l, image_rows, diag, lf, out, *rest):
    far_scores(s, (yh, ym, yl), a, b, True, top, mean, lf, out.at[4:8], *rest)
    out[0:4, :] = image_rows[...]
    out[8:9, :] = diag[...]
    out[9:16, :] = jnp.zeros((7, out.shape[1]), F32)


def merge_kernel(s, mine, got, out):
    pair = lambda ref, k: (ref[k : k + 1, :], ref[k + 1 : k + 2, :])
    n = out.shape[1]
    terms = []
    for k, ref, j in ((0, mine, 2), (2, got, 0)):
        row_stat = merge([pair(mine, k), pair(got, j)])
        col_stat = merge([pair(mine, k + 4), pair(got, j + 4)])
        out[k : k + 1, :] = row_stat[0]
        out[k + 1 : k + 2, :] = col_stat[0]
        diag = ref[8:9, :]
        terms.append(
            [
                jnp.sum(r + c - 2.0 * diag, axis=1, keepdims=True)
                for r, c in zip(row_stat, col_stat)
            ]
        )
    for k in range(2):
        both = terms[0][k] + terms[1][k]
        out[4 + k : 5 + k, :] = jnp.broadcast_to(both, (1, n))
    out[6:8, :] = jnp.zeros((2, n), F32)


def mate_kernel(s, own, m2, p2, out):
    out[...] = jnp.zeros_like(out)
    out[0:2, :] = own[4:6, :128] + jnp.where(s[2] == 0.0, p2[4:6, :128], m2[4:6, :128])


def sum_kernel(s, *refs):
    *terms, out = refs
    values = [t[...] for t in terms]
    while len(values) > 1:
        values = [a + b for a, b in zip(values[::2], values[1::2])]
    out[...] = values[0]


def last_kernel(s, a, b, loss, scale_grad):
    total = (a[...] + b[...]) * (1.0 / s[3])
    loss[...] = total[0:1, 0:1]
    scale_grad[...] = total[1:2, 0:1] / s[0]


def weigh(x, side, m):
    return jnp.exp(x - side) + jnp.exp(x - m)


def less_twice_eye(w):
    i = lax.broadcasted_iota(jnp.int32, w.shape, 0)
    j = lax.broadcasted_iota(jnp.int32, w.shape, 1)
    return jnp.where(i == j, w - 2.0, w)


def put_weights(text, sib, s, own, m2, p2, m4, p4, l0, lp, lm, lf, wh, wl):
    n = l0.shape[1]
    first = s[1] == 0.0
    rows = pl.ds(n if sib else 0, n)
    k = (2 if sib else 0) + (1 if text else 0)
    side = column(own[k : k + 1, :])
    other = slice(0, 1) if text else slice(1, 2)
    ahead, behind = p4[other, :], m4[other, :]
    if sib:
        far = jnp.where(first, ahead, behind)
    else:
        far = behind if text else ahead
    near = [(l0, own[other, :]), (lp, m2[other, :]), (lm, p2[other, :])]
    pieces = near + [(lf, far)] if sib else [(lf, far)] + near
    for k, (v, m) in enumerate(pieces):
        w = weigh(v[rows, :], side, m)
        if v is l0 and not sib:
            w = less_twice_eye(w)
        at = pl.ds(k * n, n)
        wh[:, at], wl[:, at] = two(w)


def tile_grads(wh, wl, bh, bl, rows, d):
    h, l = wh[...], wl[...]
    return (dot_nn(h, bl[rows, d]) + dot_nn(l, bh[rows, d])) + dot_nn(h, bh[rows, d])


def share_kernel(text, *refs):
    *args, bh, bl, out, wh, wl = refs
    put_weights(text, True, *args, wh, wl)
    n = out.shape[0]
    for k in range(out.shape[1] // TILE):
        d = pl.ds(k * TILE, TILE)
        out[:, d] = tile_grads(wh, wl, bh, bl, pl.ds(n, 4 * n), d)


def grads_kernel(text, *refs):
    *args, bh, bl, share, out, wh, wl, done, sem = refs
    put_weights(text, False, *args, wh, wl)
    n = share.shape[0]
    factor = 0.5 * args[0][0]
    copies = []
    for k in range(out.shape[1] // TILE):
        d = pl.ds(k * TILE, TILE)
        done[:, d] = factor * (
            tile_grads(wh, wl, bh, bl, pl.ds(0, 4 * n), d) + share[:, d]
        )
        copies.append(pltpu.make_async_copy(done.at[:, d], out.at[:, d], sem.at[k]))
        copies[-1].start()
    for copy in copies:
        copy.wait()


def on_device(image, text, scale):
    n, depth = image.shape
    device = lax.axis_index("dp")
    core, odd = (device % 2).astype(F32), (device // 2 % 2).astype(F32)
    s = jnp.stack([scale, core, odd, jnp.float32(2 * n * lax.axis_size("dp"))])
    block = ((n, depth), F32)
    both = ((2 * n, n), F32)
    part = ((2 * n, depth), BF16)
    wide = ((2 * n, 128), F32)
    four, line = ((4, n), F32), ((1, n), F32)
    split = [((n, depth), BF16)] * 3

    t_p, t_m = shift(text, 2), shift(text, -2)
    i_s, t_s = swap(image), swap(text)
    i_p, i_m = shift(image, 2), shift(image, -2)
    args = s, after(image, t_s), i_s, text
    *x, l0 = call(own_kernel, "text_own", 3.7, [part] * 3 + [both], args, split)
    args = s, after(text, l0), t_s, image
    *y, v0 = call(own_kernel, "image_own", 3.7, [part] * 3 + [both], args, split)
    t_p, t_m = after(t_p, v0), after(t_m, v0)
    t_pp, t_mm = shift(t_p, 2, (1,)), shift(t_m, -2)
    five = [((5 * n, depth), BF16)] * 2
    near_outs = [both] * 2 + five
    args = s, *x, text, t_p, t_m
    lp, lm, *t_parts = call(near_kernel, "text_near", 4.8, near_outs, args, split)
    args = s, l0, lp, lm
    top, mean, diag = call(near_stats_kernel, "text_stats", 1.8, [wide] * 2 + [line], args)
    i_p, i_m = after(i_p, top), after(i_m, top)
    i_pp, i_mm = shift(i_p, 2), shift(i_m, -2, (0,))
    args = s, *y, image, i_p, i_m
    vp, vm, *i_parts = call(near_kernel, "image_near", 4.8, near_outs, args, split)
    args = s, v0, vp, vm
    i_top, i_mean, _ = call(near_stats_kernel, "image_stats", 1.8, [wide] * 2 + [line], args)
    args = s, *x, after(t_mm, i_top), t_pp, top, mean, *t_parts
    outs = [both, four] + five
    kept = {8: 2, 9: 3}
    lf, image_rows, *t_parts = call(text_far_kernel, "text_far", 4.0, outs, args, split, alias=kept)
    args = s, *y, after(i_pp, lf), i_mm, i_top, i_mean, *i_parts, image_rows, diag
    outs = [both, ((16, n), F32)] + five
    vf, mine, *i_parts = call(image_far_kernel, "image_far", 4.0, outs, args, split, alias=kept)

    got = swap(mine)
    (own,) = call(merge_kernel, "merge", 0.6, [((8, n), F32)], (s, mine, got))
    m2, p2 = shift(own, 2), shift(own, -2)
    m4, p4 = shift(own, 4), shift(own, -4)
    terms = [((8, 128), F32)]
    (parts,) = call(mate_kernel, "pair", 0.5, terms, (s, own, m2, after(p2, m4, p4)))

    lses = m2, p2, m4, p4
    image_args = l0, lp, lm, lf, *t_parts
    text_args = v0, vp, vm, vf, *i_parts
    weights = [((n, 4 * n), BF16)] * 2
    final = weights + [block, pltpu.SemaphoreType.DMA((depth // TILE,))]
    kernel = functools.partial(share_kernel, False)
    args = s, own, *lses, *image_args
    (share,) = call(kernel, "image_share", 3.7, [block], args, weights)
    image_share = swap(share)
    y_parts = swap(parts, 16), swap(parts, 32), swap(parts, 48)
    args = s, after(parts, share), *y_parts
    (parts,) = call(sum_kernel, "sum_y", 0.5, terms, args)
    x_parts = swap(parts, 64), swap(parts, 128), swap(parts, 192)
    kernel = functools.partial(share_kernel, True)
    args = s, after(own, parts), *lses, *text_args
    (share,) = call(kernel, "text_share", 3.7, [block], args, weights)
    text_share = swap(share)
    args = s, after(parts, share), *x_parts
    (parts,) = call(sum_kernel, "sum_x", 0.5, terms, args)
    z_part = swap(parts, 4)
    kernel = functools.partial(grads_kernel, False)
    args = s, after(own, parts), *lses, *image_args, image_share
    (image_grad,) = call(kernel, "image_grads", 3.9, [block], args, final, ANY)
    args = s, after(parts, image_grad), z_part
    (parts,) = call(sum_kernel, "sum_z", 0.5, terms, args)
    z_part = swap(parts, 8)
    kernel = functools.partial(grads_kernel, True)
    args = s, after(own, parts), *lses, *text_args, text_share
    (text_grad,) = call(kernel, "text_grads", 3.9, [block], args, final, ANY)
    args = s, after(parts, text_grad), z_part
    loss, scale_grad = call(last_kernel, "last", 0.5, [((1, 1), F32)] * 2, args)
    return (loss.reshape(()), image_grad, text_grad, scale_grad.reshape(()))


def solution(mesh):
    in_specs = (P("dp", None), P("dp", None), P())
    out_specs = (P(), P("dp", None), P("dp", None), P())
    return jax.shard_map(
        on_device, mesh=mesh, in_specs=in_specs, out_specs=out_specs, check_vma=False
    )
```

time: 594 us -> 188 us (0.32)
  blocking collectives: 166 us -> 0 us
  waiting for transfers between devices: 232 us -> 74.3 us
  starting transfers between devices: 117 us -> 59 us
  Pallas kernels: 0 us -> 47.2 us
  matrix products: 47 us -> 0 us
  between operations: 12.7 us -> 1.73 us
  other arithmetic: 7.32 us -> 0.08 us
    psum x1 -> x0, blocking collectives: 166 us -> none  [on_device(): loss_total, scale_total = lax.psum((loss_part, scale_acc), 'dp')]
    ppermute x40 -> x25, waiting for transfers between devices: 232 us -> 74.3 us  [the longest x12 64.3 us: shift(): return lax.ppermute(value, 'dp', pairs)]
    ppermute x40 -> x25, starting transfers between devices: 117 us -> 59 us  [the longest x12 32.3 us: shift(): return lax.ppermute(value, 'dp', pairs)]
    pallas_call x0 -> x18, Pallas kernels: none -> 47.2 us  [call(): pl.pallas_call(kernel, name=name, out_shape=[jax.ShapeDtypeStruct(s, d) f...]
    dot_general x24 -> x0, matrix products: 47 us -> none  [the longest x8 19.6 us: on_device(): jnp.dot(weights, text_block, precision=precise, preferred_element_type=jn...]
  transfers between devices with their start and end apart: 40 -> 25, of which waited for: 23 -> 15; matrix products, arithmetic and copies ran while one was open for 7% -> 0% of each run, Pallas kernels for 0% -> 21%
where the time goes in v2:
time: 188 us; the launch traced here: 185 us
  waiting for transfers between devices  74.3 us (40%)
  starting transfers between devices  59 us (31%)
  Pallas kernels  47.2 us (25%)
  local copies, waits for them, and re-layouts  2.64 us (1%)
    ppermute x12, waiting for transfers between devices, shift(): return lax.ppermute(value, 'dp', pairs)  64.3 us
    pallas_call x18, Pallas kernels, call(): pl.pallas_call(kernel, name=name, out_shape=[jax.ShapeDtypeStruct(s, d) f...  47.2 us
    ppermute x12, starting transfers between devices, shift(): return lax.ppermute(value, 'dp', pairs)  32.3 us
    ppermute x13, starting transfers between devices, swap(): return lax.ppermute(value, 'dp', [(s, s ^ bit) for s in range(count)])  26.7 us
    ppermute x13, waiting for transfers between devices, swap(): return lax.ppermute(value, 'dp', [(s, s ^ bit) for s in range(count)])  10 us
  transfers between devices with their start and end apart: 25, of which 15 were waited for; matrix products, arithmetic and copies ran while one was open for 0% of the time, Pallas kernels for 21%

profile of v2, /device:TPU:8, one launch (start us, length us, event | category | flops | bytes accessed | tf_op | source)
XLA Modules:
  0.0 185.0 jit_solution(7336824735345197003)
XLA Ops:
  0.7 0.5 collective-permute-start.1
  1.2 5.7 %collective-permute-start.4 = (f32[256,1280]{1,0:T(8,128)}, f32[256,1280]{1,0:T(8,128)S(1)}, u32[]{:S(2)}, u32[]{:S(2)}) collective-permute-start(f32[256,1280]{1,0:T(8,128)} %b0.6), channel_id=1, source_target_pairs={{0,254},{1,255},{2,0},{3,1},{4,2},{5,3},{6,4},{7,5},{8,6},{9,7},{1... | collective-permute-start | bytes 3932168 | tf_op jit(solution)/shard_map/ppermute | solution.py:24
  7.7 4.2 %collective-permute-start.7 = (f32[256,1280]{1,0:T(8,128)}, f32[256,1280]{1,0:T(8,128)S(1)}, u32[]{:S(2)}, u32[]{:S(2)}) collective-permute-start(f32[256,1280]{1,0:T(8,128)} %b0.7), channel_id=1, source_target_pairs={{0,254},{1,255},{2,0},{3,1},{4,2},{5,3},{6,4},{7,5},{8,6},{9,7},{1... | collective-permute-start | bytes 3932168 | tf_op jit(solution)/shard_map/ppermute | solution.py:24
  11.9 1.3 copy-done
  13.2 1.3 copy-done.1
  14.5 3.7 %text_own.1 = (bf16[512,1280]{1,0:T(8,128)(2,1)S(1)}, bf16[512,1280]{1,0:T(8,128)(2,1)S(1)}, bf16[512,1280]{1,0:T(8,128)(2,1)S(1)}, f32[512,256]{1,0:T(8,128)S(1)}) custom-call(f32[4]{0:T(128)S(1)} %pad_maximum_fusion.s.refs_0_, f32[256,1280]{1,0:T(8,128)S(1)} %copy-done.1, f32[256,1280]{1,0:T(8,128)} %collective-permute-done.1.a1, f32[256,1280]{1,0:T(8,128)S(1)} %copy-done), custom_call_target="tpu_custom_call" | custom-call | flops 4255000064 | bytes 1 | tf_op jit(solution)/shard_map/text_own/pallas_call | solution.py:37
  18.2 3.6 %image_own.1 = (bf16[512,1280]{1,0:T(8,128)(2,1)S(1)}, bf16[512,1280]{1,0:T(8,128)(2,1)S(1)}, bf16[512,1280]{1,0:T(8,128)(2,1)S(1)}, f32[512,256]{1,0:T(8,128)S(1)}) custom-call(f32[4]{0:T(128)S(1)} %pad_maximum_fusion.s.refs_0_, f32[256,1280]{1,0:T(8,128)S(1)} %copy-done, f32[256,1280]{1,0:T(8,128)} %collective-permute-done.a1, f32[256,1280]{1,0:T(8,128)S(1)} %copy-done.2), custom_call_target="tpu_custom_call" | custom-call | flops 4255000064 | bytes 1 | tf_op jit(solution)/shard_map/image_own/pallas_call | solution.py:37
  21.9 14.6 %collective-permute-done.4.bm = f32[256,1280]{1,0:T(8,128)S(1)} collective-permute-done((f32[256,1280]{1,0:T(8,128)}, f32[256,1280]{1,0:T(8,128)S(1)}, u32[]{:S(2)}, u32[]{:S(2)}) %collective-permute-start.4) | collective-permute-done | bytes 1310752 | tf_op jit(solution)/shard_map/ppermute | solution.py:24
  36.4 4.6 %collective-permute-done.3.bp = f32[256,1280]{1,0:T(8,128)} collective-permute-done((f32[256,1280]{1,0:T(8,128)}, f32[256,1280]{1,0:T(8,128)}, u32[]{:S(2)}, u32[]{:S(2)}) %collective-permute-start.3) | collective-permute-done | bytes 1310752 | tf_op jit(solution)/shard_map/ppermute | solution.py:24
  41.1 0.7 collective-permute-start.8
  41.8 0.3 collective-permute-start.6
  42.2 6.0 %text_near.1 = (f32[512,256]{1,0:T(8,128)S(1)}, f32[512,256]{1,0:T(8,128)S(1)}, bf16[1280,1280]{1,0:T(8,128)(2,1)S(1)}, bf16[1280,1280]{1,0:T(8,128)(2,1)S(1)}) custom-call(f32[4]{0:T(128)S(1)} %pad_maximum_fusion.s.refs_0_, bf16[512,1280]{1,0:T(8,128)(2,1)S(1)} %get-tuple-element.57.h.xh, bf16[512,1280]{1,0:T(8,128)(2,1)S(1)} %get-tuple-element.58.m.xm, ...), custom_call_target="tpu_custom_call" | custom-call | flops 5520000000 | bytes 1 | tf_op jit(solution)/shard_map/text_near/pallas_call | solution.py:37
  48.2 1.3 text_stats.1
  49.5 19.5 %collective-permute-done.2.bp = f32[256,1280]{1,0:T(8,128)S(1)} collective-permute-done((f32[256,1280]{1,0:T(8,128)}, f32[256,1280]{1,0:T(8,128)S(1)}, u32[]{:S(2)}, u32[]{:S(2)}) %collective-permute-start.2) | collective-permute-done | bytes 1310752 | tf_op jit(solution)/shard_map/ppermute | solution.py:24
  69.1 6.0 %collective-permute-start.9 = (f32[256,1280]{1,0:T(8,128)S(1)}, f32[256,1280]{1,0:T(8,128)S(1)}, u32[]{:S(2)}, u32[]{:S(2)}) collective-permute-start(f32[256,1280]{1,0:T(8,128)S(1)} %collective-permute-done.7.bm), channel_id=1, source_target_pairs={{0,254},{2,0},{4,2},{6,4},{8,6},{10,8},{12,10},{14,12},{16,14},{18... | collective-permute-start | bytes 3932168 | tf_op jit(solution)/shard_map/ppermute | solution.py:24
  75.1 5.2 %image_near.1 = (f32[512,256]{1,0:T(8,128)S(1)}, f32[512,256]{1,0:T(8,128)S(1)}, bf16[1280,1280]{1,0:T(8,128)(2,1)S(1)}, bf16[1280,1280]{1,0:T(8,128)(2,1)S(1)}) custom-call(f32[4]{0:T(128)S(1)} %pad_maximum_fusion.s.refs_0_, bf16[512,1280]{1,0:T(8,128)(2,1)S(1)} %get-tuple-element.54.h.yh, bf16[512,1280]{1,0:T(8,128)(2,1)S(1)} %get-tuple-element.55.m.ym, ...), custom_call_target="tpu_custom_call" | custom-call | flops 5520000000 | bytes 1 | tf_op jit(solution)/shard_map/image_near/pallas_call | solution.py:37
  80.3 1.9 %image_stats.1 = (f32[512,128]{1,0:T(8,128)S(1)}, f32[512,128]{1,0:T(8,128)S(1)}, f32[1,256]{1,0:T(1,128)}) custom-call(f32[4]{0:T(128)S(1)} %pad_maximum_fusion.s.refs_0_, f32[512,256]{1,0:T(8,128)S(1)} %get-tuple-element.60.l0.refs_6_, f32[512,256]{1,0:T(8,128)S(1)} %get-tuple-element.68.lp.refs_7_, f32[512,256]{1,0:T(8,128)S(1)} %get-tuple-element.69.lm.refs_8_), custom_call_target="tpu_custom_call" | custom-call | flops 2070000000 | bytes 1 | tf_op jit(solution)/shard_map/image_stats/pallas_call | solution.py:37
  82.2 9.4 %collective-permute-done.6.a = f32[256,1280]{1,0:T(8,128)S(1)} collective-permute-done((f32[256,1280]{1,0:T(8,128)S(1)}, f32[256,1280]{1,0:T(8,128)S(1)}, u32[]{:S(2)}, u32[]{:S(2)}) %collective-permute-start.6) | collective-permute-done | bytes 1310752 | tf_op jit(solution)/shard_map/ppermute | solution.py:24
  91.7 3.6 %text_far.1 = (f32[512,256]{1,0:T(8,128)S(1)}, f32[4,256]{1,0:T(4,128)S(1)}, bf16[1280,1280]{1,0:T(8,128)(2,1)S(1)}, bf16[1280,1280]{1,0:T(8,128)(2,1)S(1)}) custom-call(f32[4]{0:T(128)S(1)} %pad_maximum_fusion.s.refs_0_, bf16[512,1280]{1,0:T(8,128)(2,1)S(1)} %get-tuple-element.57.h.xh, ...), custom_call_target="tpu_custom_call", output_to_operand_aliasing={{2}: (8, {}), {3}: (9, {})} | custom-call | flops 4600000000 | bytes 1 | tf_op jit(solution)/shard_map/text_far/pallas_call | solution.py:37
  95.3 7.6 %collective-permute-done.5.a = f32[256,1280]{1,0:T(8,128)S(1)} collective-permute-done((f32[256,1280]{1,0:T(8,128)S(1)}, f32[256,1280]{1,0:T(8,128)S(1)}, u32[]{:S(2)}, u32[]{:S(2)}) %collective-permute-start.5) | collective-permute-done | bytes 1310752 | tf_op jit(solution)/shard_map/ppermute | solution.py:24
  102.9 2.8 %collective-permute-done.9.b = f32[256,1280]{1,0:T(8,128)S(1)} collective-permute-done((f32[256,1280]{1,0:T(8,128)S(1)}, f32[256,1280]{1,0:T(8,128)S(1)}, u32[]{:S(2)}, u32[]{:S(2)}) %collective-permute-start.9) | collective-permute-done | bytes 1310752 | tf_op jit(solution)/shard_map/ppermute | solution.py:24
  105.7 3.6 %image_far.1 = (f32[512,256]{1,0:T(8,128)S(1)}, f32[16,256]{1,0:T(8,128)S(1)}, bf16[1280,1280]{1,0:T(8,128)(2,1)S(1)}, bf16[1280,1280]{1,0:T(8,128)(2,1)S(1)}) custom-call(f32[4]{0:T(128)S(1)} %pad_maximum_fusion.s.refs_0_, bf16[512,1280]{1,0:T(8,128)(2,1)S(1)} %get-tuple-element.54.h.yh, ...), custom_call_target="tpu_custom_call", output_to_operand_aliasing={{2}: (8, {}), {3}: (9, {})} | custom-call | flops 4600000000 | bytes 1 | tf_op jit(solution)/shard_map/image_far/pallas_call | solution.py:37
  109.3 4.2 %collective-permute-start.10 = (f32[16,256]{1,0:T(8,128)S(1)}, f32[16,256]{1,0:T(8,128)S(1)}, u32[]{:S(2)}, u32[]{:S(2)}) collective-permute-start(f32[16,256]{1,0:T(8,128)S(1)} %get-tuple-element.82.mine), channel_id=1, source_target_pairs={{0,1},{1,0},{2,3},{3,2},{4,5},{5,4},{6,7},{7,6},{8,9},{9,8},{10,11... | collective-permute-start | bytes 49160 | tf_op jit(solution)/shard_map/ppermute | solution.py:29
  113.5 0.8 collective-permute-done.10.got
  114.4 0.6 merge.1.own.refs_1_
  115.0 2.9 %collective-permute-start.13 = (f32[8,256]{1,0:T(8,128)S(1)}, f32[8,256]{1,0:T(8,128)S(1)}, u32[]{:S(2)}, u32[]{:S(2)}) collective-permute-start(f32[8,256]{1,0:T(8,128)S(1)} %merge.1.own.refs_1_), channel_id=1, source_target_pairs={{0,4},{1,5},{2,6},{3,7},{4,8},{5,9},{6,10},{7,11},{8,12},{9,13},{1... | collective-permute-start | bytes 24584 | tf_op jit(solution)/shard_map/ppermute | solution.py:24
  118.0 2.9 %collective-permute-start.12 = (f32[8,256]{1,0:T(8,128)S(1)}, f32[8,256]{1,0:T(8,128)S(1)}, u32[]{:S(2)}, u32[]{:S(2)}) collective-permute-start(f32[8,256]{1,0:T(8,128)S(1)} %merge.1.own.refs_1_), channel_id=1, source_target_pairs={{0,254},{1,255},{2,0},{3,1},{4,2},{5,3},{6,4},{7,5},{8,6},{9,7},{1... | collective-permute-start | bytes 24584 | tf_op jit(solution)/shard_map/ppermute | solution.py:24
  120.9 9.4 %collective-permute-start.11 = (f32[8,256]{1,0:T(8,128)S(1)}, f32[8,256]{1,0:T(8,128)S(1)}, u32[]{:S(2)}, u32[]{:S(2)}) collective-permute-start(f32[8,256]{1,0:T(8,128)S(1)} %merge.1.own.refs_1_), channel_id=1, source_target_pairs={{0,2},{1,3},{2,4},{3,5},{4,6},{5,7},{6,8},{7,9},{8,10},{9,11},{10,... | collective-permute-start | bytes 24584 | tf_op jit(solution)/shard_map/ppermute | solution.py:24
  130.3 5.7 %collective-permute-done.11.m2.refs_2_ = f32[8,256]{1,0:T(8,128)S(1)} collective-permute-done((f32[8,256]{1,0:T(8,128)S(1)}, f32[8,256]{1,0:T(8,128)S(1)}, u32[]{:S(2)}, u32[]{:S(2)}) %collective-permute-start.11) | collective-permute-done | bytes 8224 | tf_op jit(solution)/shard_map/ppermute | solution.py:24
  136.0 3.1 %image_share.1 = f32[256,1280]{1,0:T(8,128)S(1)} custom-call(f32[4]{0:T(128)S(1)} %pad_maximum_fusion.s.refs_0_, f32[8,256]{1,0:T(8,128)S(1)} %merge.1.own.refs_1_, f32[8,256]{1,0:T(8,128)S(1)} %collective-permute-done.11.m2.refs_2_, f32[8,256]{1,0:T(8,128)S(1)} %collective-permute-done.12.p2.refs_3_, f32[8,256]{1,0:T(8,128)S(1)} %collective-permute-done.13.refs_4_, ...), custom_call_target="tpu_custom_call" | custom-call | flops 4255000064 | bytes 1 | tf_op jit(solution)/shard_map/image_share/pallas_call | solution.py:37
  139.3 0.6 pair.1.refs_0_
  139.9 1.7 collective-permute-start.17
  141.5 15.7 %collective-permute-start.16 = (f32[8,128]{1,0:T(8,128)S(1)}, f32[8,128]{1,0:T(8,128)S(1)}, u32[]{:S(2)}, u32[]{:S(2)}) collective-permute-start(f32[8,128]{1,0:T(8,128)S(1)} %pair.1.refs_0_), channel_id=1, source_target_pairs={{0,32},{1,33},{2,34},{3,35},{4,36},{5,37},{6,38},{7,39},{8,40},{9,... | collective-permute-start | bytes 12296 | tf_op jit(solution)/shard_map/ppermute | solution.py:29
  157.2 1.6 collective-permute-done.16.refs_2_
  158.8 2.0 %collective-permute-done.15.refs_1_ = f32[8,128]{1,0:T(8,128)S(1)} collective-permute-done((f32[8,128]{1,0:T(8,128)S(1)}, f32[8,128]{1,0:T(8,128)S(1)}, u32[]{:S(2)}, u32[]{:S(2)}) %collective-permute-start.15) | collective-permute-done | bytes 4128 | tf_op jit(solution)/shard_map/ppermute | solution.py:29
  160.8 0.5 sum_y.1.refs_0_
  161.3 3.1 %text_share.1 = f32[256,1280]{1,0:T(8,128)S(1)} custom-call(f32[4]{0:T(128)S(1)} %pad_maximum_fusion.s.refs_0_, f32[8,256]{1,0:T(8,128)S(1)} %merge.1.own.refs_1_, f32[8,256]{1,0:T(8,128)S(1)} %collective-permute-done.11.m2.refs_2_, f32[8,256]{1,0:T(8,128)S(1)} %collective-permute-done.12.p2.refs_3_, f32[8,256]{1,0:T(8,128)S(1)} %collective-permute-done.13.refs_4_, ...), custom_call_target="tpu_custom_call" | custom-call | flops 4255000064 | bytes 1 | tf_op jit(solution)/shard_map/text_share/pallas_call | solution.py:37
  164.8 4.0 %collective-permute-start.18 = (f32[8,128]{1,0:T(8,128)S(1)}, f32[8,128]{1,0:T(8,128)S(1)}, u32[]{:S(2)}, u32[]{:S(2)}) collective-permute-start(f32[8,128]{1,0:T(8,128)S(1)} %sum_y.1.refs_0_), channel_id=1, source_target_pairs={{0,64},{1,65},{2,66},{3,67},{4,68},{5,69},{6,70},{7,71},{8,72},{9,... | collective-permute-start | bytes 12296 | tf_op jit(solution)/shard_map/ppermute | solution.py:29
  168.8 0.7 collective-permute-done.20.refs_3_
  169.5 0.4 collective-permute-done.19.refs_2_
  169.9 0.5 collective-permute-done.18.refs_1_
  170.4 0.5 sum_x.1.refs_0_
  171.1 4.0 %image_grads.1 = f32[256,1280]{1,0:T(8,128)} custom-call(f32[4]{0:T(128)S(1)} %pad_maximum_fusion.s.refs_0_, f32[8,256]{1,0:T(8,128)S(1)} %merge.1.own.refs_1_, f32[8,256]{1,0:T(8,128)S(1)} %collective-permute-done.11.m2.refs_2_, f32[8,256]{1,0:T(8,128)S(1)} %collective-permute-done.12.p2.refs_3_, f32[8,256]{1,0:T(8,128)S(1)} %collective-permute-done.13.refs_4_, ...), custom_call_target="tpu_custom_call" | custom-call | flops 4485000192 | bytes 1 | tf_op jit(solution)/shard_map/image_grads/pallas_call | solution.py:37
  175.1 0.5 collective-permute-done.22.refs_1_
  175.5 0.5 sum_z.1.a
  176.2 4.0 %text_grads.1 = f32[256,1280]{1,0:T(8,128)} custom-call(f32[4]{0:T(128)S(1)} %pad_maximum_fusion.s.refs_0_, f32[8,256]{1,0:T(8,128)S(1)} %merge.1.own.refs_1_, f32[8,256]{1,0:T(8,128)S(1)} %collective-permute-done.11.m2.refs_2_, f32[8,256]{1,0:T(8,128)S(1)} %collective-permute-done.12.p2.refs_3_, f32[8,256]{1,0:T(8,128)S(1)} %collective-permute-done.13.refs_4_, ...), custom_call_target="tpu_custom_call" | custom-call | flops 4485000192 | bytes 1 | tf_op jit(solution)/shard_map/text_grads/pallas_call | solution.py:37
  180.2 3.5 %collective-permute-done.24.b = f32[8,128]{1,0:T(8,128)S(1)} collective-permute-done((f32[8,128]{1,0:T(8,128)S(1)}, f32[8,128]{1,0:T(8,128)S(1)}, u32[]{:S(2)}, u32[]{:S(2)}) %collective-permute-start.24) | collective-permute-done | bytes 4128 | tf_op jit(solution)/shard_map/ppermute | solution.py:29
  183.7 1.1 last.1
  (27 shorter events, 0.8 us)
Async XLA Ops:
  0.6 7.1 %collective-permute-start = (f32[256,1280]{1,0:T(8,128)}, f32[256,1280]{1,0:T(8,128)}, u32[]{:S(2)}, u32[]{:S(2)}) collective-permute-start(f32[256,1280]{1,0:T(8,128)} %b0.6), channel_id=1, source_target_pairs={{0,1},{1,0},{2,3},{3,2},{4,5},{5,4},{6,7},{7,6},{8,9},{9,8},{10,11... | collective-permute-start | bytes 3932168 | tf_op jit(solution)/shard_map/ppermute | solution.py:29
  0.7 11.2 %collective-permute-start.1 = (f32[256,1280]{1,0:T(8,128)}, f32[256,1280]{1,0:T(8,128)}, u32[]{:S(2)}, u32[]{:S(2)}) collective-permute-start(f32[256,1280]{1,0:T(8,128)} %b0.7), channel_id=1, source_target_pairs={{0,1},{1,0},{2,3},{3,2},{4,5},{5,4},{6,7},{7,6},{8,9},{9,8},{10,11... | collective-permute-start | bytes 3932168 | tf_op jit(solution)/shard_map/ppermute | solution.py:29
  1.2 35.2 %collective-permute-start.4 = (f32[256,1280]{1,0:T(8,128)}, f32[256,1280]{1,0:T(8,128)S(1)}, u32[]{:S(2)}, u32[]{:S(2)}) collective-permute-start(f32[256,1280]{1,0:T(8,128)} %b0.6), channel_id=1, source_target_pairs={{0,254},{1,255},{2,0},{3,1},{4,2},{5,3},{6,4},{7,5},{8,6},{9,7},{1... | collective-permute-start | bytes 3932168 | tf_op jit(solution)/shard_map/ppermute | solution.py:24
  7.0 34.1 %collective-permute-start.3 = (f32[256,1280]{1,0:T(8,128)}, f32[256,1280]{1,0:T(8,128)}, u32[]{:S(2)}, u32[]{:S(2)}) collective-permute-start(f32[256,1280]{1,0:T(8,128)} %b0.6), channel_id=1, source_target_pairs={{0,2},{1,3},{2,4},{3,5},{4,6},{5,7},{6,8},{7,9},{8,10},{9,11},{10,... | collective-permute-start | bytes 3932168 | tf_op jit(solution)/shard_map/ppermute | solution.py:24
  7.0 62.1 %collective-permute-start.2 = (f32[256,1280]{1,0:T(8,128)}, f32[256,1280]{1,0:T(8,128)S(1)}, u32[]{:S(2)}, u32[]{:S(2)}) collective-permute-start(f32[256,1280]{1,0:T(8,128)} %b0.7), channel_id=1, source_target_pairs={{0,2},{1,3},{2,4},{3,5},{4,6},{5,7},{6,8},{7,9},{8,10},{9,11},{10,... | collective-permute-start | bytes 3932168 | tf_op jit(solution)/shard_map/ppermute | solution.py:24
  7.7 61.3 %collective-permute-start.7 = (f32[256,1280]{1,0:T(8,128)}, f32[256,1280]{1,0:T(8,128)S(1)}, u32[]{:S(2)}, u32[]{:S(2)}) collective-permute-start(f32[256,1280]{1,0:T(8,128)} %b0.7), channel_id=1, source_target_pairs={{0,254},{1,255},{2,0},{3,1},{4,2},{5,3},{6,4},{7,5},{8,6},{9,7},{1... | collective-permute-start | bytes 3932168 | tf_op jit(solution)/shard_map/ppermute | solution.py:24
  11.9 1.3 copy-start
  13.2 1.3 copy-start.1
  14.5 3.7 %copy-start.2 = (f32[256,1280]{1,0:T(8,128)S(1)}, f32[256,1280]{1,0:T(8,128)}, u32[]{:S(2)}) copy-start(f32[256,1280]{1,0:T(8,128)} %b0.7) | copy-start | bytes 3932164
  41.1 50.6 %collective-permute-start.8 = (f32[256,1280]{1,0:T(8,128)}, f32[256,1280]{1,0:T(8,128)S(1)}, u32[]{:S(2)}, u32[]{:S(2)}) collective-permute-start(f32[256,1280]{1,0:T(8,128)} %collective-permute-done.3.bp), channel_id=1, source_target_pairs={{1,3},{3,5},{5,7},{7,9},{9,11},{11,13},{13,15},{15,17},{17,19},{19... | collective-permute-start | bytes 3932168 | tf_op jit(solution)/shard_map/ppermute | solution.py:24
  41.8 49.9 %collective-permute-start.6 = (f32[256,1280]{1,0:T(8,128)S(1)}, f32[256,1280]{1,0:T(8,128)S(1)}, u32[]{:S(2)}, u32[]{:S(2)}) collective-permute-start(f32[256,1280]{1,0:T(8,128)S(1)} %collective-permute-done.4.bm), channel_id=1, source_target_pairs={{0,254},{1,255},{2,0},{3,1},{4,2},{5,3},{6,4},{7,5},{8,6},{9,7},{1... | collective-permute-start | bytes 3932168 | tf_op jit(solution)/shard_map/ppermute | solution.py:24
  69.0 33.8 %collective-permute-start.5 = (f32[256,1280]{1,0:T(8,128)S(1)}, f32[256,1280]{1,0:T(8,128)S(1)}, u32[]{:S(2)}, u32[]{:S(2)}) collective-permute-start(f32[256,1280]{1,0:T(8,128)S(1)} %collective-permute-done.2.bp), channel_id=1, source_target_pairs={{0,2},{1,3},{2,4},{3,5},{4,6},{5,7},{6,8},{7,9},{8,10},{9,11},{10,... | collective-permute-start | bytes 3932168 | tf_op jit(solution)/shard_map/ppermute | solution.py:24
  69.1 36.7 %collective-permute-start.9 = (f32[256,1280]{1,0:T(8,128)S(1)}, f32[256,1280]{1,0:T(8,128)S(1)}, u32[]{:S(2)}, u32[]{:S(2)}) collective-permute-start(f32[256,1280]{1,0:T(8,128)S(1)} %collective-permute-done.7.bm), channel_id=1, source_target_pairs={{0,254},{2,0},{4,2},{6,4},{8,6},{10,8},{12,10},{14,12},{16,14},{18... | collective-permute-start | bytes 3932168 | tf_op jit(solution)/shard_map/ppermute | solution.py:24
  109.3 5.0 %collective-permute-start.10 = (f32[16,256]{1,0:T(8,128)S(1)}, f32[16,256]{1,0:T(8,128)S(1)}, u32[]{:S(2)}, u32[]{:S(2)}) collective-permute-start(f32[16,256]{1,0:T(8,128)S(1)} %get-tuple-element.82.mine), channel_id=1, source_target_pairs={{0,1},{1,0},{2,3},{3,2},{4,5},{5,4},{6,7},{7,6},{8,9},{9,8},{10,11... | collective-permute-start | bytes 49160 | tf_op jit(solution)/shard_map/ppermute | solution.py:29
  115.0 15.3 %collective-permute-start.14 = (f32[8,256]{1,0:T(8,128)S(1)}, f32[8,256]{1,0:T(8,128)S(1)}, u32[]{:S(2)}, u32[]{:S(2)}) collective-permute-start(f32[8,256]{1,0:T(8,128)S(1)} %merge.1.own.refs_1_), channel_id=1, source_target_pairs={{0,252},{1,253},{2,254},{3,255},{4,0},{5,1},{6,2},{7,3},{8,4},{9,5... | collective-permute-start | bytes 24584 | tf_op jit(solution)/shard_map/ppermute | solution.py:24
  115.0 15.3 %collective-permute-start.13 = (f32[8,256]{1,0:T(8,128)S(1)}, f32[8,256]{1,0:T(8,128)S(1)}, u32[]{:S(2)}, u32[]{:S(2)}) collective-permute-start(f32[8,256]{1,0:T(8,128)S(1)} %merge.1.own.refs_1_), channel_id=1, source_target_pairs={{0,4},{1,5},{2,6},{3,7},{4,8},{5,9},{6,10},{7,11},{8,12},{9,13},{1... | collective-permute-start | bytes 24584 | tf_op jit(solution)/shard_map/ppermute | solution.py:24
  118.0 12.4 %collective-permute-start.12 = (f32[8,256]{1,0:T(8,128)S(1)}, f32[8,256]{1,0:T(8,128)S(1)}, u32[]{:S(2)}, u32[]{:S(2)}) collective-permute-start(f32[8,256]{1,0:T(8,128)S(1)} %merge.1.own.refs_1_), channel_id=1, source_target_pairs={{0,254},{1,255},{2,0},{3,1},{4,2},{5,3},{6,4},{7,5},{8,6},{9,7},{1... | collective-permute-start | bytes 24584 | tf_op jit(solution)/shard_map/ppermute | solution.py:24
  120.9 15.2 %collective-permute-start.11 = (f32[8,256]{1,0:T(8,128)S(1)}, f32[8,256]{1,0:T(8,128)S(1)}, u32[]{:S(2)}, u32[]{:S(2)}) collective-permute-start(f32[8,256]{1,0:T(8,128)S(1)} %merge.1.own.refs_1_), channel_id=1, source_target_pairs={{0,2},{1,3},{2,4},{3,5},{4,6},{5,7},{6,8},{7,9},{8,10},{9,11},{10,... | collective-permute-start | bytes 24584 | tf_op jit(solution)/shard_map/ppermute | solution.py:24
  139.2 31.9 %collective-permute-start.21 = (f32[256,1280]{1,0:T(8,128)S(1)}, f32[256,1280]{1,0:T(8,128)S(1)}, u32[]{:S(2)}, u32[]{:S(2)}) collective-permute-start(f32[256,1280]{1,0:T(8,128)S(1)} %image_share.1), channel_id=1, source_target_pairs={{0,1},{1,0},{2,3},{3,2},{4,5},{5,4},{6,7},{7,6},{8,9},{9,8},{10,11... | collective-permute-start | bytes 3932168 | tf_op jit(solution)/shard_map/ppermute | solution.py:29
  139.9 17.3 %collective-permute-start.17 = (f32[8,128]{1,0:T(8,128)S(1)}, f32[8,128]{1,0:T(8,128)S(1)}, u32[]{:S(2)}, u32[]{:S(2)}) collective-permute-start(f32[8,128]{1,0:T(8,128)S(1)} %pair.1.refs_0_), channel_id=1, source_target_pairs={{0,48},{1,49},{2,50},{3,51},{4,52},{5,53},{6,54},{7,55},{8,56},{9,... | collective-permute-start | bytes 12296 | tf_op jit(solution)/shard_map/ppermute | solution.py:29
  141.5 17.2 %collective-permute-start.16 = (f32[8,128]{1,0:T(8,128)S(1)}, f32[8,128]{1,0:T(8,128)S(1)}, u32[]{:S(2)}, u32[]{:S(2)}) collective-permute-start(f32[8,128]{1,0:T(8,128)S(1)} %pair.1.refs_0_), channel_id=1, source_target_pairs={{0,32},{1,33},{2,34},{3,35},{4,36},{5,37},{6,38},{7,39},{8,40},{9,... | collective-permute-start | bytes 12296 | tf_op jit(solution)/shard_map/ppermute | solution.py:29
  157.2 3.6 %collective-permute-start.15 = (f32[8,128]{1,0:T(8,128)S(1)}, f32[8,128]{1,0:T(8,128)S(1)}, u32[]{:S(2)}, u32[]{:S(2)}) collective-permute-start(f32[8,128]{1,0:T(8,128)S(1)} %pair.1.refs_0_), channel_id=1, source_target_pairs={{0,16},{1,17},{2,18},{3,19},{4,20},{5,21},{6,22},{7,23},{8,24},{9,... | collective-permute-start | bytes 12296 | tf_op jit(solution)/shard_map/ppermute | solution.py:29
  164.5 11.7 %collective-permute-start.23 = (f32[256,1280]{1,0:T(8,128)S(1)}, f32[256,1280]{1,0:T(8,128)S(1)}, u32[]{:S(2)}, u32[]{:S(2)}) collective-permute-start(f32[256,1280]{1,0:T(8,128)S(1)} %text_share.1), channel_id=1, source_target_pairs={{0,1},{1,0},{2,3},{3,2},{4,5},{5,4},{6,7},{7,6},{8,9},{9,8},{10,11... | collective-permute-start | bytes 3932168 | tf_op jit(solution)/shard_map/ppermute | solution.py:29
  164.6 4.9 %collective-permute-start.20 = (f32[8,128]{1,0:T(8,128)S(1)}, f32[8,128]{1,0:T(8,128)S(1)}, u32[]{:S(2)}, u32[]{:S(2)}) collective-permute-start(f32[8,128]{1,0:T(8,128)S(1)} %sum_y.1.refs_0_), channel_id=1, source_target_pairs={{0,192},{1,193},{2,194},{3,195},{4,196},{5,197},{6,198},{7,199},{8... | collective-permute-start | bytes 12296 | tf_op jit(solution)/shard_map/ppermute | solution.py:29
  164.7 5.2 %collective-permute-start.19 = (f32[8,128]{1,0:T(8,128)S(1)}, f32[8,128]{1,0:T(8,128)S(1)}, u32[]{:S(2)}, u32[]{:S(2)}) collective-permute-start(f32[8,128]{1,0:T(8,128)S(1)} %sum_y.1.refs_0_), channel_id=1, source_target_pairs={{0,128},{1,129},{2,130},{3,131},{4,132},{5,133},{6,134},{7,135},{8... | collective-permute-start | bytes 12296 | tf_op jit(solution)/shard_map/ppermute | solution.py:29
  164.8 5.6 %collective-permute-start.18 = (f32[8,128]{1,0:T(8,128)S(1)}, f32[8,128]{1,0:T(8,128)S(1)}, u32[]{:S(2)}, u32[]{:S(2)}) collective-permute-start(f32[8,128]{1,0:T(8,128)S(1)} %sum_y.1.refs_0_), channel_id=1, source_target_pairs={{0,64},{1,65},{2,66},{3,67},{4,68},{5,69},{6,70},{7,71},{8,72},{9,... | collective-permute-start | bytes 12296 | tf_op jit(solution)/shard_map/ppermute | solution.py:29
  171.0 4.6 %collective-permute-start.22 = (f32[8,128]{1,0:T(8,128)S(1)}, f32[8,128]{1,0:T(8,128)S(1)}, u32[]{:S(2)}, u32[]{:S(2)}) collective-permute-start(f32[8,128]{1,0:T(8,128)S(1)} %sum_x.1.refs_0_), channel_id=1, source_target_pairs={{0,4},{1,5},{2,6},{3,7},{4,0},{5,1},{6,2},{7,3},{8,12},{9,13},{10,... | collective-permute-start | bytes 12296 | tf_op jit(solution)/shard_map/ppermute | solution.py:29
  176.1 7.6 %collective-permute-start.24 = (f32[8,128]{1,0:T(8,128)S(1)}, f32[8,128]{1,0:T(8,128)S(1)}, u32[]{:S(2)}, u32[]{:S(2)}) collective-permute-start(f32[8,128]{1,0:T(8,128)S(1)} %sum_z.1.a), channel_id=1, source_target_pairs={{0,8},{1,9},{2,10},{3,11},{4,12},{5,13},{6,14},{7,15},{8,0},{9,1},... | collective-permute-start | bytes 12296 | tf_op jit(solution)/shard_map/ppermute | solution.py:29

commit v3 on v2

--- a/solution.py
+++ b/solution.py
@@ -21,6 +21,12 @@
 def shift(value, steps, cores=BOTH):
     count = lax.axis_size("dp")
     pairs = [(s, (s + steps) % count) for s in range(count) if s % 2 in cores]
+    return lax.ppermute(value, "dp", pairs)
+
+
+def along(value, sign):
+    count = lax.axis_size("dp")
+    pairs = [(s, (s + sign * (2 + 2 * (s % 2))) % count) for s in range(count)]
     return lax.ppermute(value, "dp", pairs)
 
 
@@ -125,7 +131,7 @@
     out[...] = s[0] * scores(take((h, m, l)), take((bh, bm, bl)))
 
 
-def near_kernel(s, h, m, l, b0, bp, bm, lp, lm, blocks_h, blocks_l, *parts):
+def near_kernel(s, h, m, l, b0, bm, bp, lp, lm, blocks_h, blocks_l, *parts):
     n = b0.shape[0]
     r = pl.ds(n, n)
     blocks_h[r], blocks_l[r] = two(b0[...])
@@ -199,17 +205,19 @@
     out[6:8, :] = jnp.zeros((2, n), F32)
 
 
-def mate_kernel(s, own, m2, p2, out):
-    out[...] = jnp.zeros_like(out)
-    out[0:2, :] = own[4:6, :128] + jnp.where(s[2] == 0.0, p2[4:6, :128], m2[4:6, :128])
-
-
-def sum_kernel(s, *refs):
-    *terms, out = refs
-    values = [t[...] for t in terms]
-    while len(values) > 1:
-        values = [a + b for a, b in zip(values[::2], values[1::2])]
-    out[...] = values[0]
+def sort_kernel(s, own, v, vs, u, us, out, parts):
+    first = s[1] == 0.0
+    for k, (a, b) in enumerate(((u, us), (v, vs))):
+        out[2 * k : 2 * k + 2, :] = jnp.where(first, a[0:2, :], b[2:4, :])
+        out[2 * k + 4 : 2 * k + 6, :] = jnp.where(first, b[2:4, :], a[0:2, :])
+    ahead = jnp.where(first, v[4:6, :128], vs[4:6, :128])
+    behind = jnp.where(first, u[4:6, :128], us[4:6, :128])
+    parts[...] = jnp.zeros_like(parts)
+    parts[0:2, :] = own[4:6, :128] + jnp.where(s[2] == 0.0, ahead, behind)
+
+
+def sum_kernel(s, a, b, out):
+    out[...] = a[...] + b[...]
 
 
 def last_kernel(s, a, b, loss, scale_grad):
@@ -228,19 +236,19 @@
     return jnp.where(i == j, w - 2.0, w)
 
 
-def put_weights(text, sib, s, own, m2, p2, m4, p4, l0, lp, lm, lf, wh, wl):
+def put_weights(text, sib, s, own, lses, l0, lp, lm, lf, wh, wl):
     n = l0.shape[1]
     first = s[1] == 0.0
     rows = pl.ds(n if sib else 0, n)
     k = (2 if sib else 0) + (1 if text else 0)
     side = column(own[k : k + 1, :])
-    other = slice(0, 1) if text else slice(1, 2)
-    ahead, behind = p4[other, :], m4[other, :]
+    k = 0 if text else 1
+    m2, p2, behind, ahead = (lses[j + k : j + k + 1, :] for j in (0, 2, 4, 6))
     if sib:
         far = jnp.where(first, ahead, behind)
     else:
         far = behind if text else ahead
-    near = [(l0, own[other, :]), (lp, m2[other, :]), (lm, p2[other, :])]
+    near = [(l0, own[k : k + 1, :]), (lp, m2), (lm, p2)]
     pieces = near + [(lf, far)] if sib else [(lf, far)] + near
     for k, (v, m) in enumerate(pieces):
         w = weigh(v[rows, :], side, m)
@@ -304,13 +312,13 @@
     t_pp, t_mm = shift(t_p, 2, (1,)), shift(t_m, -2)
     five = [((5 * n, depth), BF16)] * 2
     near_outs = [both] * 2 + five
-    args = s, *x, text, t_p, t_m
+    args = s, *x, text, t_m, t_p
     lp, lm, *t_parts = call(near_kernel, "text_near", 4.8, near_outs, args, split)
     args = s, l0, lp, lm
     top, mean, diag = call(near_stats_kernel, "text_stats", 1.8, [wide] * 2 + [line], args)
     i_p, i_m = after(i_p, top), after(i_m, top)
     i_pp, i_mm = shift(i_p, 2), shift(i_m, -2, (0,))
-    args = s, *y, image, i_p, i_m
+    args = s, *y, image, i_m, i_p
     vp, vm, *i_parts = call(near_kernel, "image_near", 4.8, near_outs, args, split)
     args = s, v0, vp, vm
     i_top, i_mean, _ = call(near_stats_kernel, "image_stats", 1.8, [wide] * 2 + [line], args)
@@ -324,40 +332,37 @@
 
     got = swap(mine)
     (own,) = call(merge_kernel, "merge", 0.6, [((8, n), F32)], (s, mine, got))
-    m2, p2 = shift(own, 2), shift(own, -2)
-    m4, p4 = shift(own, 4), shift(own, -4)
+    u, v = along(own, 1), along(own, -1)
+    args = s, own, v, swap(v), u, swap(u)
     terms = [((8, 128), F32)]
-    (parts,) = call(mate_kernel, "pair", 0.5, terms, (s, own, m2, after(p2, m4, p4)))
-
-    lses = m2, p2, m4, p4
+    lses, parts = call(sort_kernel, "sort", 0.5, [((8, n), F32)] + terms, args)
+
+    def add(parts, bit, *done):
+        args = s, after(parts, *done), swap(parts, bit)
+        return call(sum_kernel, "sum", 0.5, terms, args)[0]
+
     image_args = l0, lp, lm, lf, *t_parts
     text_args = v0, vp, vm, vf, *i_parts
     weights = [((n, 4 * n), BF16)] * 2
     final = weights + [block, pltpu.SemaphoreType.DMA((depth // TILE,))]
     kernel = functools.partial(share_kernel, False)
-    args = s, own, *lses, *image_args
-    (share,) = call(kernel, "image_share", 3.7, [block], args, weights)
-    image_share = swap(share)
-    y_parts = swap(parts, 16), swap(parts, 32), swap(parts, 48)
-    args = s, after(parts, share), *y_parts
-    (parts,) = call(sum_kernel, "sum_y", 0.5, terms, args)
-    x_parts = swap(parts, 64), swap(parts, 128), swap(parts, 192)
+    (share,) = call(kernel, "image_share", 3.1, [block], (s, own, lses, *image_args), weights)
+    parts = add(parts, 16, share)
+    image_share = swap(after(share, parts))
     kernel = functools.partial(share_kernel, True)
-    args = s, after(own, parts), *lses, *text_args
-    (share,) = call(kernel, "text_share", 3.7, [block], args, weights)
-    text_share = swap(share)
-    args = s, after(parts, share), *x_parts
-    (parts,) = call(sum_kernel, "sum_x", 0.5, terms, args)
-    z_part = swap(parts, 4)
+    args = s, after(own, parts), lses, *text_args
+    (share,) = call(kernel, "text_share", 3.1, [block], args, weights)
+    parts = add(parts, 32, share)
+    text_share = swap(after(share, parts))
+    parts = add(parts, 64)
     kernel = functools.partial(grads_kernel, False)
-    args = s, after(own, parts), *lses, *image_args, image_share
+    args = s, after(own, parts), lses, *image_args, image_share
     (image_grad,) = call(kernel, "image_grads", 3.9, [block], args, final, ANY)
-    args = s, after(parts, image_grad), z_part
-    (parts,) = call(sum_kernel, "sum_z", 0.5, terms, args)
+    parts = add(add(parts, 128, image_grad), 4)
+    kernel = functools.partial(grads_kernel, True)
+    args = s, after(own, parts), lses, *text_args, text_share
+    (text_grad,) = call(kernel, "text_grads", 3.9, [block], args, final, ANY)
     z_part = swap(parts, 8)
-    kernel = functools.partial(grads_kernel, True)
-    args = s, after(own, parts), *lses, *text_args, text_share
-    (text_grad,) = call(kernel, "text_grads", 3.9, [block], args, final, ANY)
     args = s, after(parts, text_grad), z_part
     loss, scale_grad = call(last_kernel, "last", 0.5, [((1, 1), F32)] * 2, args)
     return (loss.reshape(()), image_grad, text_grad, scale_grad.reshape(()))

time: 188 us -> 175 us (0.931)
  the two profiles are of different devices: /device:TPU:8 before, /device:TPU:2 now
where the time goes in v3:
time: 175 us; the launch traced here: 172 us
  waiting for transfers between devices  60.4 us (35%)
  starting transfers between devices  59 us (34%)
  Pallas kernels  48.3 us (28%)
  local copies, waits for them, and re-layouts  2.64 us (2%)
    pallas_call x20, Pallas kernels, call(): pl.pallas_call(kernel, name=name, out_shape=[jax.ShapeDtypeStruct(s, d) f...  48.3 us
    ppermute x8, waiting for transfers between devices, shift(): return lax.ppermute(value, 'dp', pairs)  48 us
    ppermute x8, starting transfers between devices, shift(): return lax.ppermute(value, 'dp', pairs)  30.1 us
    ppermute x13, starting transfers between devices, swap(): return lax.ppermute(value, 'dp', [(s, s ^ bit) for s in range(count)])  22.4 us
    ppermute x13, waiting for transfers between devices, swap(): return lax.ppermute(value, 'dp', [(s, s ^ bit) for s in range(count)])  10.8 us
    ppermute x2, starting transfers between devices, along(): return lax.ppermute(value, 'dp', pairs)  6.59 us
  transfers between devices with their start and end apart: 23, of which 14 were waited for; matrix products, arithmetic and copies ran while one was open for 0% of the time, Pallas kernels for 24%

profile of v3, /device:TPU:2, one launch (start us, length us, event | category | flops | bytes accessed | tf_op | source)
XLA Modules:
  0.0 172.2 jit_solution(8055203439373570440)
XLA Ops:
  0.7 0.5 collective-permute-start.1
  1.2 1.9 %collective-permute-start.4 = (f32[256,1280]{1,0:T(8,128)}, f32[256,1280]{1,0:T(8,128)S(1)}, u32[]{:S(2)}, u32[]{:S(2)}) collective-permute-start(f32[256,1280]{1,0:T(8,128)} %b0.6), channel_id=1, source_target_pairs={{0,2},{1,3},{2,4},{3,5},{4,6},{5,7},{6,8},{7,9},{8,10},{9,11},{10,... | collective-permute-start | bytes 3932168 | tf_op jit(solution)/shard_map/ppermute | solution.py:24
  3.1 6.4 %collective-permute-start.3 = (f32[256,1280]{1,0:T(8,128)}, f32[256,1280]{1,0:T(8,128)}, u32[]{:S(2)}, u32[]{:S(2)}) collective-permute-start(f32[256,1280]{1,0:T(8,128)} %b0.6), channel_id=1, source_target_pairs={{0,254},{1,255},{2,0},{3,1},{4,2},{5,3},{6,4},{7,5},{8,6},{9,7},{1... | collective-permute-start | bytes 3932168 | tf_op jit(solution)/shard_map/ppermute | solution.py:24
  10.2 6.3 %collective-permute-start.7 = (f32[256,1280]{1,0:T(8,128)}, f32[256,1280]{1,0:T(8,128)S(1)}, u32[]{:S(2)}, u32[]{:S(2)}) collective-permute-start(f32[256,1280]{1,0:T(8,128)} %b0.7), channel_id=1, source_target_pairs={{0,254},{1,255},{2,0},{3,1},{4,2},{5,3},{6,4},{7,5},{8,6},{9,7},{1... | collective-permute-start | bytes 3932168 | tf_op jit(solution)/shard_map/ppermute | solution.py:24
  16.5 1.3 copy-done
  17.8 1.3 copy-done.1
  19.2 3.7 %text_own.1 = (bf16[512,1280]{1,0:T(8,128)(2,1)S(1)}, bf16[512,1280]{1,0:T(8,128)(2,1)S(1)}, bf16[512,1280]{1,0:T(8,128)(2,1)S(1)}, f32[512,256]{1,0:T(8,128)S(1)}) custom-call(f32[4]{0:T(128)S(1)} %pad_maximum_fusion.s.refs_0_, f32[256,1280]{1,0:T(8,128)S(1)} %copy-done.1, f32[256,1280]{1,0:T(8,128)} %collective-permute-done.1.a1, f32[256,1280]{1,0:T(8,128)S(1)} %copy-done), custom_call_target="tpu_custom_call" | custom-call | flops 4255000064 | bytes 1 | tf_op jit(solution)/shard_map/text_own/pallas_call | solution.py:43
  22.9 3.6 %image_own.1 = (bf16[512,1280]{1,0:T(8,128)(2,1)S(1)}, bf16[512,1280]{1,0:T(8,128)(2,1)S(1)}, bf16[512,1280]{1,0:T(8,128)(2,1)S(1)}, f32[512,256]{1,0:T(8,128)S(1)}) custom-call(f32[4]{0:T(128)S(1)} %pad_maximum_fusion.s.refs_0_, f32[256,1280]{1,0:T(8,128)S(1)} %copy-done, f32[256,1280]{1,0:T(8,128)} %collective-permute-done.a1, f32[256,1280]{1,0:T(8,128)S(1)} %copy-done.2), custom_call_target="tpu_custom_call" | custom-call | flops 4255000064 | bytes 1 | tf_op jit(solution)/shard_map/image_own/pallas_call | solution.py:43
  26.5 12.8 %collective-permute-done.4.bp = f32[256,1280]{1,0:T(8,128)S(1)} collective-permute-done((f32[256,1280]{1,0:T(8,128)}, f32[256,1280]{1,0:T(8,128)S(1)}, u32[]{:S(2)}, u32[]{:S(2)}) %collective-permute-start.4) | collective-permute-done | bytes 1310752 | tf_op jit(solution)/shard_map/ppermute | solution.py:24
  39.3 6.4 %collective-permute-start.6 = (f32[256,1280]{1,0:T(8,128)}, f32[256,1280]{1,0:T(8,128)S(1)}, u32[]{:S(2)}, u32[]{:S(2)}) collective-permute-start(f32[256,1280]{1,0:T(8,128)} %collective-permute-done.3.bm), channel_id=1, source_target_pairs={{0,254},{1,255},{2,0},{3,1},{4,2},{5,3},{6,4},{7,5},{8,6},{9,7},{1... | collective-permute-start | bytes 3932168 | tf_op jit(solution)/shard_map/ppermute | solution.py:24
  45.7 1.0 collective-permute-start.8
  46.7 6.0 %text_near.1 = (f32[512,256]{1,0:T(8,128)S(1)}, f32[512,256]{1,0:T(8,128)S(1)}, bf16[1280,1280]{1,0:T(8,128)(2,1)S(1)}, bf16[1280,1280]{1,0:T(8,128)(2,1)S(1)}) custom-call(f32[4]{0:T(128)S(1)} %pad_maximum_fusion.s.refs_0_, bf16[512,1280]{1,0:T(8,128)(2,1)S(1)} %get-tuple-element.60.h.xh, bf16[512,1280]{1,0:T(8,128)(2,1)S(1)} %get-tuple-element.61.m.xm, ...), custom_call_target="tpu_custom_call" | custom-call | flops 5520000000 | bytes 1 | tf_op jit(solution)/shard_map/text_near/pallas_call | solution.py:43
  52.7 1.3 text_stats.1
  54.1 13.3 %collective-permute-done.2.bp = f32[256,1280]{1,0:T(8,128)S(1)} collective-permute-done((f32[256,1280]{1,0:T(8,128)}, f32[256,1280]{1,0:T(8,128)S(1)}, u32[]{:S(2)}, u32[]{:S(2)}) %collective-permute-start.2) | collective-permute-done | bytes 1310752 | tf_op jit(solution)/shard_map/ppermute | solution.py:24
  67.4 8.2 %collective-permute-start.9 = (f32[256,1280]{1,0:T(8,128)S(1)}, f32[256,1280]{1,0:T(8,128)S(1)}, u32[]{:S(2)}, u32[]{:S(2)}) collective-permute-start(f32[256,1280]{1,0:T(8,128)S(1)} %collective-permute-done.7.bm), channel_id=1, source_target_pairs={{0,254},{2,0},{4,2},{6,4},{8,6},{10,8},{12,10},{14,12},{16,14},{18... | collective-permute-start | bytes 3932168 | tf_op jit(solution)/shard_map/ppermute | solution.py:24
  75.6 5.2 %image_near.1 = (f32[512,256]{1,0:T(8,128)S(1)}, f32[512,256]{1,0:T(8,128)S(1)}, bf16[1280,1280]{1,0:T(8,128)(2,1)S(1)}, bf16[1280,1280]{1,0:T(8,128)(2,1)S(1)}) custom-call(f32[4]{0:T(128)S(1)} %pad_maximum_fusion.s.refs_0_, bf16[512,1280]{1,0:T(8,128)(2,1)S(1)} %get-tuple-element.57.h.yh, bf16[512,1280]{1,0:T(8,128)(2,1)S(1)} %get-tuple-element.58.m.ym, ...), custom_call_target="tpu_custom_call" | custom-call | flops 5520000000 | bytes 1 | tf_op jit(solution)/shard_map/image_near/pallas_call | solution.py:43
  80.8 1.9 %image_stats.1 = (f32[512,128]{1,0:T(8,128)S(1)}, f32[512,128]{1,0:T(8,128)S(1)}, f32[1,256]{1,0:T(1,128)}) custom-call(f32[4]{0:T(128)S(1)} %pad_maximum_fusion.s.refs_0_, f32[512,256]{1,0:T(8,128)S(1)} %get-tuple-element.63.l0.refs_3_, f32[512,256]{1,0:T(8,128)S(1)} %get-tuple-element.71.lp.refs_4_, f32[512,256]{1,0:T(8,128)S(1)} %get-tuple-element.72.lm.refs_5_), custom_call_target="tpu_custom_call" | custom-call | flops 2070000000 | bytes 1 | tf_op jit(solution)/shard_map/image_stats/pallas_call | solution.py:43
  82.7 11.6 %collective-permute-done.6.a = f32[256,1280]{1,0:T(8,128)S(1)} collective-permute-done((f32[256,1280]{1,0:T(8,128)}, f32[256,1280]{1,0:T(8,128)S(1)}, u32[]{:S(2)}, u32[]{:S(2)}) %collective-permute-start.6) | collective-permute-done | bytes 1310752 | tf_op jit(solution)/shard_map/ppermute | solution.py:24
  94.3 3.6 %text_far.1 = (f32[512,256]{1,0:T(8,128)S(1)}, f32[4,256]{1,0:T(4,128)S(1)}, bf16[1280,1280]{1,0:T(8,128)(2,1)S(1)}, bf16[1280,1280]{1,0:T(8,128)(2,1)S(1)}) custom-call(f32[4]{0:T(128)S(1)} %pad_maximum_fusion.s.refs_0_, bf16[512,1280]{1,0:T(8,128)(2,1)S(1)} %get-tuple-element.60.h.xh, ...), custom_call_target="tpu_custom_call", output_to_operand_aliasing={{2}: (8, {}), {3}: (9, {})} | custom-call | flops 4600000000 | bytes 1 | tf_op jit(solution)/shard_map/text_far/pallas_call | solution.py:43
  97.9 5.4 %collective-permute-done.5.a = f32[256,1280]{1,0:T(8,128)S(1)} collective-permute-done((f32[256,1280]{1,0:T(8,128)S(1)}, f32[256,1280]{1,0:T(8,128)S(1)}, u32[]{:S(2)}, u32[]{:S(2)}) %collective-permute-start.5) | collective-permute-done | bytes 1310752 | tf_op jit(solution)/shard_map/ppermute | solution.py:24
  103.3 4.9 %collective-permute-done.9.b = f32[256,1280]{1,0:T(8,128)S(1)} collective-permute-done((f32[256,1280]{1,0:T(8,128)S(1)}, f32[256,1280]{1,0:T(8,128)S(1)}, u32[]{:S(2)}, u32[]{:S(2)}) %collective-permute-start.9) | collective-permute-done | bytes 1310752 | tf_op jit(solution)/shard_map/ppermute | solution.py:24
  108.2 3.6 %image_far.1 = (f32[512,256]{1,0:T(8,128)S(1)}, f32[16,256]{1,0:T(8,128)S(1)}, bf16[1280,1280]{1,0:T(8,128)(2,1)S(1)}, bf16[1280,1280]{1,0:T(8,128)(2,1)S(1)}) custom-call(f32[4]{0:T(128)S(1)} %pad_maximum_fusion.s.refs_0_, bf16[512,1280]{1,0:T(8,128)(2,1)S(1)} %get-tuple-element.57.h.yh, ...), custom_call_target="tpu_custom_call", output_to_operand_aliasing={{2}: (8, {}), {3}: (9, {})} | custom-call | flops 4600000000 | bytes 1 | tf_op jit(solution)/shard_map/image_far/pallas_call | solution.py:43
  111.9 0.6 collective-permute-start.10
  112.5 0.8 collective-permute-done.10.got
  113.3 0.6 merge.1.own.refs_1_
  114.0 6.6 %collective-permute-start.11 = (f32[8,256]{1,0:T(8,128)S(1)}, f32[8,256]{1,0:T(8,128)S(1)}, u32[]{:S(2)}, u32[]{:S(2)}) collective-permute-start(f32[8,256]{1,0:T(8,128)S(1)} %merge.1.own.refs_1_), channel_id=1, source_target_pairs={{0,254},{1,253},{2,0},{3,255},{4,2},{5,1},{6,4},{7,3},{8,6},{9,5},... | collective-permute-start | bytes 24584 | tf_op jit(solution)/shard_map/ppermute | solution.py:30
  120.6 1.6 collective-permute-done.13.u
  122.1 0.5 collective-permute-start.12
  122.6 0.7 collective-permute-done.14.us
  123.5 0.6 sort.1
  124.0 8.7 %collective-permute-start.15 = (f32[8,128]{1,0:T(8,128)S(1)}, f32[8,128]{1,0:T(8,128)S(1)}, u32[]{:S(2)}, u32[]{:S(2)}) collective-permute-start(f32[8,128]{1,0:T(8,128)S(1)} %get-tuple-element.90.a), channel_id=1, source_target_pairs={{0,16},{1,17},{2,18},{3,19},{4,20},{5,21},{6,22},{7,23},{8,24},{9,... | collective-permute-start | bytes 12296 | tf_op jit(solution)/shard_map/ppermute | solution.py:35
  132.8 3.1 %image_share.1 = f32[256,1280]{1,0:T(8,128)S(1)} custom-call(f32[4]{0:T(128)S(1)} %pad_maximum_fusion.s.refs_0_, f32[8,256]{1,0:T(8,128)S(1)} %merge.1.own.refs_1_, f32[8,256]{1,0:T(8,128)S(1)} %get-tuple-element.87.refs_2_, f32[512,256]{1,0:T(8,128)S(1)} %get-tuple-element.55.l0.refs_3_, f32[512,256]{1,0:T(8,128)S(1)} %get-tuple-element.66.lp.refs_4_, ...), custom_call_target="tpu_custom_call" | custom-call | flops 3564999936 | bytes 1 | tf_op jit(solution)/shard_map/image_share/pallas_call | solution.py:43
  136.4 0.5 sum.5.a
  137.1 3.1 %text_share.1 = f32[256,1280]{1,0:T(8,128)S(1)} custom-call(f32[4]{0:T(128)S(1)} %pad_maximum_fusion.s.refs_0_, f32[8,256]{1,0:T(8,128)S(1)} %merge.1.own.refs_1_, f32[8,256]{1,0:T(8,128)S(1)} %get-tuple-element.87.refs_2_, f32[512,256]{1,0:T(8,128)S(1)} %get-tuple-element.63.l0.refs_3_, f32[512,256]{1,0:T(8,128)S(1)} %get-tuple-element.71.lp.refs_4_, ...), custom_call_target="tpu_custom_call" | custom-call | flops 3564999936 | bytes 1 | tf_op jit(solution)/shard_map/text_share/pallas_call | solution.py:43
  140.2 2.0 %collective-permute-done.16.b = f32[8,128]{1,0:T(8,128)S(1)} collective-permute-done((f32[8,128]{1,0:T(8,128)S(1)}, f32[8,128]{1,0:T(8,128)S(1)}, u32[]{:S(2)}, u32[]{:S(2)}) %collective-permute-start.16) | collective-permute-done | bytes 4128 | tf_op jit(solution)/shard_map/ppermute | solution.py:35
  142.2 0.5 sum.6.a
  142.9 4.1 %collective-permute-start.17 = (f32[8,128]{1,0:T(8,128)S(1)}, f32[8,128]{1,0:T(8,128)S(1)}, u32[]{:S(2)}, u32[]{:S(2)}) collective-permute-start(f32[8,128]{1,0:T(8,128)S(1)} %sum.6.a), channel_id=1, source_target_pairs={{0,64},{1,65},{2,66},{3,67},{4,68},{5,69},{6,70},{7,71},{8,72},{9,... | collective-permute-start | bytes 12296 | tf_op jit(solution)/shard_map/ppermute | solution.py:35
  146.9 1.6 collective-permute-done.17.b
  148.5 0.5 sum.7.a
  149.1 0.6 collective-permute-start.19
  149.6 4.0 %image_grads.1 = f32[256,1280]{1,0:T(8,128)} custom-call(f32[4]{0:T(128)S(1)} %pad_maximum_fusion.s.refs_0_, f32[8,256]{1,0:T(8,128)S(1)} %merge.1.own.refs_1_, f32[8,256]{1,0:T(8,128)S(1)} %get-tuple-element.87.refs_2_, f32[512,256]{1,0:T(8,128)S(1)} %get-tuple-element.55.l0.refs_3_, f32[512,256]{1,0:T(8,128)S(1)} %get-tuple-element.66.lp.refs_4_, ...), custom_call_target="tpu_custom_call" | custom-call | flops 4485000192 | bytes 1 | tf_op jit(solution)/shard_map/image_grads/pallas_call | solution.py:43
  153.6 0.6 collective-permute-done.19.b
  154.3 0.5 sum.8.a
  154.9 4.5 %collective-permute-done.20.b = f32[8,128]{1,0:T(8,128)S(1)} collective-permute-done((f32[8,128]{1,0:T(8,128)S(1)}, f32[8,128]{1,0:T(8,128)S(1)}, u32[]{:S(2)}, u32[]{:S(2)}) %collective-permute-start.20) | collective-permute-done | bytes 4128 | tf_op jit(solution)/shard_map/ppermute | solution.py:35
  159.4 0.5 sum.9.a
  160.0 6.9 %collective-permute-start.22 = (f32[8,128]{1,0:T(8,128)S(1)}, f32[8,128]{1,0:T(8,128)S(1)}, u32[]{:S(2)}, u32[]{:S(2)}) collective-permute-start(f32[8,128]{1,0:T(8,128)S(1)} %sum.9.a), channel_id=1, source_target_pairs={{0,8},{1,9},{2,10},{3,11},{4,12},{5,13},{6,14},{7,15},{8,0},{9,1},... | collective-permute-start | bytes 12296 | tf_op jit(solution)/shard_map/ppermute | solution.py:35
  166.9 4.0 %text_grads.1 = f32[256,1280]{1,0:T(8,128)} custom-call(f32[4]{0:T(128)S(1)} %pad_maximum_fusion.s.refs_0_, f32[8,256]{1,0:T(8,128)S(1)} %merge.1.own.refs_1_, f32[8,256]{1,0:T(8,128)S(1)} %get-tuple-element.87.refs_2_, f32[512,256]{1,0:T(8,128)S(1)} %get-tuple-element.63.l0.refs_3_, f32[512,256]{1,0:T(8,128)S(1)} %get-tuple-element.71.lp.refs_4_, ...), custom_call_target="tpu_custom_call" | custom-call | flops 4485000192 | bytes 1 | tf_op jit(solution)/shard_map/text_grads/pallas_call | solution.py:43
  170.9 1.1 last.1
  (25 shorter events, 1.2 us)
Async XLA Ops:
  0.6 9.6 %collective-permute-start = (f32[256,1280]{1,0:T(8,128)}, f32[256,1280]{1,0:T(8,128)}, u32[]{:S(2)}, u32[]{:S(2)}) collective-permute-start(f32[256,1280]{1,0:T(8,128)} %b0.6), channel_id=1, source_target_pairs={{0,1},{1,0},{2,3},{3,2},{4,5},{5,4},{6,7},{7,6},{8,9},{9,8},{10,11... | collective-permute-start | bytes 3932168 | tf_op jit(solution)/shard_map/ppermute | solution.py:35
  0.7 15.8 %collective-permute-start.1 = (f32[256,1280]{1,0:T(8,128)}, f32[256,1280]{1,0:T(8,128)}, u32[]{:S(2)}, u32[]{:S(2)}) collective-permute-start(f32[256,1280]{1,0:T(8,128)} %b0.7), channel_id=1, source_target_pairs={{0,1},{1,0},{2,3},{3,2},{4,5},{5,4},{6,7},{7,6},{8,9},{9,8},{10,11... | collective-permute-start | bytes 3932168 | tf_op jit(solution)/shard_map/ppermute | solution.py:35
  1.2 38.1 %collective-permute-start.4 = (f32[256,1280]{1,0:T(8,128)}, f32[256,1280]{1,0:T(8,128)S(1)}, u32[]{:S(2)}, u32[]{:S(2)}) collective-permute-start(f32[256,1280]{1,0:T(8,128)} %b0.6), channel_id=1, source_target_pairs={{0,2},{1,3},{2,4},{3,5},{4,6},{5,7},{6,8},{7,9},{8,10},{9,11},{10,... | collective-permute-start | bytes 3932168 | tf_op jit(solution)/shard_map/ppermute | solution.py:24
  3.1 36.1 %collective-permute-start.3 = (f32[256,1280]{1,0:T(8,128)}, f32[256,1280]{1,0:T(8,128)}, u32[]{:S(2)}, u32[]{:S(2)}) collective-permute-start(f32[256,1280]{1,0:T(8,128)} %b0.6), channel_id=1, source_target_pairs={{0,254},{1,255},{2,0},{3,1},{4,2},{5,3},{6,4},{7,5},{8,6},{9,7},{1... | collective-permute-start | bytes 3932168 | tf_op jit(solution)/shard_map/ppermute | solution.py:24
  9.5 57.9 %collective-permute-start.2 = (f32[256,1280]{1,0:T(8,128)}, f32[256,1280]{1,0:T(8,128)S(1)}, u32[]{:S(2)}, u32[]{:S(2)}) collective-permute-start(f32[256,1280]{1,0:T(8,128)} %b0.7), channel_id=1, source_target_pairs={{0,2},{1,3},{2,4},{3,5},{4,6},{5,7},{6,8},{7,9},{8,10},{9,11},{10,... | collective-permute-start | bytes 3932168 | tf_op jit(solution)/shard_map/ppermute | solution.py:24
  10.2 57.1 %collective-permute-start.7 = (f32[256,1280]{1,0:T(8,128)}, f32[256,1280]{1,0:T(8,128)S(1)}, u32[]{:S(2)}, u32[]{:S(2)}) collective-permute-start(f32[256,1280]{1,0:T(8,128)} %b0.7), channel_id=1, source_target_pairs={{0,254},{1,255},{2,0},{3,1},{4,2},{5,3},{6,4},{7,5},{8,6},{9,7},{1... | collective-permute-start | bytes 3932168 | tf_op jit(solution)/shard_map/ppermute | solution.py:24
  16.5 1.3 copy-start
  17.8 1.3 copy-start.1
  19.1 3.7 %copy-start.2 = (f32[256,1280]{1,0:T(8,128)S(1)}, f32[256,1280]{1,0:T(8,128)}, u32[]{:S(2)}) copy-start(f32[256,1280]{1,0:T(8,128)} %b0.7) | copy-start | bytes 3932164
  39.3 55.0 %collective-permute-start.6 = (f32[256,1280]{1,0:T(8,128)}, f32[256,1280]{1,0:T(8,128)S(1)}, u32[]{:S(2)}, u32[]{:S(2)}) collective-permute-start(f32[256,1280]{1,0:T(8,128)} %collective-permute-done.3.bm), channel_id=1, source_target_pairs={{0,254},{1,255},{2,0},{3,1},{4,2},{5,3},{6,4},{7,5},{8,6},{9,7},{1... | collective-permute-start | bytes 3932168 | tf_op jit(solution)/shard_map/ppermute | solution.py:24
  45.7 48.6 %collective-permute-start.8 = (f32[256,1280]{1,0:T(8,128)S(1)}, f32[256,1280]{1,0:T(8,128)S(1)}, u32[]{:S(2)}, u32[]{:S(2)}) collective-permute-start(f32[256,1280]{1,0:T(8,128)S(1)} %collective-permute-done.4.bp), channel_id=1, source_target_pairs={{1,3},{3,5},{5,7},{7,9},{9,11},{11,13},{13,15},{15,17},{17,19},{19... | collective-permute-start | bytes 3932168 | tf_op jit(solution)/shard_map/ppermute | solution.py:24
  67.4 35.9 %collective-permute-start.5 = (f32[256,1280]{1,0:T(8,128)S(1)}, f32[256,1280]{1,0:T(8,128)S(1)}, u32[]{:S(2)}, u32[]{:S(2)}) collective-permute-start(f32[256,1280]{1,0:T(8,128)S(1)} %collective-permute-done.2.bp), channel_id=1, source_target_pairs={{0,2},{1,3},{2,4},{3,5},{4,6},{5,7},{6,8},{7,9},{8,10},{9,11},{10,... | collective-permute-start | bytes 3932168 | tf_op jit(solution)/shard_map/ppermute | solution.py:24
  67.4 40.9 %collective-permute-start.9 = (f32[256,1280]{1,0:T(8,128)S(1)}, f32[256,1280]{1,0:T(8,128)S(1)}, u32[]{:S(2)}, u32[]{:S(2)}) collective-permute-start(f32[256,1280]{1,0:T(8,128)S(1)} %collective-permute-done.7.bm), channel_id=1, source_target_pairs={{0,254},{2,0},{4,2},{6,4},{8,6},{10,8},{12,10},{14,12},{16,14},{18... | collective-permute-start | bytes 3932168 | tf_op jit(solution)/shard_map/ppermute | solution.py:24
  111.9 1.5 collective-permute-start.10
  114.0 8.1 %collective-permute-start.13 = (f32[8,256]{1,0:T(8,128)S(1)}, f32[8,256]{1,0:T(8,128)S(1)}, u32[]{:S(2)}, u32[]{:S(2)}) collective-permute-start(f32[8,256]{1,0:T(8,128)S(1)} %merge.1.own.refs_1_), channel_id=1, source_target_pairs={{0,2},{1,5},{2,4},{3,7},{4,6},{5,9},{6,8},{7,11},{8,10},{9,13},{10... | collective-permute-start | bytes 24584 | tf_op jit(solution)/shard_map/ppermute | solution.py:30
  114.0 8.1 %collective-permute-start.11 = (f32[8,256]{1,0:T(8,128)S(1)}, f32[8,256]{1,0:T(8,128)S(1)}, u32[]{:S(2)}, u32[]{:S(2)}) collective-permute-start(f32[8,256]{1,0:T(8,128)S(1)} %merge.1.own.refs_1_), channel_id=1, source_target_pairs={{0,254},{1,253},{2,0},{3,255},{4,2},{5,1},{6,4},{7,3},{8,6},{9,5},... | collective-permute-start | bytes 24584 | tf_op jit(solution)/shard_map/ppermute | solution.py:30
  122.1 1.2 collective-permute-start.14
  122.1 1.3 collective-permute-start.12
  124.0 12.3 %collective-permute-start.15 = (f32[8,128]{1,0:T(8,128)S(1)}, f32[8,128]{1,0:T(8,128)S(1)}, u32[]{:S(2)}, u32[]{:S(2)}) collective-permute-start(f32[8,128]{1,0:T(8,128)S(1)} %get-tuple-element.90.a), channel_id=1, source_target_pairs={{0,16},{1,17},{2,18},{3,19},{4,20},{5,21},{6,22},{7,23},{8,24},{9,... | collective-permute-start | bytes 12296 | tf_op jit(solution)/shard_map/ppermute | solution.py:35
  136.9 12.7 %collective-permute-start.18 = (f32[256,1280]{1,0:T(8,128)S(1)}, f32[256,1280]{1,0:T(8,128)S(1)}, u32[]{:S(2)}, u32[]{:S(2)}) collective-permute-start(f32[256,1280]{1,0:T(8,128)S(1)} %image_share.1), channel_id=1, source_target_pairs={{0,1},{1,0},{2,3},{3,2},{4,5},{5,4},{6,7},{7,6},{8,9},{9,8},{10,11... | collective-permute-start | bytes 3932168 | tf_op jit(solution)/shard_map/ppermute | solution.py:35
  137.0 5.2 %collective-permute-start.16 = (f32[8,128]{1,0:T(8,128)S(1)}, f32[8,128]{1,0:T(8,128)S(1)}, u32[]{:S(2)}, u32[]{:S(2)}) collective-permute-start(f32[8,128]{1,0:T(8,128)S(1)} %sum.5.a), channel_id=1, source_target_pairs={{0,32},{1,33},{2,34},{3,35},{4,36},{5,37},{6,38},{7,39},{8,40},{9,... | collective-permute-start | bytes 12296 | tf_op jit(solution)/shard_map/ppermute | solution.py:35
  142.8 24.1 %collective-permute-start.21 = (f32[256,1280]{1,0:T(8,128)S(1)}, f32[256,1280]{1,0:T(8,128)S(1)}, u32[]{:S(2)}, u32[]{:S(2)}) collective-permute-start(f32[256,1280]{1,0:T(8,128)S(1)} %text_share.1), channel_id=1, source_target_pairs={{0,1},{1,0},{2,3},{3,2},{4,5},{5,4},{6,7},{7,6},{8,9},{9,8},{10,11... | collective-permute-start | bytes 3932168 | tf_op jit(solution)/shard_map/ppermute | solution.py:35
  142.9 5.6 %collective-permute-start.17 = (f32[8,128]{1,0:T(8,128)S(1)}, f32[8,128]{1,0:T(8,128)S(1)}, u32[]{:S(2)}, u32[]{:S(2)}) collective-permute-start(f32[8,128]{1,0:T(8,128)S(1)} %sum.6.a), channel_id=1, source_target_pairs={{0,64},{1,65},{2,66},{3,67},{4,68},{5,69},{6,70},{7,71},{8,72},{9,... | collective-permute-start | bytes 12296 | tf_op jit(solution)/shard_map/ppermute | solution.py:35
  149.1 5.2 %collective-permute-start.19 = (f32[8,128]{1,0:T(8,128)S(1)}, f32[8,128]{1,0:T(8,128)S(1)}, u32[]{:S(2)}, u32[]{:S(2)}) collective-permute-start(f32[8,128]{1,0:T(8,128)S(1)} %sum.7.a), channel_id=1, source_target_pairs={{0,128},{1,129},{2,130},{3,131},{4,132},{5,133},{6,134},{7,135},{8... | collective-permute-start | bytes 12296 | tf_op jit(solution)/shard_map/ppermute | solution.py:35
  154.8 4.6 %collective-permute-start.20 = (f32[8,128]{1,0:T(8,128)S(1)}, f32[8,128]{1,0:T(8,128)S(1)}, u32[]{:S(2)}, u32[]{:S(2)}) collective-permute-start(f32[8,128]{1,0:T(8,128)S(1)} %sum.8.a), channel_id=1, source_target_pairs={{0,4},{1,5},{2,6},{3,7},{4,0},{5,1},{6,2},{7,3},{8,12},{9,13},{10,... | collective-permute-start | bytes 12296 | tf_op jit(solution)/shard_map/ppermute | solution.py:35
  160.0 10.9 %collective-permute-start.22 = (f32[8,128]{1,0:T(8,128)S(1)}, f32[8,128]{1,0:T(8,128)S(1)}, u32[]{:S(2)}, u32[]{:S(2)}) collective-permute-start(f32[8,128]{1,0:T(8,128)S(1)} %sum.9.a), channel_id=1, source_target_pairs={{0,8},{1,9},{2,10},{3,11},{4,12},{5,13},{6,14},{7,15},{8,0},{9,1},... | collective-permute-start | bytes 12296 | tf_op jit(solution)/shard_map/ppermute | solution.py:35

commit v4 on v3

--- a/solution.py
+++ b/solution.py
@@ -39,16 +39,14 @@
     return lax.optimization_barrier((value, done))[0]
 
 
-def call(kernel, name, micros, outs, args, scratch=(), out_space=VMEM, alias=None):
+def call(kernel, name, micros, outs, args, scratch=(), alias=None, in_hbm=(), out_hbm=()):
     return pl.pallas_call(
         kernel,
         name=name,
         out_shape=[jax.ShapeDtypeStruct(s, d) for s, d in outs],
-        in_specs=[SMEM] + [VMEM] * (len(args) - 1),
-        out_specs=[out_space] * len(outs),
-        scratch_shapes=[
-            pltpu.VMEM(*x) if isinstance(x, tuple) else x for x in scratch
-        ],
+        in_specs=[SMEM] + [ANY if k in in_hbm else VMEM for k in range(1, len(args))],
+        out_specs=[ANY if k in out_hbm else VMEM for k in range(len(outs))],
+        scratch_shapes=[pltpu.VMEM(*x) if isinstance(x, tuple) else x for x in scratch],
         compiler_params=pltpu.CompilerParams(vmem_limit_bytes=LIMIT),
         input_output_aliases=alias or {},
         cost_estimate=pl.CostEstimate(
@@ -152,35 +150,49 @@
     diag[...] = jnp.sum(jnp.where(i == j, l0[0:n, :], 0.0), axis=0, keepdims=True)
 
 
-def other_far(s, a, b, text):
+def put_far(s, parts, k, block, lf, blocks_h, blocks_l, split):
+    n = block.shape[0]
+    put_three(block, *split)
+    r = pl.ds(4 * k * n, n)
+    blocks_h[r], blocks_l[r] = split[0][...], split[1][...]
+    r = pl.ds(k * n, n)
+    lf[r, :] = s[0] * scores(take(parts, r), take(split))
+
+
+def put_rows(k, top, mean, lf, out, at):
+    n = lf.shape[1]
+    r = pl.ds(k * n, n)
+    t, m = merge([(top[r, :1], mean[r, :1]), lse([lf[r, :]], 1)])
+    out[at : at + 1, :] = row(t)
+    out[at + 1 : at + 2, :] = row(m)
+
+
+def text_far_kernel(s, xh, xm, xl, a, b, top, mean, old_h, old_l, lf, rows_out, blocks_h, blocks_l, *split):
     first = s[1] == 0.0
-    return jnp.where(first, b[...], a[...]) if text else jnp.where(first, a[...], b[...])
-
-
-def far_scores(s, parts, a, b, text, top, mean, lf, rows_out, blocks_h, blocks_l, *split):
-    n = a.shape[0]
-    for k, block in enumerate((a[...], other_far(s, a, b, text))):
-        put_three(block, *split)
-        r = pl.ds(4 * k * n, n)
-        blocks_h[r], blocks_l[r] = split[0][...], split[1][...]
-        r = pl.ds(k * n, n)
-        lf[r, :] = s[0] * scores(take(parts, r), take(split))
-    t, m = merge([(top[:, :1], mean[:, :1]), lse([lf[...]], 1)])
-    rows_out[0:1, :] = row(t[:n])
-    rows_out[1:2, :] = row(m[:n])
-    rows_out[2:3, :] = row(t[n:])
-    rows_out[3:4, :] = row(m[n:])
-
-
-def text_far_kernel(s, xh, xm, xl, a, b, top, mean, old_h, old_l, lf, rows_out, *rest):
-    far_scores(s, (xh, xm, xl), a, b, False, top, mean, lf, rows_out, *rest)
-
-
-def image_far_kernel(s, yh, ym, yl, a, b, top, mean, old_h, old_l, image_rows, diag, lf, out, *rest):
-    far_scores(s, (yh, ym, yl), a, b, True, top, mean, lf, out.at[4:8], *rest)
+    for k, block in ((0, a[...]), (1, jnp.where(first, a[...], b[...]))):
+        put_far(s, (xh, xm, xl), k, block, lf, blocks_h, blocks_l, split)
+        put_rows(k, top, mean, lf, rows_out, 2 * k)
+
+
+def image_behind_kernel(s, yh, ym, yl, block, top, mean, old_h, old_l, image_rows, diag, lf, out, blocks_h, blocks_l, *split):
+    n = block.shape[0]
+    put_far(s, (yh, ym, yl), 0, block[...], lf, blocks_h, blocks_l, split)
+    put_rows(0, top, mean, lf, out, 4)
     out[0:4, :] = image_rows[...]
     out[8:9, :] = diag[...]
-    out[9:16, :] = jnp.zeros((7, out.shape[1]), F32)
+    out[9:16, :] = jnp.zeros((7, n), F32)
+
+    @pl.when(s[1] != 0.0)
+    def _():
+        put_far(s, (yh, ym, yl), 1, block[...], lf, blocks_h, blocks_l, split)
+        put_rows(1, top, mean, lf, out, 6)
+
+
+def image_ahead_kernel(s, yh, ym, yl, block, top, mean, old_h, old_l, old_lf, old, lf, out, blocks_h, blocks_l, *split):
+    @pl.when(s[1] == 0.0)
+    def _():
+        put_far(s, (yh, ym, yl), 1, block[...], lf, blocks_h, blocks_l, split)
+        put_rows(1, top, mean, lf, out, 6)
 
 
 def merge_kernel(s, mine, got, out):
@@ -205,23 +217,31 @@
     out[6:8, :] = jnp.zeros((2, n), F32)
 
 
-def sort_kernel(s, own, v, vs, u, us, out, parts):
+def sort_kernel(s, own, v, vs, u, us, out):
     first = s[1] == 0.0
     for k, (a, b) in enumerate(((u, us), (v, vs))):
         out[2 * k : 2 * k + 2, :] = jnp.where(first, a[0:2, :], b[2:4, :])
         out[2 * k + 4 : 2 * k + 6, :] = jnp.where(first, b[2:4, :], a[0:2, :])
-    ahead = jnp.where(first, v[4:6, :128], vs[4:6, :128])
-    behind = jnp.where(first, u[4:6, :128], us[4:6, :128])
-    parts[...] = jnp.zeros_like(parts)
-    parts[0:2, :] = own[4:6, :128] + jnp.where(s[2] == 0.0, ahead, behind)
-
-
-def sum_kernel(s, a, b, out):
-    out[...] = a[...] + b[...]
-
-
-def last_kernel(s, a, b, loss, scale_grad):
-    total = (a[...] + b[...]) * (1.0 / s[3])
+
+
+def pair_kernel(s, own, mate, out):
+    out[...] = jnp.zeros_like(out)
+    out[0:2, :] = own[4:6, :128] + mate[4:6, :128]
+
+
+def paired(values):
+    if len(values) == 1:
+        return values[0]
+    return paired([a + b for a, b in zip(values[::2], values[1::2])])
+
+
+def sum_kernel(s, *refs):
+    refs[-1][...] = paired([r[...] for r in refs[:-1]])
+
+
+def last_kernel(s, *refs):
+    *terms, loss, scale_grad = refs
+    total = paired([t[...] for t in terms]) * (1.0 / s[2])
     loss[...] = total[0:1, 0:1]
     scale_grad[...] = total[1:2, 0:1] / s[0]
 
@@ -280,9 +300,8 @@
     copies = []
     for k in range(out.shape[1] // TILE):
         d = pl.ds(k * TILE, TILE)
-        done[:, d] = factor * (
-            tile_grads(wh, wl, bh, bl, pl.ds(0, 4 * n), d) + share[:, d]
-        )
+        total = tile_grads(wh, wl, bh, bl, pl.ds(0, 4 * n), d) + share[:, d]
+        done[:, d] = factor * total
         copies.append(pltpu.make_async_copy(done.at[:, d], out.at[:, d], sem.at[k]))
         copies[-1].start()
     for copy in copies:
@@ -292,8 +311,8 @@
 def on_device(image, text, scale):
     n, depth = image.shape
     device = lax.axis_index("dp")
-    core, odd = (device % 2).astype(F32), (device // 2 % 2).astype(F32)
-    s = jnp.stack([scale, core, odd, jnp.float32(2 * n * lax.axis_size("dp"))])
+    core = (device % 2).astype(F32)
+    s = jnp.stack([scale, core, jnp.float32(2 * n * lax.axis_size("dp"))])
     block = ((n, depth), F32)
     both = ((2 * n, n), F32)
     part = ((2 * n, depth), BF16)
@@ -325,45 +344,55 @@
     args = s, *x, after(t_mm, i_top), t_pp, top, mean, *t_parts
     outs = [both, four] + five
     kept = {8: 2, 9: 3}
-    lf, image_rows, *t_parts = call(text_far_kernel, "text_far", 4.0, outs, args, split, alias=kept)
-    args = s, *y, after(i_pp, lf), i_mm, i_top, i_mean, *i_parts, image_rows, diag
+    lf, image_rows, *t_parts = call(text_far_kernel, "text_far", 4.0, outs, args, split, kept)
+    args = s, *y, after(i_pp, lf), i_top, i_mean, *i_parts, image_rows, diag
     outs = [both, ((16, n), F32)] + five
-    vf, mine, *i_parts = call(image_far_kernel, "image_far", 4.0, outs, args, split, alias=kept)
+    kept = {7: 2, 8: 3}
+    vf, mine, *i_parts = call(image_behind_kernel, "image_behind", 3.0, outs, args, split, kept)
+    args = s, *y, i_mm, i_top, i_mean, *i_parts, vf, mine
+    kept = {7: 2, 8: 3, 9: 0, 10: 1}
+    vf, mine, *i_parts = call(image_ahead_kernel, "image_ahead", 2.0, outs, args, split, kept)
 
     got = swap(mine)
     (own,) = call(merge_kernel, "merge", 0.6, [((8, n), F32)], (s, mine, got))
     u, v = along(own, 1), along(own, -1)
-    args = s, own, v, swap(v), u, swap(u)
     terms = [((8, 128), F32)]
-    lses, parts = call(sort_kernel, "sort", 0.5, [((8, n), F32)] + terms, args)
-
-    def add(parts, bit, *done):
-        args = s, after(parts, *done), swap(parts, bit)
+    (parts,) = call(pair_kernel, "pair", 0.5, terms, (s, own, swap(own, 2)))
+
+    def add(parts, bits, *done):
+        args = s, after(parts, *done), *(swap(parts, b) for b in bits)
         return call(sum_kernel, "sum", 0.5, terms, args)[0]
+
+    parts = add(parts, (4,))
+    args = s, after(own, parts), v, swap(v), u, swap(u)
+    (lses,) = call(sort_kernel, "sort", 0.5, [((8, n), F32)], args)
 
     image_args = l0, lp, lm, lf, *t_parts
     text_args = v0, vp, vm, vf, *i_parts
     weights = [((n, 4 * n), BF16)] * 2
-    final = weights + [block, pltpu.SemaphoreType.DMA((depth // TILE,))]
+    final = [block, pltpu.SemaphoreType.DMA((depth // TILE,))]
     kernel = functools.partial(share_kernel, False)
     (share,) = call(kernel, "image_share", 3.1, [block], (s, own, lses, *image_args), weights)
-    parts = add(parts, 16, share)
+    parts = add(parts, (8,), share)
     image_share = swap(after(share, parts))
     kernel = functools.partial(share_kernel, True)
     args = s, after(own, parts), lses, *text_args
     (share,) = call(kernel, "text_share", 3.1, [block], args, weights)
-    parts = add(parts, 32, share)
+    parts = add(parts, (64, 128, 192), share)
     text_share = swap(after(share, parts))
-    parts = add(parts, 64)
+
+    y_part = swap(parts, 32)
     kernel = functools.partial(grads_kernel, False)
     args = s, after(own, parts), lses, *image_args, image_share
-    (image_grad,) = call(kernel, "image_grads", 3.9, [block], args, final, ANY)
-    parts = add(add(parts, 128, image_grad), 4)
+    final = weights + final
+    (image_grad,) = call(kernel, "image_grads", 3.9, [block], args, final, out_hbm=(0,))
+    args = s, after(parts, image_grad), y_part
+    (parts,) = call(sum_kernel, "sum", 0.5, terms, args)
+    y_part = swap(parts, 16)
     kernel = functools.partial(grads_kernel, True)
     args = s, after(own, parts), lses, *text_args, text_share
-    (text_grad,) = call(kernel, "text_grads", 3.9, [block], args, final, ANY)
-    z_part = swap(parts, 8)
-    args = s, after(parts, text_grad), z_part
+    (text_grad,) = call(kernel, "text_grads", 3.9, [block], args, final, out_hbm=(0,))
+    args = s, after(parts, text_grad), y_part
     loss, scale_grad = call(last_kernel, "last", 0.5, [((1, 1), F32)] * 2, args)
     return (loss.reshape(()), image_grad, text_grad, scale_grad.reshape(()))
 

time: 175 us -> 170 us (0.971)
  the two profiles are of different devices: /device:TPU:2 before, /device:TPU:8 now
where the time goes in v4:
time: 170 us; the launch traced here: 168 us
  waiting for transfers between devices  58.9 us (35%)
  starting transfers between devices  55.6 us (33%)
  Pallas kernels  48.9 us (29%)
  local copies, waits for them, and re-layouts  2.63 us (2%)
  between operations  1.71 us (1%)
    ppermute x8, waiting for transfers between devices, shift(): return lax.ppermute(value, 'dp', pairs)  54.4 us
    pallas_call x21, Pallas kernels, call(): pl.pallas_call(kernel, name=name, out_shape=[jax.ShapeDtypeStruct(s, d) f...  48.9 us
    ppermute x15, starting transfers between devices, swap(): return lax.ppermute(value, 'dp', [(s, s ^ bit) for s in range(count)])  22.5 us
    ppermute x8, starting transfers between devices, shift(): return lax.ppermute(value, 'dp', pairs)  19.1 us
    ppermute x2, starting transfers between devices, along(): return lax.ppermute(value, 'dp', pairs)  14 us
    ppermute x15, waiting for transfers between devices, swap(): return lax.ppermute(value, 'dp', [(s, s ^ bit) for s in range(count)])  4.5 us
  transfers between devices with their start and end apart: 25, of which 9 were waited for; matrix products, arithmetic and copies ran while one was open for 0% of the time, Pallas kernels for 26%

profile of v4, /device:TPU:8, one launch (start us, length us, event | category | flops | bytes accessed | tf_op | source)
XLA Modules:
  0.0 167.8 jit_solution(6485555970663449914)
XLA Ops:
  1.2 1.9 %collective-permute-start.4 = (f32[256,1280]{1,0:T(8,128)}, f32[256,1280]{1,0:T(8,128)S(1)}, u32[]{:S(2)}, u32[]{:S(2)}) collective-permute-start(f32[256,1280]{1,0:T(8,128)} %b0.6), channel_id=1, source_target_pairs={{0,2},{1,3},{2,4},{3,5},{4,6},{5,7},{6,8},{7,9},{8,10},{9,11},{10,... | collective-permute-start | bytes 3932168 | tf_op jit(solution)/shard_map/ppermute | solution.py:24
  3.1 3.8 %collective-permute-start.3 = (f32[256,1280]{1,0:T(8,128)}, f32[256,1280]{1,0:T(8,128)}, u32[]{:S(2)}, u32[]{:S(2)}) collective-permute-start(f32[256,1280]{1,0:T(8,128)} %b0.6), channel_id=1, source_target_pairs={{0,254},{1,255},{2,0},{3,1},{4,2},{5,3},{6,4},{7,5},{8,6},{9,7},{1... | collective-permute-start | bytes 3932168 | tf_op jit(solution)/shard_map/ppermute | solution.py:24
  7.0 2.0 %collective-permute-start.2 = (f32[256,1280]{1,0:T(8,128)}, f32[256,1280]{1,0:T(8,128)S(1)}, u32[]{:S(2)}, u32[]{:S(2)}) collective-permute-start(f32[256,1280]{1,0:T(8,128)} %b0.7), channel_id=1, source_target_pairs={{0,254},{1,255},{2,0},{3,1},{4,2},{5,3},{6,4},{7,5},{8,6},{9,7},{1... | collective-permute-start | bytes 3932168 | tf_op jit(solution)/shard_map/ppermute | solution.py:24
  9.8 1.3 copy-done
  11.1 1.3 copy-done.1
  12.4 3.7 %text_own.1 = (bf16[512,1280]{1,0:T(8,128)(2,1)S(1)}, bf16[512,1280]{1,0:T(8,128)(2,1)S(1)}, bf16[512,1280]{1,0:T(8,128)(2,1)S(1)}, f32[512,256]{1,0:T(8,128)S(1)}) custom-call(f32[3]{0:T(128)S(1)} %pad_maximum_fusion.s.refs_0_, f32[256,1280]{1,0:T(8,128)S(1)} %copy-done.1, f32[256,1280]{1,0:T(8,128)} %collective-permute-done.1.a1, f32[256,1280]{1,0:T(8,128)S(1)} %copy-done), custom_call_target="tpu_custom_call" | custom-call | flops 4255000064 | bytes 1 | tf_op jit(solution)/shard_map/text_own/pallas_call | solution.py:43
  16.1 3.6 %image_own.1 = (bf16[512,1280]{1,0:T(8,128)(2,1)S(1)}, bf16[512,1280]{1,0:T(8,128)(2,1)S(1)}, bf16[512,1280]{1,0:T(8,128)(2,1)S(1)}, f32[512,256]{1,0:T(8,128)S(1)}) custom-call(f32[3]{0:T(128)S(1)} %pad_maximum_fusion.s.refs_0_, f32[256,1280]{1,0:T(8,128)S(1)} %copy-done, f32[256,1280]{1,0:T(8,128)} %collective-permute-done.a1, f32[256,1280]{1,0:T(8,128)S(1)} %copy-done.2), custom_call_target="tpu_custom_call" | custom-call | flops 4255000064 | bytes 1 | tf_op jit(solution)/shard_map/image_own/pallas_call | solution.py:43
  19.7 17.0 %collective-permute-done.4.bp = f32[256,1280]{1,0:T(8,128)S(1)} collective-permute-done((f32[256,1280]{1,0:T(8,128)}, f32[256,1280]{1,0:T(8,128)S(1)}, u32[]{:S(2)}, u32[]{:S(2)}) %collective-permute-start.4) | collective-permute-done | bytes 1310752 | tf_op jit(solution)/shard_map/ppermute | solution.py:24
  36.8 4.3 %collective-permute-start.8 = (f32[256,1280]{1,0:T(8,128)}, f32[256,1280]{1,0:T(8,128)S(1)}, u32[]{:S(2)}, u32[]{:S(2)}) collective-permute-start(f32[256,1280]{1,0:T(8,128)} %collective-permute-done.3.bm), channel_id=1, source_target_pairs={{0,254},{1,255},{2,0},{3,1},{4,2},{5,3},{6,4},{7,5},{8,6},{9,7},{1... | collective-permute-start | bytes 3932168 | tf_op jit(solution)/shard_map/ppermute | solution.py:24
  41.0 1.0 collective-permute-start.9
  42.0 6.0 %text_near.1 = (f32[512,256]{1,0:T(8,128)S(1)}, f32[512,256]{1,0:T(8,128)S(1)}, bf16[1280,1280]{1,0:T(8,128)(2,1)S(1)}, bf16[1280,1280]{1,0:T(8,128)(2,1)S(1)}) custom-call(f32[3]{0:T(128)S(1)} %pad_maximum_fusion.s.refs_0_, bf16[512,1280]{1,0:T(8,128)(2,1)S(1)} %get-tuple-element.63.h.xh, bf16[512,1280]{1,0:T(8,128)(2,1)S(1)} %get-tuple-element.64.m.xm, ...), custom_call_target="tpu_custom_call" | custom-call | flops 5520000000 | bytes 1 | tf_op jit(solution)/shard_map/text_near/pallas_call | solution.py:43
  48.0 1.3 text_stats.1
  49.4 15.5 %collective-permute-done.6.bp = f32[256,1280]{1,0:T(8,128)S(1)} collective-permute-done((f32[256,1280]{1,0:T(8,128)}, f32[256,1280]{1,0:T(8,128)S(1)}, u32[]{:S(2)}, u32[]{:S(2)}) %collective-permute-start.6) | collective-permute-done | bytes 1310752 | tf_op jit(solution)/shard_map/ppermute | solution.py:24
  64.8 6.1 %collective-permute-start.5 = (f32[256,1280]{1,0:T(8,128)S(1)}, f32[256,1280]{1,0:T(8,128)S(1)}, u32[]{:S(2)}, u32[]{:S(2)}) collective-permute-start(f32[256,1280]{1,0:T(8,128)S(1)} %collective-permute-done.2.bm), channel_id=1, source_target_pairs={{0,254},{2,0},{4,2},{6,4},{8,6},{10,8},{12,10},{14,12},{16,14},{18... | collective-permute-start | bytes 3932168 | tf_op jit(solution)/shard_map/ppermute | solution.py:24
  70.9 5.2 %image_near.1 = (f32[512,256]{1,0:T(8,128)S(1)}, f32[512,256]{1,0:T(8,128)S(1)}, bf16[1280,1280]{1,0:T(8,128)(2,1)S(1)}, bf16[1280,1280]{1,0:T(8,128)(2,1)S(1)}) custom-call(f32[3]{0:T(128)S(1)} %pad_maximum_fusion.s.refs_0_, bf16[512,1280]{1,0:T(8,128)(2,1)S(1)} %get-tuple-element.60.h.yh, bf16[512,1280]{1,0:T(8,128)(2,1)S(1)} %get-tuple-element.61.m.ym, ...), custom_call_target="tpu_custom_call" | custom-call | flops 5520000000 | bytes 1 | tf_op jit(solution)/shard_map/image_near/pallas_call | solution.py:43
  76.2 1.9 %image_stats.1 = (f32[512,128]{1,0:T(8,128)S(1)}, f32[512,128]{1,0:T(8,128)S(1)}, f32[1,256]{1,0:T(1,128)}) custom-call(f32[3]{0:T(128)S(1)} %pad_maximum_fusion.s.refs_0_, f32[512,256]{1,0:T(8,128)S(1)} %get-tuple-element.66.l0.refs_3_, f32[512,256]{1,0:T(8,128)S(1)} %get-tuple-element.74.lp.refs_4_, f32[512,256]{1,0:T(8,128)S(1)} %get-tuple-element.75.lm.refs_5_), custom_call_target="tpu_custom_call" | custom-call | flops 2070000000 | bytes 1 | tf_op jit(solution)/shard_map/image_stats/pallas_call | solution.py:43
  78.1 13.7 %collective-permute-done.8.a = f32[256,1280]{1,0:T(8,128)S(1)} collective-permute-done((f32[256,1280]{1,0:T(8,128)}, f32[256,1280]{1,0:T(8,128)S(1)}, u32[]{:S(2)}, u32[]{:S(2)}) %collective-permute-start.8) | collective-permute-done | bytes 1310752 | tf_op jit(solution)/shard_map/ppermute | solution.py:24
  91.8 3.6 %text_far.1 = (f32[512,256]{1,0:T(8,128)S(1)}, f32[4,256]{1,0:T(4,128)S(1)}, bf16[1280,1280]{1,0:T(8,128)(2,1)S(1)}, bf16[1280,1280]{1,0:T(8,128)(2,1)S(1)}) custom-call(f32[3]{0:T(128)S(1)} %pad_maximum_fusion.s.refs_0_, bf16[512,1280]{1,0:T(8,128)(2,1)S(1)} %get-tuple-element.63.h.xh, ...), custom_call_target="tpu_custom_call", output_to_operand_aliasing={{2}: (8, {}), {3}: (9, {})} | custom-call | flops 4600000000 | bytes 1 | tf_op jit(solution)/shard_map/text_far/pallas_call | solution.py:43
  95.4 3.3 %collective-permute-done.7.block = f32[256,1280]{1,0:T(8,128)S(1)} collective-permute-done((f32[256,1280]{1,0:T(8,128)S(1)}, f32[256,1280]{1,0:T(8,128)S(1)}, u32[]{:S(2)}, u32[]{:S(2)}) %collective-permute-start.7) | collective-permute-done | bytes 1310752 | tf_op jit(solution)/shard_map/ppermute | solution.py:24
  98.7 2.1 %image_behind.1 = (f32[512,256]{1,0:T(8,128)S(1)}, f32[16,256]{1,0:T(8,128)S(1)}, bf16[1280,1280]{1,0:T(8,128)(2,1)S(1)}, bf16[1280,1280]{1,0:T(8,128)(2,1)S(1)}) custom-call(f32[3]{0:T(128)S(1)} %pad_maximum_fusion.s.refs_0_, bf16[512,1280]{1,0:T(8,128)(2,1)S(1)} %get-tuple-element.60.h.yh, ...), custom_call_target="tpu_custom_call", output_to_operand_aliasing={{2}: (7, {}), {3}: (8, {})} | custom-call | flops 3449999872 | bytes 1 | tf_op jit(solution)/shard_map/image_behind/pallas_call | solution.py:43
  100.8 4.9 %collective-permute-done.5.block = f32[256,1280]{1,0:T(8,128)S(1)} collective-permute-done((f32[256,1280]{1,0:T(8,128)S(1)}, f32[256,1280]{1,0:T(8,128)S(1)}, u32[]{:S(2)}, u32[]{:S(2)}) %collective-permute-start.5) | collective-permute-done | bytes 1310752 | tf_op jit(solution)/shard_map/ppermute | solution.py:24
  105.7 2.2 %image_ahead.1 = (f32[512,256]{1,0:T(8,128)S(1)}, f32[16,256]{1,0:T(8,128)S(1)}, bf16[1280,1280]{1,0:T(8,128)(2,1)S(1)}, bf16[1280,1280]{1,0:T(8,128)(2,1)S(1)}) custom-call(f32[3]{0:T(128)S(1)} %pad_maximum_fusion.s.refs_0_, bf16[512,1280]{1,0:T(8,128)(2,1)S(1)} %get-tuple-element.60.h.yh, ...), custom_call_target="tpu_custom_call", output_to_operand_aliasing={{2}: (7, {}), {3}: (8, {}), {0}: (9, {}), {1}: (10, {})} | custom-call | flops 2300000000 | bytes 1 | tf_op jit(solution)/shard_map/image_ahead/pallas_call | solution.py:43
  107.9 2.8 %collective-permute-start.10 = (f32[16,256]{1,0:T(8,128)S(1)}, f32[16,256]{1,0:T(8,128)S(1)}, u32[]{:S(2)}, u32[]{:S(2)}) collective-permute-start(f32[16,256]{1,0:T(8,128)S(1)} %get-tuple-element.92.mine), channel_id=1, source_target_pairs={{0,1},{1,0},{2,3},{3,2},{4,5},{5,4},{6,7},{7,6},{8,9},{9,8},{10,11... | collective-permute-start | bytes 49160 | tf_op jit(solution)/shard_map/ppermute | solution.py:35
  110.7 0.8 collective-permute-done.10.got
  111.6 0.6 merge.1.own.refs_1_
  112.3 2.0 %collective-permute-start.15 = (f32[8,256]{1,0:T(8,128)S(1)}, f32[8,256]{1,0:T(8,128)S(1)}, u32[]{:S(2)}, u32[]{:S(2)}) collective-permute-start(f32[8,256]{1,0:T(8,128)S(1)} %merge.1.own.refs_1_), channel_id=1, source_target_pairs={{0,2},{1,5},{2,4},{3,7},{4,6},{5,9},{6,8},{7,11},{8,10},{9,13},{10... | collective-permute-start | bytes 24584 | tf_op jit(solution)/shard_map/ppermute | solution.py:30
  114.3 12.0 %collective-permute-start.13 = (f32[8,256]{1,0:T(8,128)S(1)}, f32[8,256]{1,0:T(8,128)S(1)}, u32[]{:S(2)}, u32[]{:S(2)}) collective-permute-start(f32[8,256]{1,0:T(8,128)S(1)} %merge.1.own.refs_1_), channel_id=1, source_target_pairs={{0,254},{1,253},{2,0},{3,255},{4,2},{5,1},{6,4},{7,3},{8,6},{9,5},... | collective-permute-start | bytes 24584 | tf_op jit(solution)/shard_map/ppermute | solution.py:30
  126.2 0.5 pair.1.refs_0_
  126.8 1.4 collective-permute-start.12
  128.3 0.5 collective-permute-start.14
  128.8 2.6 %collective-permute-done.12.refs_1_ = f32[8,128]{1,0:T(8,128)S(1)} collective-permute-done((f32[8,128]{1,0:T(8,128)S(1)}, f32[8,128]{1,0:T(8,128)S(1)}, u32[]{:S(2)}, u32[]{:S(2)}) %collective-permute-start.12) | collective-permute-done | bytes 4128 | tf_op jit(solution)/shard_map/ppermute | solution.py:35
  131.4 0.5 sum.4.refs_0_
  131.9 3.6 %collective-permute-start.17 = (f32[8,128]{1,0:T(8,128)S(1)}, f32[8,128]{1,0:T(8,128)S(1)}, u32[]{:S(2)}, u32[]{:S(2)}) collective-permute-start(f32[8,128]{1,0:T(8,128)S(1)} %sum.4.refs_0_), channel_id=1, source_target_pairs={{0,8},{1,9},{2,10},{3,11},{4,12},{5,13},{6,14},{7,15},{8,0},{9,1},... | collective-permute-start | bytes 12296 | tf_op jit(solution)/shard_map/ppermute | solution.py:35
  135.5 0.6 sort.1.refs_2_
  136.1 3.1 %image_share.1 = f32[256,1280]{1,0:T(8,128)S(1)} custom-call(f32[3]{0:T(128)S(1)} %pad_maximum_fusion.s.refs_0_, f32[8,256]{1,0:T(8,128)S(1)} %merge.1.own.refs_1_, f32[8,256]{1,0:T(8,128)S(1)} %sort.1.refs_2_, f32[512,256]{1,0:T(8,128)S(1)} %get-tuple-element.58.l0.refs_3_, f32[512,256]{1,0:T(8,128)S(1)} %get-tuple-element.69.lp.refs_4_, ...), custom_call_target="tpu_custom_call" | custom-call | flops 3564999936 | bytes 1 | tf_op jit(solution)/shard_map/image_share/pallas_call | solution.py:43
  139.6 0.5 sum.5.refs_0_
  140.2 2.8 %collective-permute-start.20 = (f32[8,128]{1,0:T(8,128)S(1)}, f32[8,128]{1,0:T(8,128)S(1)}, u32[]{:S(2)}, u32[]{:S(2)}) collective-permute-start(f32[8,128]{1,0:T(8,128)S(1)} %sum.5.refs_0_), channel_id=1, source_target_pairs={{0,192},{1,193},{2,194},{3,195},{4,196},{5,197},{6,198},{7,199},{8... | collective-permute-start | bytes 12296 | tf_op jit(solution)/shard_map/ppermute | solution.py:35
  143.1 0.8 collective-permute-start.19
  143.9 0.5 collective-permute-start.18
  144.4 3.1 %text_share.1 = f32[256,1280]{1,0:T(8,128)S(1)} custom-call(f32[3]{0:T(128)S(1)} %pad_maximum_fusion.s.refs_0_, f32[8,256]{1,0:T(8,128)S(1)} %merge.1.own.refs_1_, f32[8,256]{1,0:T(8,128)S(1)} %sort.1.refs_2_, f32[512,256]{1,0:T(8,128)S(1)} %get-tuple-element.66.l0.refs_3_, f32[512,256]{1,0:T(8,128)S(1)} %get-tuple-element.74.lp.refs_4_, ...), custom_call_target="tpu_custom_call" | custom-call | flops 3564999936 | bytes 1 | tf_op jit(solution)/shard_map/text_share/pallas_call | solution.py:43
  147.5 0.7 collective-permute-done.19.refs_2_
  148.2 0.5 sum.6.refs_0_
  148.8 2.9 %collective-permute-start.22 = (f32[8,128]{1,0:T(8,128)S(1)}, f32[8,128]{1,0:T(8,128)S(1)}, u32[]{:S(2)}, u32[]{:S(2)}) collective-permute-start(f32[8,128]{1,0:T(8,128)S(1)} %sum.6.refs_0_), channel_id=1, source_target_pairs={{0,32},{1,33},{2,34},{3,35},{4,36},{5,37},{6,38},{7,39},{8,40},{9,... | collective-permute-start | bytes 12296 | tf_op jit(solution)/shard_map/ppermute | solution.py:35
  151.7 4.0 %image_grads.1 = f32[256,1280]{1,0:T(8,128)} custom-call(f32[3]{0:T(128)S(1)} %pad_maximum_fusion.s.refs_0_, f32[8,256]{1,0:T(8,128)S(1)} %merge.1.own.refs_1_, f32[8,256]{1,0:T(8,128)S(1)} %sort.1.refs_2_, f32[512,256]{1,0:T(8,128)S(1)} %get-tuple-element.58.l0.refs_3_, f32[512,256]{1,0:T(8,128)S(1)} %get-tuple-element.69.lp.refs_4_, ...), custom_call_target="tpu_custom_call" | custom-call | flops 4485000192 | bytes 1 | tf_op jit(solution)/shard_map/image_grads/pallas_call | solution.py:43
  155.7 0.5 sum.7.refs_0_
  156.3 6.2 %collective-permute-start.24 = (f32[8,128]{1,0:T(8,128)S(1)}, f32[8,128]{1,0:T(8,128)S(1)}, u32[]{:S(2)}, u32[]{:S(2)}) collective-permute-start(f32[8,128]{1,0:T(8,128)S(1)} %sum.7.refs_0_), channel_id=1, source_target_pairs={{0,16},{1,17},{2,18},{3,19},{4,20},{5,21},{6,22},{7,23},{8,24},{9,... | collective-permute-start | bytes 12296 | tf_op jit(solution)/shard_map/ppermute | solution.py:35
  162.5 3.9 %text_grads.1 = f32[256,1280]{1,0:T(8,128)} custom-call(f32[3]{0:T(128)S(1)} %pad_maximum_fusion.s.refs_0_, f32[8,256]{1,0:T(8,128)S(1)} %merge.1.own.refs_1_, f32[8,256]{1,0:T(8,128)S(1)} %sort.1.refs_2_, f32[512,256]{1,0:T(8,128)S(1)} %get-tuple-element.66.l0.refs_3_, f32[512,256]{1,0:T(8,128)S(1)} %get-tuple-element.74.lp.refs_4_, ...), custom_call_target="tpu_custom_call" | custom-call | flops 4485000192 | bytes 1 | tf_op jit(solution)/shard_map/text_grads/pallas_call | solution.py:43
  166.5 1.1 last.1
  (30 shorter events, 1.3 us)
Async XLA Ops:
  0.6 9.1 %collective-permute-start = (f32[256,1280]{1,0:T(8,128)}, f32[256,1280]{1,0:T(8,128)}, u32[]{:S(2)}, u32[]{:S(2)}) collective-permute-start(f32[256,1280]{1,0:T(8,128)} %b0.6), channel_id=1, source_target_pairs={{0,1},{1,0},{2,3},{3,2},{4,5},{5,4},{6,7},{7,6},{8,9},{9,8},{10,11... | collective-permute-start | bytes 3932168 | tf_op jit(solution)/shard_map/ppermute | solution.py:35
  0.7 9.0 %collective-permute-start.1 = (f32[256,1280]{1,0:T(8,128)}, f32[256,1280]{1,0:T(8,128)}, u32[]{:S(2)}, u32[]{:S(2)}) collective-permute-start(f32[256,1280]{1,0:T(8,128)} %b0.7), channel_id=1, source_target_pairs={{0,1},{1,0},{2,3},{3,2},{4,5},{5,4},{6,7},{7,6},{8,9},{9,8},{10,11... | collective-permute-start | bytes 3932168 | tf_op jit(solution)/shard_map/ppermute | solution.py:35
  1.2 35.5 %collective-permute-start.4 = (f32[256,1280]{1,0:T(8,128)}, f32[256,1280]{1,0:T(8,128)S(1)}, u32[]{:S(2)}, u32[]{:S(2)}) collective-permute-start(f32[256,1280]{1,0:T(8,128)} %b0.6), channel_id=1, source_target_pairs={{0,2},{1,3},{2,4},{3,5},{4,6},{5,7},{6,8},{7,9},{8,10},{9,11},{10,... | collective-permute-start | bytes 3932168 | tf_op jit(solution)/shard_map/ppermute | solution.py:24
  3.1 33.6 %collective-permute-start.3 = (f32[256,1280]{1,0:T(8,128)}, f32[256,1280]{1,0:T(8,128)}, u32[]{:S(2)}, u32[]{:S(2)}) collective-permute-start(f32[256,1280]{1,0:T(8,128)} %b0.6), channel_id=1, source_target_pairs={{0,254},{1,255},{2,0},{3,1},{4,2},{5,3},{6,4},{7,5},{8,6},{9,7},{1... | collective-permute-start | bytes 3932168 | tf_op jit(solution)/shard_map/ppermute | solution.py:24
  7.0 57.9 %collective-permute-start.2 = (f32[256,1280]{1,0:T(8,128)}, f32[256,1280]{1,0:T(8,128)S(1)}, u32[]{:S(2)}, u32[]{:S(2)}) collective-permute-start(f32[256,1280]{1,0:T(8,128)} %b0.7), channel_id=1, source_target_pairs={{0,254},{1,255},{2,0},{3,1},{4,2},{5,3},{6,4},{7,5},{8,6},{9,7},{1... | collective-permute-start | bytes 3932168 | tf_op jit(solution)/shard_map/ppermute | solution.py:24
  9.7 55.1 %collective-permute-start.6 = (f32[256,1280]{1,0:T(8,128)}, f32[256,1280]{1,0:T(8,128)S(1)}, u32[]{:S(2)}, u32[]{:S(2)}) collective-permute-start(f32[256,1280]{1,0:T(8,128)} %b0.7), channel_id=1, source_target_pairs={{0,2},{1,3},{2,4},{3,5},{4,6},{5,7},{6,8},{7,9},{8,10},{9,11},{10,... | collective-permute-start | bytes 3932168 | tf_op jit(solution)/shard_map/ppermute | solution.py:24
  9.8 1.3 copy-start
  11.1 1.3 copy-start.1
  12.4 3.7 %copy-start.2 = (f32[256,1280]{1,0:T(8,128)S(1)}, f32[256,1280]{1,0:T(8,128)}, u32[]{:S(2)}) copy-start(f32[256,1280]{1,0:T(8,128)} %b0.7) | copy-start | bytes 3932164
  36.8 55.0 %collective-permute-start.8 = (f32[256,1280]{1,0:T(8,128)}, f32[256,1280]{1,0:T(8,128)S(1)}, u32[]{:S(2)}, u32[]{:S(2)}) collective-permute-start(f32[256,1280]{1,0:T(8,128)} %collective-permute-done.3.bm), channel_id=1, source_target_pairs={{0,254},{1,255},{2,0},{3,1},{4,2},{5,3},{6,4},{7,5},{8,6},{9,7},{1... | collective-permute-start | bytes 3932168 | tf_op jit(solution)/shard_map/ppermute | solution.py:24
  41.0 50.7 %collective-permute-start.9 = (f32[256,1280]{1,0:T(8,128)S(1)}, f32[256,1280]{1,0:T(8,128)S(1)}, u32[]{:S(2)}, u32[]{:S(2)}) collective-permute-start(f32[256,1280]{1,0:T(8,128)S(1)} %collective-permute-done.4.bp), channel_id=1, source_target_pairs={{1,3},{3,5},{5,7},{7,9},{9,11},{11,13},{13,15},{15,17},{17,19},{19... | collective-permute-start | bytes 3932168 | tf_op jit(solution)/shard_map/ppermute | solution.py:24
  64.8 33.8 %collective-permute-start.7 = (f32[256,1280]{1,0:T(8,128)S(1)}, f32[256,1280]{1,0:T(8,128)S(1)}, u32[]{:S(2)}, u32[]{:S(2)}) collective-permute-start(f32[256,1280]{1,0:T(8,128)S(1)} %collective-permute-done.6.bp), channel_id=1, source_target_pairs={{0,2},{1,3},{2,4},{3,5},{4,6},{5,7},{6,8},{7,9},{8,10},{9,11},{10,... | collective-permute-start | bytes 3932168 | tf_op jit(solution)/shard_map/ppermute | solution.py:24
  64.8 40.9 %collective-permute-start.5 = (f32[256,1280]{1,0:T(8,128)S(1)}, f32[256,1280]{1,0:T(8,128)S(1)}, u32[]{:S(2)}, u32[]{:S(2)}) collective-permute-start(f32[256,1280]{1,0:T(8,128)S(1)} %collective-permute-done.2.bm), channel_id=1, source_target_pairs={{0,254},{2,0},{4,2},{6,4},{8,6},{10,8},{12,10},{14,12},{16,14},{18... | collective-permute-start | bytes 3932168 | tf_op jit(solution)/shard_map/ppermute | solution.py:24
  107.9 3.7 %collective-permute-start.10 = (f32[16,256]{1,0:T(8,128)S(1)}, f32[16,256]{1,0:T(8,128)S(1)}, u32[]{:S(2)}, u32[]{:S(2)}) collective-permute-start(f32[16,256]{1,0:T(8,128)S(1)} %get-tuple-element.92.mine), channel_id=1, source_target_pairs={{0,1},{1,0},{2,3},{3,2},{4,5},{5,4},{6,7},{7,6},{8,9},{9,8},{10,11... | collective-permute-start | bytes 49160 | tf_op jit(solution)/shard_map/ppermute | solution.py:35
  112.2 14.0 %collective-permute-start.11 = (f32[8,256]{1,0:T(8,128)S(1)}, f32[8,256]{1,0:T(8,128)S(1)}, u32[]{:S(2)}, u32[]{:S(2)}) collective-permute-start(f32[8,256]{1,0:T(8,128)S(1)} %merge.1.own.refs_1_), channel_id=1, source_target_pairs={{0,2},{1,3},{2,0},{3,1},{4,6},{5,7},{6,4},{7,5},{8,10},{9,11},{10,... | collective-permute-start | bytes 24584 | tf_op jit(solution)/shard_map/ppermute | solution.py:35
  112.3 16.0 %collective-permute-start.15 = (f32[8,256]{1,0:T(8,128)S(1)}, f32[8,256]{1,0:T(8,128)S(1)}, u32[]{:S(2)}, u32[]{:S(2)}) collective-permute-start(f32[8,256]{1,0:T(8,128)S(1)} %merge.1.own.refs_1_), channel_id=1, source_target_pairs={{0,2},{1,5},{2,4},{3,7},{4,6},{5,9},{6,8},{7,11},{8,10},{9,13},{10... | collective-permute-start | bytes 24584 | tf_op jit(solution)/shard_map/ppermute | solution.py:30
  114.3 14.0 %collective-permute-start.13 = (f32[8,256]{1,0:T(8,128)S(1)}, f32[8,256]{1,0:T(8,128)S(1)}, u32[]{:S(2)}, u32[]{:S(2)}) collective-permute-start(f32[8,256]{1,0:T(8,128)S(1)} %merge.1.own.refs_1_), channel_id=1, source_target_pairs={{0,254},{1,253},{2,0},{3,255},{4,2},{5,1},{6,4},{7,3},{8,6},{9,5},... | collective-permute-start | bytes 24584 | tf_op jit(solution)/shard_map/ppermute | solution.py:30
  126.8 4.6 %collective-permute-start.12 = (f32[8,128]{1,0:T(8,128)S(1)}, f32[8,128]{1,0:T(8,128)S(1)}, u32[]{:S(2)}, u32[]{:S(2)}) collective-permute-start(f32[8,128]{1,0:T(8,128)S(1)} %pair.1.refs_0_), channel_id=1, source_target_pairs={{0,4},{1,5},{2,6},{3,7},{4,0},{5,1},{6,2},{7,3},{8,12},{9,13},{10,... | collective-permute-start | bytes 12296 | tf_op jit(solution)/shard_map/ppermute | solution.py:35
  128.2 7.3 %collective-permute-start.16 = (f32[8,256]{1,0:T(8,128)S(1)}, f32[8,256]{1,0:T(8,128)S(1)}, u32[]{:S(2)}, u32[]{:S(2)}) collective-permute-start(f32[8,256]{1,0:T(8,128)S(1)} %collective-permute-done.15.u), channel_id=1, source_target_pairs={{0,1},{1,0},{2,3},{3,2},{4,5},{5,4},{6,7},{7,6},{8,9},{9,8},{10,11... | collective-permute-start | bytes 24584 | tf_op jit(solution)/shard_map/ppermute | solution.py:35
  128.3 7.3 %collective-permute-start.14 = (f32[8,256]{1,0:T(8,128)S(1)}, f32[8,256]{1,0:T(8,128)S(1)}, u32[]{:S(2)}, u32[]{:S(2)}) collective-permute-start(f32[8,256]{1,0:T(8,128)S(1)} %collective-permute-done.13.v), channel_id=1, source_target_pairs={{0,1},{1,0},{2,3},{3,2},{4,5},{5,4},{6,7},{7,6},{8,9},{9,8},{10,11... | collective-permute-start | bytes 24584 | tf_op jit(solution)/shard_map/ppermute | solution.py:35
  131.9 7.6 %collective-permute-start.17 = (f32[8,128]{1,0:T(8,128)S(1)}, f32[8,128]{1,0:T(8,128)S(1)}, u32[]{:S(2)}, u32[]{:S(2)}) collective-permute-start(f32[8,128]{1,0:T(8,128)S(1)} %sum.4.refs_0_), channel_id=1, source_target_pairs={{0,8},{1,9},{2,10},{3,11},{4,12},{5,13},{6,14},{7,15},{8,0},{9,1},... | collective-permute-start | bytes 12296 | tf_op jit(solution)/shard_map/ppermute | solution.py:35
  140.1 11.6 %collective-permute-start.21 = (f32[256,1280]{1,0:T(8,128)S(1)}, f32[256,1280]{1,0:T(8,128)S(1)}, u32[]{:S(2)}, u32[]{:S(2)}) collective-permute-start(f32[256,1280]{1,0:T(8,128)S(1)} %image_share.1), channel_id=1, source_target_pairs={{0,1},{1,0},{2,3},{3,2},{4,5},{5,4},{6,7},{7,6},{8,9},{9,8},{10,11... | collective-permute-start | bytes 3932168 | tf_op jit(solution)/shard_map/ppermute | solution.py:35
  140.2 7.3 %collective-permute-start.20 = (f32[8,128]{1,0:T(8,128)S(1)}, f32[8,128]{1,0:T(8,128)S(1)}, u32[]{:S(2)}, u32[]{:S(2)}) collective-permute-start(f32[8,128]{1,0:T(8,128)S(1)} %sum.5.refs_0_), channel_id=1, source_target_pairs={{0,192},{1,193},{2,194},{3,195},{4,196},{5,197},{6,198},{7,199},{8... | collective-permute-start | bytes 12296 | tf_op jit(solution)/shard_map/ppermute | solution.py:35
  143.1 5.1 %collective-permute-start.19 = (f32[8,128]{1,0:T(8,128)S(1)}, f32[8,128]{1,0:T(8,128)S(1)}, u32[]{:S(2)}, u32[]{:S(2)}) collective-permute-start(f32[8,128]{1,0:T(8,128)S(1)} %sum.5.refs_0_), channel_id=1, source_target_pairs={{0,128},{1,129},{2,130},{3,131},{4,132},{5,133},{6,134},{7,135},{8... | collective-permute-start | bytes 12296 | tf_op jit(solution)/shard_map/ppermute | solution.py:35
  143.9 4.3 %collective-permute-start.18 = (f32[8,128]{1,0:T(8,128)S(1)}, f32[8,128]{1,0:T(8,128)S(1)}, u32[]{:S(2)}, u32[]{:S(2)}) collective-permute-start(f32[8,128]{1,0:T(8,128)S(1)} %sum.5.refs_0_), channel_id=1, source_target_pairs={{0,64},{1,65},{2,66},{3,67},{4,68},{5,69},{6,70},{7,71},{8,72},{9,... | collective-permute-start | bytes 12296 | tf_op jit(solution)/shard_map/ppermute | solution.py:35
  148.7 13.8 %collective-permute-start.23 = (f32[256,1280]{1,0:T(8,128)S(1)}, f32[256,1280]{1,0:T(8,128)S(1)}, u32[]{:S(2)}, u32[]{:S(2)}) collective-permute-start(f32[256,1280]{1,0:T(8,128)S(1)} %text_share.1), channel_id=1, source_target_pairs={{0,1},{1,0},{2,3},{3,2},{4,5},{5,4},{6,7},{7,6},{8,9},{9,8},{10,11... | collective-permute-start | bytes 3932168 | tf_op jit(solution)/shard_map/ppermute | solution.py:35
  148.8 6.9 %collective-permute-start.22 = (f32[8,128]{1,0:T(8,128)S(1)}, f32[8,128]{1,0:T(8,128)S(1)}, u32[]{:S(2)}, u32[]{:S(2)}) collective-permute-start(f32[8,128]{1,0:T(8,128)S(1)} %sum.6.refs_0_), channel_id=1, source_target_pairs={{0,32},{1,33},{2,34},{3,35},{4,36},{5,37},{6,38},{7,39},{8,40},{9,... | collective-permute-start | bytes 12296 | tf_op jit(solution)/shard_map/ppermute | solution.py:35
  156.3 10.2 %collective-permute-start.24 = (f32[8,128]{1,0:T(8,128)S(1)}, f32[8,128]{1,0:T(8,128)S(1)}, u32[]{:S(2)}, u32[]{:S(2)}) collective-permute-start(f32[8,128]{1,0:T(8,128)S(1)} %sum.7.refs_0_), channel_id=1, source_target_pairs={{0,16},{1,17},{2,18},{3,19},{4,20},{5,21},{6,22},{7,23},{8,24},{9,... | collective-permute-start | bytes 12296 | tf_op jit(solution)/shard_map/ppermute | solution.py:35

commit v5 on v4

--- a/solution.py
+++ b/solution.py
@@ -131,7 +131,7 @@
 
 def near_kernel(s, h, m, l, b0, bm, bp, lp, lm, blocks_h, blocks_l, *parts):
     n = b0.shape[0]
-    r = pl.ds(n, n)
+    r = pl.ds(0, n)
     blocks_h[r], blocks_l[r] = two(b0[...])
     for k, (block, out) in enumerate(((bp, lp), (bm, lm))):
         put_three(block[...], *parts)
@@ -153,7 +153,7 @@
 def put_far(s, parts, k, block, lf, blocks_h, blocks_l, split):
     n = block.shape[0]
     put_three(block, *split)
-    r = pl.ds(4 * k * n, n)
+    r = pl.ds((1 + 3 * k) * n, n)
     blocks_h[r], blocks_l[r] = split[0][...], split[1][...]
     r = pl.ds(k * n, n)
     lf[r, :] = s[0] * scores(take(parts, r), take(split))
@@ -256,8 +256,8 @@
     return jnp.where(i == j, w - 2.0, w)
 
 
-def put_weights(text, sib, s, own, lses, l0, lp, lm, lf, wh, wl):
-    n = l0.shape[1]
+def put_weights(text, sib, s, own, lses, lp, lm, lf, wh, wl):
+    n = lp.shape[1]
     first = s[1] == 0.0
     rows = pl.ds(n if sib else 0, n)
     k = (2 if sib else 0) + (1 if text else 0)
@@ -268,12 +268,10 @@
         far = jnp.where(first, ahead, behind)
     else:
         far = behind if text else ahead
-    near = [(l0, own[k : k + 1, :]), (lp, m2), (lm, p2)]
+    near = [(lp, m2), (lm, p2)]
     pieces = near + [(lf, far)] if sib else [(lf, far)] + near
     for k, (v, m) in enumerate(pieces):
         w = weigh(v[rows, :], side, m)
-        if v is l0 and not sib:
-            w = less_twice_eye(w)
         at = pl.ds(k * n, n)
         wh[:, at], wl[:, at] = two(w)
 
@@ -283,25 +281,39 @@
     return (dot_nn(h, bl[rows, d]) + dot_nn(l, bh[rows, d])) + dot_nn(h, bh[rows, d])
 
 
+def own_blocks_kernel(s, own, l0, v0, th, tl, ih, il, image_out, text_out, wh, wl):
+    n = l0.shape[1]
+    for text, x, bh, bl, out in ((0, l0, th, tl, image_out), (1, v0, ih, il, text_out)):
+        side = jnp.concatenate(
+            [column(own[text : text + 1, :]), column(own[text + 2 : text + 3, :])]
+        )
+        w = weigh(x[...], side, own[1 - text : 2 - text, :])
+        wh[...], wl[...] = two(less_twice_eye(w))
+        for k in range(out.shape[1] // TILE):
+            d = pl.ds(k * TILE, TILE)
+            out[:, d] = tile_grads(wh, wl, bh, bl, pl.ds(0, n), d)
+
+
 def share_kernel(text, *refs):
-    *args, bh, bl, out, wh, wl = refs
+    *args, bh, bl, first, out, wh, wl = refs
     put_weights(text, True, *args, wh, wl)
     n = out.shape[0]
     for k in range(out.shape[1] // TILE):
         d = pl.ds(k * TILE, TILE)
-        out[:, d] = tile_grads(wh, wl, bh, bl, pl.ds(n, 4 * n), d)
+        total = tile_grads(wh, wl, bh, bl, pl.ds(2 * n, 3 * n), d)
+        out[:, d] = total + first[n:, d]
 
 
 def grads_kernel(text, *refs):
-    *args, bh, bl, share, out, wh, wl, done, sem = refs
+    *args, bh, bl, first, share, out, wh, wl, done, sem = refs
     put_weights(text, False, *args, wh, wl)
     n = share.shape[0]
     factor = 0.5 * args[0][0]
     copies = []
     for k in range(out.shape[1] // TILE):
         d = pl.ds(k * TILE, TILE)
-        total = tile_grads(wh, wl, bh, bl, pl.ds(0, 4 * n), d) + share[:, d]
-        done[:, d] = factor * total
+        total = tile_grads(wh, wl, bh, bl, pl.ds(n, 3 * n), d)
+        done[:, d] = factor * ((total + first[0:n, d]) + share[:, d])
         copies.append(pltpu.make_async_copy(done.at[:, d], out.at[:, d], sem.at[k]))
         copies[-1].start()
     for copy in copies:
@@ -364,16 +376,20 @@
         return call(sum_kernel, "sum", 0.5, terms, args)[0]
 
     parts = add(parts, (4,))
-    args = s, after(own, parts), v, swap(v), u, swap(u)
+    args = s, own, l0, v0, *t_parts, *i_parts
+    firsts = [((2 * n, depth), F32)] * 2
+    w_part = [((2 * n, n), BF16)] * 2
+    image_first, text_first = call(own_blocks_kernel, "own_blocks", 3.0, firsts, args, w_part)
+    args = s, after(own, parts), v, swap(after(v, image_first)), u, swap(u)
     (lses,) = call(sort_kernel, "sort", 0.5, [((8, n), F32)], args)
 
-    image_args = l0, lp, lm, lf, *t_parts
-    text_args = v0, vp, vm, vf, *i_parts
-    weights = [((n, 4 * n), BF16)] * 2
+    image_args = lp, lm, lf, *t_parts, image_first
+    text_args = vp, vm, vf, *i_parts, text_first
+    weights = [((n, 3 * n), BF16)] * 2
     final = [block, pltpu.SemaphoreType.DMA((depth // TILE,))]
     kernel = functools.partial(share_kernel, False)
     (share,) = call(kernel, "image_share", 3.1, [block], (s, own, lses, *image_args), weights)
-    parts = add(parts, (8,), share)
+    parts = add(parts, (16,), share)
     image_share = swap(after(share, parts))
     kernel = functools.partial(share_kernel, True)
     args = s, after(own, parts), lses, *text_args
@@ -381,14 +397,14 @@
     parts = add(parts, (64, 128, 192), share)
     text_share = swap(after(share, parts))
 
-    y_part = swap(parts, 32)
+    far_part = swap(parts, 8)
     kernel = functools.partial(grads_kernel, False)
     args = s, after(own, parts), lses, *image_args, image_share
     final = weights + final
     (image_grad,) = call(kernel, "image_grads", 3.9, [block], args, final, out_hbm=(0,))
-    args = s, after(parts, image_grad), y_part
+    args = s, after(parts, image_grad), far_part
     (parts,) = call(sum_kernel, "sum", 0.5, terms, args)
-    y_part = swap(parts, 16)
+    y_part = swap(parts, 32)
     kernel = functools.partial(grads_kernel, True)
     args = s, after(own, parts), lses, *text_args, text_share
     (text_grad,) = call(kernel, "text_grads", 3.9, [block], args, final, out_hbm=(0,))

time: 170 us -> 168 us (0.988)
  starting transfers between devices: 55.6 us -> 49.1 us
  waiting for transfers between devices: 58.9 us -> 61 us
    ppermute x15, starting transfers between devices: 22.5 us -> 18.3 us  [swap(): return lax.ppermute(value, 'dp', [(s, s ^ bit) for s in range(count)])]
    ppermute x2, starting transfers between devices: 14 us -> 11.6 us  [along(): return lax.ppermute(value, 'dp', pairs)]
    ppermute x15, waiting for transfers between devices: 4.5 us -> 6.6 us  [swap(): return lax.ppermute(value, 'dp', [(s, s ^ bit) for s in range(count)])]
    pallas_call x21 -> x22, Pallas kernels: 48.9 us -> 49.6 us  [call(): pl.pallas_call(kernel, name=name, out_shape=[jax.ShapeDtypeStruct(s, d) f...]
  transfers between devices with their start and end apart: 25 -> 25, of which waited for: 9 -> 8; matrix products, arithmetic and copies ran while one was open for 0% -> 0% of each run, Pallas kernels for 26% -> 27%
where the time goes in v5:
time: 168 us; the launch traced here: 164 us
  waiting for transfers between devices  61 us (36%)
  Pallas kernels  49.6 us (30%)
  starting transfers between devices  49.1 us (29%)
  local copies, waits for them, and re-layouts  2.63 us (2%)
  between operations  1.82 us (1%)
    ppermute x8, waiting for transfers between devices, shift(): return lax.ppermute(value, 'dp', pairs)  54.4 us
    pallas_call x22, Pallas kernels, call(): pl.pallas_call(kernel, name=name, out_shape=[jax.ShapeDtypeStruct(s, d) f...  49.6 us
    ppermute x8, starting transfers between devices, shift(): return lax.ppermute(value, 'dp', pairs)  19.1 us
    ppermute x15, starting transfers between devices, swap(): return lax.ppermute(value, 'dp', [(s, s ^ bit) for s in range(count)])  18.3 us
    ppermute x2, starting transfers between devices, along(): return lax.ppermute(value, 'dp', pairs)  11.6 us
    ppermute x15, waiting for transfers between devices, swap(): return lax.ppermute(value, 'dp', [(s, s ^ bit) for s in range(count)])  6.6 us
  transfers between devices with their start and end apart: 25, of which 8 were waited for; matrix products, arithmetic and copies ran while one was open for 0% of the time, Pallas kernels for 27%

profile of v5, /device:TPU:8, one launch (start us, length us, event | category | flops | bytes accessed | tf_op | source)
XLA Modules:
  0.0 164.3 jit_solution(11071488665537756798)
XLA Ops:
  0.7 0.5 collective-permute-start.1
  1.2 1.9 %collective-permute-start.4 = (f32[256,1280]{1,0:T(8,128)}, f32[256,1280]{1,0:T(8,128)S(1)}, u32[]{:S(2)}, u32[]{:S(2)}) collective-permute-start(f32[256,1280]{1,0:T(8,128)} %b0.6), channel_id=1, source_target_pairs={{0,2},{1,3},{2,4},{3,5},{4,6},{5,7},{6,8},{7,9},{8,10},{9,11},{10,... | collective-permute-start | bytes 3932168 | tf_op jit(solution)/shard_map/ppermute | solution.py:24
  3.1 3.8 %collective-permute-start.3 = (f32[256,1280]{1,0:T(8,128)}, f32[256,1280]{1,0:T(8,128)}, u32[]{:S(2)}, u32[]{:S(2)}) collective-permute-start(f32[256,1280]{1,0:T(8,128)} %b0.6), channel_id=1, source_target_pairs={{0,254},{1,255},{2,0},{3,1},{4,2},{5,3},{6,4},{7,5},{8,6},{9,7},{1... | collective-permute-start | bytes 3932168 | tf_op jit(solution)/shard_map/ppermute | solution.py:24
  7.0 2.0 %collective-permute-start.2 = (f32[256,1280]{1,0:T(8,128)}, f32[256,1280]{1,0:T(8,128)S(1)}, u32[]{:S(2)}, u32[]{:S(2)}) collective-permute-start(f32[256,1280]{1,0:T(8,128)} %b0.7), channel_id=1, source_target_pairs={{0,254},{1,255},{2,0},{3,1},{4,2},{5,3},{6,4},{7,5},{8,6},{9,7},{1... | collective-permute-start | bytes 3932168 | tf_op jit(solution)/shard_map/ppermute | solution.py:24
  9.8 1.3 copy-done
  11.1 1.3 copy-done.1
  12.4 3.7 %text_own.1 = (bf16[512,1280]{1,0:T(8,128)(2,1)S(1)}, bf16[512,1280]{1,0:T(8,128)(2,1)S(1)}, bf16[512,1280]{1,0:T(8,128)(2,1)S(1)}, f32[512,256]{1,0:T(8,128)S(1)}) custom-call(f32[3]{0:T(128)S(1)} %pad_maximum_fusion.s.refs_0_, f32[256,1280]{1,0:T(8,128)S(1)} %copy-done.1, f32[256,1280]{1,0:T(8,128)} %collective-permute-done.1.a1, f32[256,1280]{1,0:T(8,128)S(1)} %copy-done), custom_call_target="tpu_custom_call" | custom-call | flops 4255000064 | bytes 1 | tf_op jit(solution)/shard_map/text_own/pallas_call | solution.py:43
  16.1 3.6 %image_own.1 = (bf16[512,1280]{1,0:T(8,128)(2,1)S(1)}, bf16[512,1280]{1,0:T(8,128)(2,1)S(1)}, bf16[512,1280]{1,0:T(8,128)(2,1)S(1)}, f32[512,256]{1,0:T(8,128)S(1)}) custom-call(f32[3]{0:T(128)S(1)} %pad_maximum_fusion.s.refs_0_, f32[256,1280]{1,0:T(8,128)S(1)} %copy-done, f32[256,1280]{1,0:T(8,128)} %collective-permute-done.a1, f32[256,1280]{1,0:T(8,128)S(1)} %copy-done.2), custom_call_target="tpu_custom_call" | custom-call | flops 4255000064 | bytes 1 | tf_op jit(solution)/shard_map/image_own/pallas_call | solution.py:43
  19.7 17.0 %collective-permute-done.4.bp = f32[256,1280]{1,0:T(8,128)S(1)} collective-permute-done((f32[256,1280]{1,0:T(8,128)}, f32[256,1280]{1,0:T(8,128)S(1)}, u32[]{:S(2)}, u32[]{:S(2)}) %collective-permute-start.4) | collective-permute-done | bytes 1310752 | tf_op jit(solution)/shard_map/ppermute | solution.py:24
  36.8 4.3 %collective-permute-start.8 = (f32[256,1280]{1,0:T(8,128)}, f32[256,1280]{1,0:T(8,128)S(1)}, u32[]{:S(2)}, u32[]{:S(2)}) collective-permute-start(f32[256,1280]{1,0:T(8,128)} %collective-permute-done.3.bm), channel_id=1, source_target_pairs={{0,254},{1,255},{2,0},{3,1},{4,2},{5,3},{6,4},{7,5},{8,6},{9,7},{1... | collective-permute-start | bytes 3932168 | tf_op jit(solution)/shard_map/ppermute | solution.py:24
  41.0 1.0 collective-permute-start.9
  42.0 6.0 %text_near.1 = (f32[512,256]{1,0:T(8,128)S(1)}, f32[512,256]{1,0:T(8,128)S(1)}, bf16[1280,1280]{1,0:T(8,128)(2,1)S(1)}, bf16[1280,1280]{1,0:T(8,128)(2,1)S(1)}) custom-call(f32[3]{0:T(128)S(1)} %pad_maximum_fusion.s.refs_0_, bf16[512,1280]{1,0:T(8,128)(2,1)S(1)} %get-tuple-element.66.h.xh, bf16[512,1280]{1,0:T(8,128)(2,1)S(1)} %get-tuple-element.67.m.xm, ...), custom_call_target="tpu_custom_call" | custom-call | flops 5520000000 | bytes 1 | tf_op jit(solution)/shard_map/text_near/pallas_call | solution.py:43
  48.0 1.3 text_stats.1
  49.3 15.5 %collective-permute-done.6.bp = f32[256,1280]{1,0:T(8,128)S(1)} collective-permute-done((f32[256,1280]{1,0:T(8,128)}, f32[256,1280]{1,0:T(8,128)S(1)}, u32[]{:S(2)}, u32[]{:S(2)}) %collective-permute-start.6) | collective-permute-done | bytes 1310752 | tf_op jit(solution)/shard_map/ppermute | solution.py:24
  64.8 6.1 %collective-permute-start.5 = (f32[256,1280]{1,0:T(8,128)S(1)}, f32[256,1280]{1,0:T(8,128)S(1)}, u32[]{:S(2)}, u32[]{:S(2)}) collective-permute-start(f32[256,1280]{1,0:T(8,128)S(1)} %collective-permute-done.2.bm), channel_id=1, source_target_pairs={{0,254},{2,0},{4,2},{6,4},{8,6},{10,8},{12,10},{14,12},{16,14},{18... | collective-permute-start | bytes 3932168 | tf_op jit(solution)/shard_map/ppermute | solution.py:24
  70.9 5.2 %image_near.1 = (f32[512,256]{1,0:T(8,128)S(1)}, f32[512,256]{1,0:T(8,128)S(1)}, bf16[1280,1280]{1,0:T(8,128)(2,1)S(1)}, bf16[1280,1280]{1,0:T(8,128)(2,1)S(1)}) custom-call(f32[3]{0:T(128)S(1)} %pad_maximum_fusion.s.refs_0_, bf16[512,1280]{1,0:T(8,128)(2,1)S(1)} %get-tuple-element.63.h.yh, bf16[512,1280]{1,0:T(8,128)(2,1)S(1)} %get-tuple-element.64.m.ym, ...), custom_call_target="tpu_custom_call" | custom-call | flops 5520000000 | bytes 1 | tf_op jit(solution)/shard_map/image_near/pallas_call | solution.py:43
  76.2 1.9 %image_stats.1 = (f32[512,128]{1,0:T(8,128)S(1)}, f32[512,128]{1,0:T(8,128)S(1)}, f32[1,256]{1,0:T(1,128)}) custom-call(f32[3]{0:T(128)S(1)} %pad_maximum_fusion.s.refs_0_, f32[512,256]{1,0:T(8,128)S(1)} %get-tuple-element.69.l0.v0, f32[512,256]{1,0:T(8,128)S(1)} %get-tuple-element.77.lp.refs_3_, f32[512,256]{1,0:T(8,128)S(1)} %get-tuple-element.78.lm.refs_4_), custom_call_target="tpu_custom_call" | custom-call | flops 2070000000 | bytes 1 | tf_op jit(solution)/shard_map/image_stats/pallas_call | solution.py:43
  78.0 13.7 %collective-permute-done.8.a = f32[256,1280]{1,0:T(8,128)S(1)} collective-permute-done((f32[256,1280]{1,0:T(8,128)}, f32[256,1280]{1,0:T(8,128)S(1)}, u32[]{:S(2)}, u32[]{:S(2)}) %collective-permute-start.8) | collective-permute-done | bytes 1310752 | tf_op jit(solution)/shard_map/ppermute | solution.py:24
  91.8 3.6 %text_far.1 = (f32[512,256]{1,0:T(8,128)S(1)}, f32[4,256]{1,0:T(4,128)S(1)}, bf16[1280,1280]{1,0:T(8,128)(2,1)S(1)}, bf16[1280,1280]{1,0:T(8,128)(2,1)S(1)}) custom-call(f32[3]{0:T(128)S(1)} %pad_maximum_fusion.s.refs_0_, bf16[512,1280]{1,0:T(8,128)(2,1)S(1)} %get-tuple-element.66.h.xh, ...), custom_call_target="tpu_custom_call", output_to_operand_aliasing={{2}: (8, {}), {3}: (9, {})} | custom-call | flops 4600000000 | bytes 1 | tf_op jit(solution)/shard_map/text_far/pallas_call | solution.py:43
  95.4 3.3 %collective-permute-done.7.block = f32[256,1280]{1,0:T(8,128)S(1)} collective-permute-done((f32[256,1280]{1,0:T(8,128)S(1)}, f32[256,1280]{1,0:T(8,128)S(1)}, u32[]{:S(2)}, u32[]{:S(2)}) %collective-permute-start.7) | collective-permute-done | bytes 1310752 | tf_op jit(solution)/shard_map/ppermute | solution.py:24
  98.7 2.2 %image_behind.1 = (f32[512,256]{1,0:T(8,128)S(1)}, f32[16,256]{1,0:T(8,128)S(1)}, bf16[1280,1280]{1,0:T(8,128)(2,1)S(1)}, bf16[1280,1280]{1,0:T(8,128)(2,1)S(1)}) custom-call(f32[3]{0:T(128)S(1)} %pad_maximum_fusion.s.refs_0_, bf16[512,1280]{1,0:T(8,128)(2,1)S(1)} %get-tuple-element.63.h.yh, ...), custom_call_target="tpu_custom_call", output_to_operand_aliasing={{2}: (7, {}), {3}: (8, {})} | custom-call | flops 3449999872 | bytes 1 | tf_op jit(solution)/shard_map/image_behind/pallas_call | solution.py:43
  100.8 4.9 %collective-permute-done.5.block = f32[256,1280]{1,0:T(8,128)S(1)} collective-permute-done((f32[256,1280]{1,0:T(8,128)S(1)}, f32[256,1280]{1,0:T(8,128)S(1)}, u32[]{:S(2)}, u32[]{:S(2)}) %collective-permute-start.5) | collective-permute-done | bytes 1310752 | tf_op jit(solution)/shard_map/ppermute | solution.py:24
  105.7 2.2 %image_ahead.1 = (f32[512,256]{1,0:T(8,128)S(1)}, f32[16,256]{1,0:T(8,128)S(1)}, bf16[1280,1280]{1,0:T(8,128)(2,1)S(1)}, bf16[1280,1280]{1,0:T(8,128)(2,1)S(1)}) custom-call(f32[3]{0:T(128)S(1)} %pad_maximum_fusion.s.refs_0_, bf16[512,1280]{1,0:T(8,128)(2,1)S(1)} %get-tuple-element.63.h.yh, ...), custom_call_target="tpu_custom_call", output_to_operand_aliasing={{2}: (7, {}), {3}: (8, {}), {0}: (9, {}), {1}: (10, {})} | custom-call | flops 2300000000 | bytes 1 | tf_op jit(solution)/shard_map/image_ahead/pallas_call | solution.py:43
  107.9 2.8 %collective-permute-start.10 = (f32[16,256]{1,0:T(8,128)S(1)}, f32[16,256]{1,0:T(8,128)S(1)}, u32[]{:S(2)}, u32[]{:S(2)}) collective-permute-start(f32[16,256]{1,0:T(8,128)S(1)} %get-tuple-element.95.mine), channel_id=1, source_target_pairs={{0,1},{1,0},{2,3},{3,2},{4,5},{5,4},{6,7},{7,6},{8,9},{9,8},{10,11... | collective-permute-start | bytes 49160 | tf_op jit(solution)/shard_map/ppermute | solution.py:35
  110.8 0.8 collective-permute-done.10.got
  111.6 0.6 merge.1.own.refs_1_
  112.3 2.0 %collective-permute-start.15 = (f32[8,256]{1,0:T(8,128)S(1)}, f32[8,256]{1,0:T(8,128)S(1)}, u32[]{:S(2)}, u32[]{:S(2)}) collective-permute-start(f32[8,256]{1,0:T(8,128)S(1)} %merge.1.own.refs_1_), channel_id=1, source_target_pairs={{0,2},{1,5},{2,4},{3,7},{4,6},{5,9},{6,8},{7,11},{8,10},{9,13},{10... | collective-permute-start | bytes 24584 | tf_op jit(solution)/shard_map/ppermute | solution.py:30
  114.3 9.6 %collective-permute-start.13 = (f32[8,256]{1,0:T(8,128)S(1)}, f32[8,256]{1,0:T(8,128)S(1)}, u32[]{:S(2)}, u32[]{:S(2)}) collective-permute-start(f32[8,256]{1,0:T(8,128)S(1)} %merge.1.own.refs_1_), channel_id=1, source_target_pairs={{0,254},{1,253},{2,0},{3,255},{4,2},{5,1},{6,4},{7,3},{8,6},{9,5},... | collective-permute-start | bytes 24584 | tf_op jit(solution)/shard_map/ppermute | solution.py:30
  123.9 0.5 pair.1.refs_0_
  124.5 1.4 collective-permute-start.12
  125.9 3.1 %own_blocks.1 = (f32[512,1280]{1,0:T(8,128)S(1)}, f32[512,1280]{1,0:T(8,128)S(1)}) custom-call(f32[3]{0:T(128)S(1)} %pad_maximum_fusion.s.refs_0_, f32[8,256]{1,0:T(8,128)S(1)} %merge.1.own.refs_1_, f32[512,256]{1,0:T(8,128)S(1)} %get-tuple-element.61.l0, f32[512,256]{1,0:T(8,128)S(1)} %get-tuple-element.69.l0.v0, ...), custom_call_target="tpu_custom_call" | custom-call | flops 3449999872 | bytes 1 | tf_op jit(solution)/shard_map/own_blocks/pallas_call | solution.py:43
  129.1 0.5 collective-permute-start.16
  129.6 0.5 sum.4.refs_0_
  130.2 8.1 %collective-permute-start.17 = (f32[8,128]{1,0:T(8,128)S(1)}, f32[8,128]{1,0:T(8,128)S(1)}, u32[]{:S(2)}, u32[]{:S(2)}) collective-permute-start(f32[8,128]{1,0:T(8,128)S(1)} %sum.4.refs_0_), channel_id=1, source_target_pairs={{0,16},{1,17},{2,18},{3,19},{4,20},{5,21},{6,22},{7,23},{8,24},{9,... | collective-permute-start | bytes 12296 | tf_op jit(solution)/shard_map/ppermute | solution.py:35
  138.2 0.6 sort.1.refs_2_
  138.8 2.5 %image_share.1 = f32[256,1280]{1,0:T(8,128)S(1)} custom-call(f32[3]{0:T(128)S(1)} %pad_maximum_fusion.s.refs_0_, f32[8,256]{1,0:T(8,128)S(1)} %merge.1.own.refs_1_, f32[8,256]{1,0:T(8,128)S(1)} %sort.1.refs_2_, f32[512,256]{1,0:T(8,128)S(1)} %get-tuple-element.72.lp.refs_3_, f32[512,256]{1,0:T(8,128)S(1)} %get-tuple-element.73.lm.refs_4_, ...), custom_call_target="tpu_custom_call" | custom-call | flops 3564999936 | bytes 1 | tf_op jit(solution)/shard_map/image_share/pallas_call | solution.py:43
  141.3 0.5 sum.5.refs_0_
  142.1 0.1 collective-permute-start.19
  142.2 4.0 %collective-permute-start.18 = (f32[8,128]{1,0:T(8,128)S(1)}, f32[8,128]{1,0:T(8,128)S(1)}, u32[]{:S(2)}, u32[]{:S(2)}) collective-permute-start(f32[8,128]{1,0:T(8,128)S(1)} %sum.5.refs_0_), channel_id=1, source_target_pairs={{0,64},{1,65},{2,66},{3,67},{4,68},{5,69},{6,70},{7,71},{8,72},{9,... | collective-permute-start | bytes 12296 | tf_op jit(solution)/shard_map/ppermute | solution.py:35
  146.1 2.5 %text_share.1 = f32[256,1280]{1,0:T(8,128)S(1)} custom-call(f32[3]{0:T(128)S(1)} %pad_maximum_fusion.s.refs_0_, f32[8,256]{1,0:T(8,128)S(1)} %merge.1.own.refs_1_, f32[8,256]{1,0:T(8,128)S(1)} %sort.1.refs_2_, f32[512,256]{1,0:T(8,128)S(1)} %get-tuple-element.77.lp.refs_3_, f32[512,256]{1,0:T(8,128)S(1)} %get-tuple-element.78.lm.refs_4_, ...), custom_call_target="tpu_custom_call" | custom-call | flops 3564999936 | bytes 1 | tf_op jit(solution)/shard_map/text_share/pallas_call | solution.py:43
  148.7 0.5 sum.6.refs_0_
  149.3 0.3 collective-permute-start.22
  149.7 3.4 %image_grads.1 = f32[256,1280]{1,0:T(8,128)} custom-call(f32[3]{0:T(128)S(1)} %pad_maximum_fusion.s.refs_0_, f32[8,256]{1,0:T(8,128)S(1)} %merge.1.own.refs_1_, f32[8,256]{1,0:T(8,128)S(1)} %sort.1.refs_2_, f32[512,256]{1,0:T(8,128)S(1)} %get-tuple-element.72.lp.refs_3_, f32[512,256]{1,0:T(8,128)S(1)} %get-tuple-element.73.lm.refs_4_, ...), custom_call_target="tpu_custom_call" | custom-call | flops 4485000192 | bytes 1 | tf_op jit(solution)/shard_map/image_grads/pallas_call | solution.py:43
  153.1 4.1 %collective-permute-done.22.refs_1_ = f32[8,128]{1,0:T(8,128)S(1)} collective-permute-done((f32[8,128]{1,0:T(8,128)S(1)}, f32[8,128]{1,0:T(8,128)S(1)}, u32[]{:S(2)}, u32[]{:S(2)}) %collective-permute-start.22) | collective-permute-done | bytes 4128 | tf_op jit(solution)/shard_map/ppermute | solution.py:35
  157.2 0.5 sum.7.refs_0_
  157.8 3.5 %text_grads.1 = f32[256,1280]{1,0:T(8,128)} custom-call(f32[3]{0:T(128)S(1)} %pad_maximum_fusion.s.refs_0_, f32[8,256]{1,0:T(8,128)S(1)} %merge.1.own.refs_1_, f32[8,256]{1,0:T(8,128)S(1)} %sort.1.refs_2_, f32[512,256]{1,0:T(8,128)S(1)} %get-tuple-element.77.lp.refs_3_, f32[512,256]{1,0:T(8,128)S(1)} %get-tuple-element.78.lm.refs_4_, ...), custom_call_target="tpu_custom_call" | custom-call | flops 4485000192 | bytes 1 | tf_op jit(solution)/shard_map/text_grads/pallas_call | solution.py:43
  161.3 1.6 collective-permute-done.24.refs_1_
  162.9 1.1 last.1
  (31 shorter events, 0.8 us)
Async XLA Ops:
  0.6 9.1 %collective-permute-start = (f32[256,1280]{1,0:T(8,128)}, f32[256,1280]{1,0:T(8,128)}, u32[]{:S(2)}, u32[]{:S(2)}) collective-permute-start(f32[256,1280]{1,0:T(8,128)} %b0.6), channel_id=1, source_target_pairs={{0,1},{1,0},{2,3},{3,2},{4,5},{5,4},{6,7},{7,6},{8,9},{9,8},{10,11... | collective-permute-start | bytes 3932168 | tf_op jit(solution)/shard_map/ppermute | solution.py:35
  0.7 9.0 %collective-permute-start.1 = (f32[256,1280]{1,0:T(8,128)}, f32[256,1280]{1,0:T(8,128)}, u32[]{:S(2)}, u32[]{:S(2)}) collective-permute-start(f32[256,1280]{1,0:T(8,128)} %b0.7), channel_id=1, source_target_pairs={{0,1},{1,0},{2,3},{3,2},{4,5},{5,4},{6,7},{7,6},{8,9},{9,8},{10,11... | collective-permute-start | bytes 3932168 | tf_op jit(solution)/shard_map/ppermute | solution.py:35
  1.2 35.5 %collective-permute-start.4 = (f32[256,1280]{1,0:T(8,128)}, f32[256,1280]{1,0:T(8,128)S(1)}, u32[]{:S(2)}, u32[]{:S(2)}) collective-permute-start(f32[256,1280]{1,0:T(8,128)} %b0.6), channel_id=1, source_target_pairs={{0,2},{1,3},{2,4},{3,5},{4,6},{5,7},{6,8},{7,9},{8,10},{9,11},{10,... | collective-permute-start | bytes 3932168 | tf_op jit(solution)/shard_map/ppermute | solution.py:24
  3.1 33.6 %collective-permute-start.3 = (f32[256,1280]{1,0:T(8,128)}, f32[256,1280]{1,0:T(8,128)}, u32[]{:S(2)}, u32[]{:S(2)}) collective-permute-start(f32[256,1280]{1,0:T(8,128)} %b0.6), channel_id=1, source_target_pairs={{0,254},{1,255},{2,0},{3,1},{4,2},{5,3},{6,4},{7,5},{8,6},{9,7},{1... | collective-permute-start | bytes 3932168 | tf_op jit(solution)/shard_map/ppermute | solution.py:24
  7.0 57.9 %collective-permute-start.2 = (f32[256,1280]{1,0:T(8,128)}, f32[256,1280]{1,0:T(8,128)S(1)}, u32[]{:S(2)}, u32[]{:S(2)}) collective-permute-start(f32[256,1280]{1,0:T(8,128)} %b0.7), channel_id=1, source_target_pairs={{0,254},{1,255},{2,0},{3,1},{4,2},{5,3},{6,4},{7,5},{8,6},{9,7},{1... | collective-permute-start | bytes 3932168 | tf_op jit(solution)/shard_map/ppermute | solution.py:24
  9.7 55.1 %collective-permute-start.6 = (f32[256,1280]{1,0:T(8,128)}, f32[256,1280]{1,0:T(8,128)S(1)}, u32[]{:S(2)}, u32[]{:S(2)}) collective-permute-start(f32[256,1280]{1,0:T(8,128)} %b0.7), channel_id=1, source_target_pairs={{0,2},{1,3},{2,4},{3,5},{4,6},{5,7},{6,8},{7,9},{8,10},{9,11},{10,... | collective-permute-start | bytes 3932168 | tf_op jit(solution)/shard_map/ppermute | solution.py:24
  9.8 1.3 copy-start
  11.1 1.3 copy-start.1
  12.4 3.7 %copy-start.2 = (f32[256,1280]{1,0:T(8,128)S(1)}, f32[256,1280]{1,0:T(8,128)}, u32[]{:S(2)}) copy-start(f32[256,1280]{1,0:T(8,128)} %b0.7) | copy-start | bytes 3932164
  36.8 55.0 %collective-permute-start.8 = (f32[256,1280]{1,0:T(8,128)}, f32[256,1280]{1,0:T(8,128)S(1)}, u32[]{:S(2)}, u32[]{:S(2)}) collective-permute-start(f32[256,1280]{1,0:T(8,128)} %collective-permute-done.3.bm), channel_id=1, source_target_pairs={{0,254},{1,255},{2,0},{3,1},{4,2},{5,3},{6,4},{7,5},{8,6},{9,7},{1... | collective-permute-start | bytes 3932168 | tf_op jit(solution)/shard_map/ppermute | solution.py:24
  41.0 50.7 %collective-permute-start.9 = (f32[256,1280]{1,0:T(8,128)S(1)}, f32[256,1280]{1,0:T(8,128)S(1)}, u32[]{:S(2)}, u32[]{:S(2)}) collective-permute-start(f32[256,1280]{1,0:T(8,128)S(1)} %collective-permute-done.4.bp), channel_id=1, source_target_pairs={{1,3},{3,5},{5,7},{7,9},{9,11},{11,13},{13,15},{15,17},{17,19},{19... | collective-permute-start | bytes 3932168 | tf_op jit(solution)/shard_map/ppermute | solution.py:24
  64.8 33.8 %collective-permute-start.7 = (f32[256,1280]{1,0:T(8,128)S(1)}, f32[256,1280]{1,0:T(8,128)S(1)}, u32[]{:S(2)}, u32[]{:S(2)}) collective-permute-start(f32[256,1280]{1,0:T(8,128)S(1)} %collective-permute-done.6.bp), channel_id=1, source_target_pairs={{0,2},{1,3},{2,4},{3,5},{4,6},{5,7},{6,8},{7,9},{8,10},{9,11},{10,... | collective-permute-start | bytes 3932168 | tf_op jit(solution)/shard_map/ppermute | solution.py:24
  64.8 40.9 %collective-permute-start.5 = (f32[256,1280]{1,0:T(8,128)S(1)}, f32[256,1280]{1,0:T(8,128)S(1)}, u32[]{:S(2)}, u32[]{:S(2)}) collective-permute-start(f32[256,1280]{1,0:T(8,128)S(1)} %collective-permute-done.2.bm), channel_id=1, source_target_pairs={{0,254},{2,0},{4,2},{6,4},{8,6},{10,8},{12,10},{14,12},{16,14},{18... | collective-permute-start | bytes 3932168 | tf_op jit(solution)/shard_map/ppermute | solution.py:24
  107.9 3.7 %collective-permute-start.10 = (f32[16,256]{1,0:T(8,128)S(1)}, f32[16,256]{1,0:T(8,128)S(1)}, u32[]{:S(2)}, u32[]{:S(2)}) collective-permute-start(f32[16,256]{1,0:T(8,128)S(1)} %get-tuple-element.95.mine), channel_id=1, source_target_pairs={{0,1},{1,0},{2,3},{3,2},{4,5},{5,4},{6,7},{7,6},{8,9},{9,8},{10,11... | collective-permute-start | bytes 49160 | tf_op jit(solution)/shard_map/ppermute | solution.py:35
  112.3 11.7 %collective-permute-start.11 = (f32[8,256]{1,0:T(8,128)S(1)}, f32[8,256]{1,0:T(8,128)S(1)}, u32[]{:S(2)}, u32[]{:S(2)}) collective-permute-start(f32[8,256]{1,0:T(8,128)S(1)} %merge.1.own.refs_1_), channel_id=1, source_target_pairs={{0,2},{1,3},{2,0},{3,1},{4,6},{5,7},{6,4},{7,5},{8,10},{9,11},{10,... | collective-permute-start | bytes 24584 | tf_op jit(solution)/shard_map/ppermute | solution.py:35
  112.3 16.8 %collective-permute-start.15 = (f32[8,256]{1,0:T(8,128)S(1)}, f32[8,256]{1,0:T(8,128)S(1)}, u32[]{:S(2)}, u32[]{:S(2)}) collective-permute-start(f32[8,256]{1,0:T(8,128)S(1)} %merge.1.own.refs_1_), channel_id=1, source_target_pairs={{0,2},{1,5},{2,4},{3,7},{4,6},{5,9},{6,8},{7,11},{8,10},{9,13},{10... | collective-permute-start | bytes 24584 | tf_op jit(solution)/shard_map/ppermute | solution.py:30
  114.3 14.7 %collective-permute-start.13 = (f32[8,256]{1,0:T(8,128)S(1)}, f32[8,256]{1,0:T(8,128)S(1)}, u32[]{:S(2)}, u32[]{:S(2)}) collective-permute-start(f32[8,256]{1,0:T(8,128)S(1)} %merge.1.own.refs_1_), channel_id=1, source_target_pairs={{0,254},{1,253},{2,0},{3,255},{4,2},{5,1},{6,4},{7,3},{8,6},{9,5},... | collective-permute-start | bytes 24584 | tf_op jit(solution)/shard_map/ppermute | solution.py:30
  124.5 5.1 %collective-permute-start.12 = (f32[8,128]{1,0:T(8,128)S(1)}, f32[8,128]{1,0:T(8,128)S(1)}, u32[]{:S(2)}, u32[]{:S(2)}) collective-permute-start(f32[8,128]{1,0:T(8,128)S(1)} %pair.1.refs_0_), channel_id=1, source_target_pairs={{0,4},{1,5},{2,6},{3,7},{4,0},{5,1},{6,2},{7,3},{8,12},{9,13},{10,... | collective-permute-start | bytes 12296 | tf_op jit(solution)/shard_map/ppermute | solution.py:35
  129.0 9.2 %collective-permute-start.14 = (f32[8,256]{1,0:T(8,128)S(1)}, f32[8,256]{1,0:T(8,128)S(1)}, u32[]{:S(2)}, u32[]{:S(2)}) collective-permute-start(f32[8,256]{1,0:T(8,128)S(1)} %collective-permute-done.13.v), channel_id=1, source_target_pairs={{0,1},{1,0},{2,3},{3,2},{4,5},{5,4},{6,7},{7,6},{8,9},{9,8},{10,11... | collective-permute-start | bytes 24584 | tf_op jit(solution)/shard_map/ppermute | solution.py:35
  129.1 9.1 %collective-permute-start.16 = (f32[8,256]{1,0:T(8,128)S(1)}, f32[8,256]{1,0:T(8,128)S(1)}, u32[]{:S(2)}, u32[]{:S(2)}) collective-permute-start(f32[8,256]{1,0:T(8,128)S(1)} %collective-permute-done.15.u), channel_id=1, source_target_pairs={{0,1},{1,0},{2,3},{3,2},{4,5},{5,4},{6,7},{7,6},{8,9},{9,8},{10,11... | collective-permute-start | bytes 24584 | tf_op jit(solution)/shard_map/ppermute | solution.py:35
  130.2 11.2 %collective-permute-start.17 = (f32[8,128]{1,0:T(8,128)S(1)}, f32[8,128]{1,0:T(8,128)S(1)}, u32[]{:S(2)}, u32[]{:S(2)}) collective-permute-start(f32[8,128]{1,0:T(8,128)S(1)} %sum.4.refs_0_), channel_id=1, source_target_pairs={{0,16},{1,17},{2,18},{3,19},{4,20},{5,21},{6,22},{7,23},{8,24},{9,... | collective-permute-start | bytes 12296 | tf_op jit(solution)/shard_map/ppermute | solution.py:35
  141.9 7.8 %collective-permute-start.21 = (f32[256,1280]{1,0:T(8,128)S(1)}, f32[256,1280]{1,0:T(8,128)S(1)}, u32[]{:S(2)}, u32[]{:S(2)}) collective-permute-start(f32[256,1280]{1,0:T(8,128)S(1)} %image_share.1), channel_id=1, source_target_pairs={{0,1},{1,0},{2,3},{3,2},{4,5},{5,4},{6,7},{7,6},{8,9},{9,8},{10,11... | collective-permute-start | bytes 3932168 | tf_op jit(solution)/shard_map/ppermute | solution.py:35
  142.0 6.7 %collective-permute-start.20 = (f32[8,128]{1,0:T(8,128)S(1)}, f32[8,128]{1,0:T(8,128)S(1)}, u32[]{:S(2)}, u32[]{:S(2)}) collective-permute-start(f32[8,128]{1,0:T(8,128)S(1)} %sum.5.refs_0_), channel_id=1, source_target_pairs={{0,192},{1,193},{2,194},{3,195},{4,196},{5,197},{6,198},{7,199},{8... | collective-permute-start | bytes 12296 | tf_op jit(solution)/shard_map/ppermute | solution.py:35
  142.1 6.6 %collective-permute-start.19 = (f32[8,128]{1,0:T(8,128)S(1)}, f32[8,128]{1,0:T(8,128)S(1)}, u32[]{:S(2)}, u32[]{:S(2)}) collective-permute-start(f32[8,128]{1,0:T(8,128)S(1)} %sum.5.refs_0_), channel_id=1, source_target_pairs={{0,128},{1,129},{2,130},{3,131},{4,132},{5,133},{6,134},{7,135},{8... | collective-permute-start | bytes 12296 | tf_op jit(solution)/shard_map/ppermute | solution.py:35
  142.2 6.5 %collective-permute-start.18 = (f32[8,128]{1,0:T(8,128)S(1)}, f32[8,128]{1,0:T(8,128)S(1)}, u32[]{:S(2)}, u32[]{:S(2)}) collective-permute-start(f32[8,128]{1,0:T(8,128)S(1)} %sum.5.refs_0_), channel_id=1, source_target_pairs={{0,64},{1,65},{2,66},{3,67},{4,68},{5,69},{6,70},{7,71},{8,72},{9,... | collective-permute-start | bytes 12296 | tf_op jit(solution)/shard_map/ppermute | solution.py:35
  149.2 8.6 %collective-permute-start.23 = (f32[256,1280]{1,0:T(8,128)S(1)}, f32[256,1280]{1,0:T(8,128)S(1)}, u32[]{:S(2)}, u32[]{:S(2)}) collective-permute-start(f32[256,1280]{1,0:T(8,128)S(1)} %text_share.1), channel_id=1, source_target_pairs={{0,1},{1,0},{2,3},{3,2},{4,5},{5,4},{6,7},{7,6},{8,9},{9,8},{10,11... | collective-permute-start | bytes 3932168 | tf_op jit(solution)/shard_map/ppermute | solution.py:35
  149.3 7.8 %collective-permute-start.22 = (f32[8,128]{1,0:T(8,128)S(1)}, f32[8,128]{1,0:T(8,128)S(1)}, u32[]{:S(2)}, u32[]{:S(2)}) collective-permute-start(f32[8,128]{1,0:T(8,128)S(1)} %sum.6.refs_0_), channel_id=1, source_target_pairs={{0,8},{1,9},{2,10},{3,11},{4,12},{5,13},{6,14},{7,15},{8,0},{9,1},... | collective-permute-start | bytes 12296 | tf_op jit(solution)/shard_map/ppermute | solution.py:35
  157.7 5.2 %collective-permute-start.24 = (f32[8,128]{1,0:T(8,128)S(1)}, f32[8,128]{1,0:T(8,128)S(1)}, u32[]{:S(2)}, u32[]{:S(2)}) collective-permute-start(f32[8,128]{1,0:T(8,128)S(1)} %sum.7.refs_0_), channel_id=1, source_target_pairs={{0,32},{1,33},{2,34},{3,35},{4,36},{5,37},{6,38},{7,39},{8,40},{9,... | collective-permute-start | bytes 12296 | tf_op jit(solution)/shard_map/ppermute | solution.py:35

commit v6 on v5

--- a/solution.py
+++ b/solution.py
@@ -369,13 +369,13 @@
     (own,) = call(merge_kernel, "merge", 0.6, [((8, n), F32)], (s, mine, got))
     u, v = along(own, 1), along(own, -1)
     terms = [((8, 128), F32)]
-    (parts,) = call(pair_kernel, "pair", 0.5, terms, (s, own, swap(own, 2)))
+    (parts,) = call(pair_kernel, "pair", 0.5, terms, (s, own, swap(own, 16)))
 
     def add(parts, bits, *done):
         args = s, after(parts, *done), *(swap(parts, b) for b in bits)
         return call(sum_kernel, "sum", 0.5, terms, args)[0]
 
-    parts = add(parts, (4,))
+    parts = add(parts, (32,))
     args = s, own, l0, v0, *t_parts, *i_parts
     firsts = [((2 * n, depth), F32)] * 2
     w_part = [((2 * n, n), BF16)] * 2
@@ -389,7 +389,7 @@
     final = [block, pltpu.SemaphoreType.DMA((depth // TILE,))]
     kernel = functools.partial(share_kernel, False)
     (share,) = call(kernel, "image_share", 3.1, [block], (s, own, lses, *image_args), weights)
-    parts = add(parts, (16,), share)
+    parts = add(parts, (2,), share)
     image_share = swap(after(share, parts))
     kernel = functools.partial(share_kernel, True)
     args = s, after(own, parts), lses, *text_args
@@ -404,11 +404,11 @@
     (image_grad,) = call(kernel, "image_grads", 3.9, [block], args, final, out_hbm=(0,))
     args = s, after(parts, image_grad), far_part
     (parts,) = call(sum_kernel, "sum", 0.5, terms, args)
-    y_part = swap(parts, 32)
+    last_part = swap(parts, 4)
     kernel = functools.partial(grads_kernel, True)
     args = s, after(own, parts), lses, *text_args, text_share
     (text_grad,) = call(kernel, "text_grads", 3.9, [block], args, final, out_hbm=(0,))
-    args = s, after(parts, text_grad), y_part
+    args = s, after(parts, text_grad), last_part
     loss, scale_grad = call(last_kernel, "last", 0.5, [((1, 1), F32)] * 2, args)
     return (loss.reshape(()), image_grad, text_grad, scale_grad.reshape(()))
 

time: 168 us -> 167 us (level)
  the two profiles are of different devices: /device:TPU:8 before, /device:TPU:32 now
where the time goes in v6:
time: 167 us; the launch traced here: 164 us
  starting transfers between devices  60.2 us (36%)
  Pallas kernels  49.6 us (30%)
  waiting for transfers between devices  49.5 us (30%)
  local copies, waits for them, and re-layouts  2.63 us (2%)
  between operations  1.8 us (1%)
    pallas_call x22, Pallas kernels, call(): pl.pallas_call(kernel, name=name, out_shape=[jax.ShapeDtypeStruct(s, d) f...  49.6 us
    ppermute x8, waiting for transfers between devices, shift(): return lax.ppermute(value, 'dp', pairs)  43.5 us
    ppermute x8, starting transfers between devices, shift(): return lax.ppermute(value, 'dp', pairs)  28.6 us
    ppermute x15, starting transfers between devices, swap(): return lax.ppermute(value, 'dp', [(s, s ^ bit) for s in range(count)])  16.8 us
    ppermute x2, starting transfers between devices, along(): return lax.ppermute(value, 'dp', pairs)  14.8 us
    ppermute x15, waiting for transfers between devices, swap(): return lax.ppermute(value, 'dp', [(s, s ^ bit) for s in range(count)])  5.99 us
  transfers between devices with their start and end apart: 25, of which 9 were waited for; matrix products, arithmetic and copies ran while one was open for 0% of the time, Pallas kernels for 28%

profile of v6, /device:TPU:32, one launch (start us, length us, event | category | flops | bytes accessed | tf_op | source)
XLA Modules:
  0.0 163.9 jit_solution(1224635579936941699)
XLA Ops:
  0.7 0.5 collective-permute-start.1
  1.2 1.9 %collective-permute-start.4 = (f32[256,1280]{1,0:T(8,128)}, f32[256,1280]{1,0:T(8,128)S(1)}, u32[]{:S(2)}, u32[]{:S(2)}) collective-permute-start(f32[256,1280]{1,0:T(8,128)} %b0.6), channel_id=1, source_target_pairs={{0,2},{1,3},{2,4},{3,5},{4,6},{5,7},{6,8},{7,9},{8,10},{9,11},{10,... | collective-permute-start | bytes 3932168 | tf_op jit(solution)/shard_map/ppermute | solution.py:24
  3.3 8.6 %collective-permute-start.2 = (f32[256,1280]{1,0:T(8,128)}, f32[256,1280]{1,0:T(8,128)S(1)}, u32[]{:S(2)}, u32[]{:S(2)}) collective-permute-start(f32[256,1280]{1,0:T(8,128)} %b0.7), channel_id=1, source_target_pairs={{0,254},{1,255},{2,0},{3,1},{4,2},{5,3},{6,4},{7,5},{8,6},{9,7},{1... | collective-permute-start | bytes 3932168 | tf_op jit(solution)/shard_map/ppermute | solution.py:24
  12.6 1.3 copy-done
  13.9 1.3 copy-done.1
  15.3 3.7 %text_own.1 = (bf16[512,1280]{1,0:T(8,128)(2,1)S(1)}, bf16[512,1280]{1,0:T(8,128)(2,1)S(1)}, bf16[512,1280]{1,0:T(8,128)(2,1)S(1)}, f32[512,256]{1,0:T(8,128)S(1)}) custom-call(f32[3]{0:T(128)S(1)} %pad_maximum_fusion.s.refs_0_, f32[256,1280]{1,0:T(8,128)S(1)} %copy-done.1, f32[256,1280]{1,0:T(8,128)} %collective-permute-done.1.a1, f32[256,1280]{1,0:T(8,128)S(1)} %copy-done), custom_call_target="tpu_custom_call" | custom-call | flops 4255000064 | bytes 1 | tf_op jit(solution)/shard_map/text_own/pallas_call | solution.py:43
  19.0 3.6 %image_own.1 = (bf16[512,1280]{1,0:T(8,128)(2,1)S(1)}, bf16[512,1280]{1,0:T(8,128)(2,1)S(1)}, bf16[512,1280]{1,0:T(8,128)(2,1)S(1)}, f32[512,256]{1,0:T(8,128)S(1)}) custom-call(f32[3]{0:T(128)S(1)} %pad_maximum_fusion.s.refs_0_, f32[256,1280]{1,0:T(8,128)S(1)} %copy-done, f32[256,1280]{1,0:T(8,128)} %collective-permute-done.a1, f32[256,1280]{1,0:T(8,128)S(1)} %copy-done.2), custom_call_target="tpu_custom_call" | custom-call | flops 4255000064 | bytes 1 | tf_op jit(solution)/shard_map/image_own/pallas_call | solution.py:43
  22.6 10.5 %collective-permute-done.4.bp = f32[256,1280]{1,0:T(8,128)S(1)} collective-permute-done((f32[256,1280]{1,0:T(8,128)}, f32[256,1280]{1,0:T(8,128)S(1)}, u32[]{:S(2)}, u32[]{:S(2)}) %collective-permute-start.4) | collective-permute-done | bytes 1310752 | tf_op jit(solution)/shard_map/ppermute | solution.py:24
  33.1 2.0 %collective-permute-done.3.bm = f32[256,1280]{1,0:T(8,128)} collective-permute-done((f32[256,1280]{1,0:T(8,128)}, f32[256,1280]{1,0:T(8,128)}, u32[]{:S(2)}, u32[]{:S(2)}) %collective-permute-start.3) | collective-permute-done | bytes 1310752 | tf_op jit(solution)/shard_map/ppermute | solution.py:24
  35.1 6.5 %collective-permute-start.8 = (f32[256,1280]{1,0:T(8,128)}, f32[256,1280]{1,0:T(8,128)S(1)}, u32[]{:S(2)}, u32[]{:S(2)}) collective-permute-start(f32[256,1280]{1,0:T(8,128)} %collective-permute-done.3.bm), channel_id=1, source_target_pairs={{0,254},{1,255},{2,0},{3,1},{4,2},{5,3},{6,4},{7,5},{8,6},{9,7},{1... | collective-permute-start | bytes 3932168 | tf_op jit(solution)/shard_map/ppermute | solution.py:24
  41.6 1.0 collective-permute-start.9
  42.6 6.0 %text_near.1 = (f32[512,256]{1,0:T(8,128)S(1)}, f32[512,256]{1,0:T(8,128)S(1)}, bf16[1280,1280]{1,0:T(8,128)(2,1)S(1)}, bf16[1280,1280]{1,0:T(8,128)(2,1)S(1)}) custom-call(f32[3]{0:T(128)S(1)} %pad_maximum_fusion.s.refs_0_, bf16[512,1280]{1,0:T(8,128)(2,1)S(1)} %get-tuple-element.66.h.xh, bf16[512,1280]{1,0:T(8,128)(2,1)S(1)} %get-tuple-element.67.m.xm, ...), custom_call_target="tpu_custom_call" | custom-call | flops 5520000000 | bytes 1 | tf_op jit(solution)/shard_map/text_near/pallas_call | solution.py:43
  48.6 1.3 text_stats.1
  49.9 11.2 %collective-permute-done.6.bp = f32[256,1280]{1,0:T(8,128)S(1)} collective-permute-done((f32[256,1280]{1,0:T(8,128)}, f32[256,1280]{1,0:T(8,128)S(1)}, u32[]{:S(2)}, u32[]{:S(2)}) %collective-permute-start.6) | collective-permute-done | bytes 1310752 | tf_op jit(solution)/shard_map/ppermute | solution.py:24
  61.1 1.9 %collective-permute-start.7 = (f32[256,1280]{1,0:T(8,128)S(1)}, f32[256,1280]{1,0:T(8,128)S(1)}, u32[]{:S(2)}, u32[]{:S(2)}) collective-permute-start(f32[256,1280]{1,0:T(8,128)S(1)} %collective-permute-done.6.bp), channel_id=1, source_target_pairs={{0,2},{1,3},{2,4},{3,5},{4,6},{5,7},{6,8},{7,9},{8,10},{9,11},{10,... | collective-permute-start | bytes 3932168 | tf_op jit(solution)/shard_map/ppermute | solution.py:24
  63.1 8.5 %collective-permute-start.5 = (f32[256,1280]{1,0:T(8,128)S(1)}, f32[256,1280]{1,0:T(8,128)S(1)}, u32[]{:S(2)}, u32[]{:S(2)}) collective-permute-start(f32[256,1280]{1,0:T(8,128)S(1)} %collective-permute-done.2.bm), channel_id=1, source_target_pairs={{0,254},{2,0},{4,2},{6,4},{8,6},{10,8},{12,10},{14,12},{16,14},{18... | collective-permute-start | bytes 3932168 | tf_op jit(solution)/shard_map/ppermute | solution.py:24
  71.6 5.2 %image_near.1 = (f32[512,256]{1,0:T(8,128)S(1)}, f32[512,256]{1,0:T(8,128)S(1)}, bf16[1280,1280]{1,0:T(8,128)(2,1)S(1)}, bf16[1280,1280]{1,0:T(8,128)(2,1)S(1)}) custom-call(f32[3]{0:T(128)S(1)} %pad_maximum_fusion.s.refs_0_, bf16[512,1280]{1,0:T(8,128)(2,1)S(1)} %get-tuple-element.63.h.yh, bf16[512,1280]{1,0:T(8,128)(2,1)S(1)} %get-tuple-element.64.m.ym, ...), custom_call_target="tpu_custom_call" | custom-call | flops 5520000000 | bytes 1 | tf_op jit(solution)/shard_map/image_near/pallas_call | solution.py:43
  76.9 1.9 %image_stats.1 = (f32[512,128]{1,0:T(8,128)S(1)}, f32[512,128]{1,0:T(8,128)S(1)}, f32[1,256]{1,0:T(1,128)}) custom-call(f32[3]{0:T(128)S(1)} %pad_maximum_fusion.s.refs_0_, f32[512,256]{1,0:T(8,128)S(1)} %get-tuple-element.69.l0.v0, f32[512,256]{1,0:T(8,128)S(1)} %get-tuple-element.77.lp.refs_3_, f32[512,256]{1,0:T(8,128)S(1)} %get-tuple-element.78.lm.refs_4_), custom_call_target="tpu_custom_call" | custom-call | flops 2070000000 | bytes 1 | tf_op jit(solution)/shard_map/image_stats/pallas_call | solution.py:43
  78.7 11.5 %collective-permute-done.8.a = f32[256,1280]{1,0:T(8,128)S(1)} collective-permute-done((f32[256,1280]{1,0:T(8,128)}, f32[256,1280]{1,0:T(8,128)S(1)}, u32[]{:S(2)}, u32[]{:S(2)}) %collective-permute-start.8) | collective-permute-done | bytes 1310752 | tf_op jit(solution)/shard_map/ppermute | solution.py:24
  90.2 3.6 %text_far.1 = (f32[512,256]{1,0:T(8,128)S(1)}, f32[4,256]{1,0:T(4,128)S(1)}, bf16[1280,1280]{1,0:T(8,128)(2,1)S(1)}, bf16[1280,1280]{1,0:T(8,128)(2,1)S(1)}) custom-call(f32[3]{0:T(128)S(1)} %pad_maximum_fusion.s.refs_0_, bf16[512,1280]{1,0:T(8,128)(2,1)S(1)} %get-tuple-element.66.h.xh, ...), custom_call_target="tpu_custom_call", output_to_operand_aliasing={{2}: (8, {}), {3}: (9, {})} | custom-call | flops 4600000000 | bytes 1 | tf_op jit(solution)/shard_map/text_far/pallas_call | solution.py:43
  93.8 5.5 %collective-permute-done.7.block = f32[256,1280]{1,0:T(8,128)S(1)} collective-permute-done((f32[256,1280]{1,0:T(8,128)S(1)}, f32[256,1280]{1,0:T(8,128)S(1)}, u32[]{:S(2)}, u32[]{:S(2)}) %collective-permute-start.7) | collective-permute-done | bytes 1310752 | tf_op jit(solution)/shard_map/ppermute | solution.py:24
  99.4 2.2 %image_behind.1 = (f32[512,256]{1,0:T(8,128)S(1)}, f32[16,256]{1,0:T(8,128)S(1)}, bf16[1280,1280]{1,0:T(8,128)(2,1)S(1)}, bf16[1280,1280]{1,0:T(8,128)(2,1)S(1)}) custom-call(f32[3]{0:T(128)S(1)} %pad_maximum_fusion.s.refs_0_, bf16[512,1280]{1,0:T(8,128)(2,1)S(1)} %get-tuple-element.63.h.yh, ...), custom_call_target="tpu_custom_call", output_to_operand_aliasing={{2}: (7, {}), {3}: (8, {})} | custom-call | flops 3449999872 | bytes 1 | tf_op jit(solution)/shard_map/image_behind/pallas_call | solution.py:43
  101.6 2.7 %collective-permute-done.5.block = f32[256,1280]{1,0:T(8,128)S(1)} collective-permute-done((f32[256,1280]{1,0:T(8,128)S(1)}, f32[256,1280]{1,0:T(8,128)S(1)}, u32[]{:S(2)}, u32[]{:S(2)}) %collective-permute-start.5) | collective-permute-done | bytes 1310752 | tf_op jit(solution)/shard_map/ppermute | solution.py:24
  104.3 2.2 %image_ahead.1 = (f32[512,256]{1,0:T(8,128)S(1)}, f32[16,256]{1,0:T(8,128)S(1)}, bf16[1280,1280]{1,0:T(8,128)(2,1)S(1)}, bf16[1280,1280]{1,0:T(8,128)(2,1)S(1)}) custom-call(f32[3]{0:T(128)S(1)} %pad_maximum_fusion.s.refs_0_, bf16[512,1280]{1,0:T(8,128)(2,1)S(1)} %get-tuple-element.63.h.yh, ...), custom_call_target="tpu_custom_call", output_to_operand_aliasing={{2}: (7, {}), {3}: (8, {}), {0}: (9, {}), {1}: (10, {})} | custom-call | flops 2300000000 | bytes 1 | tf_op jit(solution)/shard_map/image_ahead/pallas_call | solution.py:43
  106.5 0.6 collective-permute-start.10
  107.2 0.8 collective-permute-done.10.got
  108.0 0.6 merge.1.own.refs_1_
  108.7 1.5 collective-permute-start.11
  110.2 3.0 %collective-permute-start.15 = (f32[8,256]{1,0:T(8,128)S(1)}, f32[8,256]{1,0:T(8,128)S(1)}, u32[]{:S(2)}, u32[]{:S(2)}) collective-permute-start(f32[8,256]{1,0:T(8,128)S(1)} %merge.1.own.refs_1_), channel_id=1, source_target_pairs={{0,2},{1,5},{2,4},{3,7},{4,6},{5,9},{6,8},{7,11},{8,10},{9,13},{10... | collective-permute-start | bytes 24584 | tf_op jit(solution)/shard_map/ppermute | solution.py:30
  113.1 11.9 %collective-permute-start.13 = (f32[8,256]{1,0:T(8,128)S(1)}, f32[8,256]{1,0:T(8,128)S(1)}, u32[]{:S(2)}, u32[]{:S(2)}) collective-permute-start(f32[8,256]{1,0:T(8,128)S(1)} %merge.1.own.refs_1_), channel_id=1, source_target_pairs={{0,254},{1,253},{2,0},{3,255},{4,2},{5,1},{6,4},{7,3},{8,6},{9,5},... | collective-permute-start | bytes 24584 | tf_op jit(solution)/shard_map/ppermute | solution.py:30
  125.0 0.5 pair.1.refs_0_
  125.7 3.1 %own_blocks.1 = (f32[512,1280]{1,0:T(8,128)S(1)}, f32[512,1280]{1,0:T(8,128)S(1)}) custom-call(f32[3]{0:T(128)S(1)} %pad_maximum_fusion.s.refs_0_, f32[8,256]{1,0:T(8,128)S(1)} %merge.1.own.refs_1_, f32[512,256]{1,0:T(8,128)S(1)} %get-tuple-element.61.l0, f32[512,256]{1,0:T(8,128)S(1)} %get-tuple-element.69.l0.v0, ...), custom_call_target="tpu_custom_call" | custom-call | flops 3449999872 | bytes 1 | tf_op jit(solution)/shard_map/own_blocks/pallas_call | solution.py:43
  128.7 4.9 %collective-permute-start.14 = (f32[8,256]{1,0:T(8,128)S(1)}, f32[8,256]{1,0:T(8,128)S(1)}, u32[]{:S(2)}, u32[]{:S(2)}) collective-permute-start(f32[8,256]{1,0:T(8,128)S(1)} %collective-permute-done.13.v), channel_id=1, source_target_pairs={{0,1},{1,0},{2,3},{3,2},{4,5},{5,4},{6,7},{7,6},{8,9},{9,8},{10,11... | collective-permute-start | bytes 24584 | tf_op jit(solution)/shard_map/ppermute | solution.py:35
  133.7 0.5 sum.4.refs_0_
  134.3 4.2 %collective-permute-start.17 = (f32[8,128]{1,0:T(8,128)S(1)}, f32[8,128]{1,0:T(8,128)S(1)}, u32[]{:S(2)}, u32[]{:S(2)}) collective-permute-start(f32[8,128]{1,0:T(8,128)S(1)} %sum.4.refs_0_), channel_id=1, source_target_pairs={{0,2},{1,3},{2,0},{3,1},{4,6},{5,7},{6,4},{7,5},{8,10},{9,11},{10,... | collective-permute-start | bytes 12296 | tf_op jit(solution)/shard_map/ppermute | solution.py:35
  138.5 0.6 sort.1.refs_2_
  139.1 2.5 %image_share.1 = f32[256,1280]{1,0:T(8,128)S(1)} custom-call(f32[3]{0:T(128)S(1)} %pad_maximum_fusion.s.refs_0_, f32[8,256]{1,0:T(8,128)S(1)} %merge.1.own.refs_1_, f32[8,256]{1,0:T(8,128)S(1)} %sort.1.refs_2_, f32[512,256]{1,0:T(8,128)S(1)} %get-tuple-element.72.lp.refs_3_, f32[512,256]{1,0:T(8,128)S(1)} %get-tuple-element.73.lm.refs_4_, ...), custom_call_target="tpu_custom_call" | custom-call | flops 3564999936 | bytes 1 | tf_op jit(solution)/shard_map/image_share/pallas_call | solution.py:43
  141.6 0.5 sum.5.refs_0_
  142.4 4.0 %collective-permute-start.18 = (f32[8,128]{1,0:T(8,128)S(1)}, f32[8,128]{1,0:T(8,128)S(1)}, u32[]{:S(2)}, u32[]{:S(2)}) collective-permute-start(f32[8,128]{1,0:T(8,128)S(1)} %sum.5.refs_0_), channel_id=1, source_target_pairs={{0,64},{1,65},{2,66},{3,67},{4,68},{5,69},{6,70},{7,71},{8,72},{9,... | collective-permute-start | bytes 12296 | tf_op jit(solution)/shard_map/ppermute | solution.py:35
  146.4 2.5 %text_share.1 = f32[256,1280]{1,0:T(8,128)S(1)} custom-call(f32[3]{0:T(128)S(1)} %pad_maximum_fusion.s.refs_0_, f32[8,256]{1,0:T(8,128)S(1)} %merge.1.own.refs_1_, f32[8,256]{1,0:T(8,128)S(1)} %sort.1.refs_2_, f32[512,256]{1,0:T(8,128)S(1)} %get-tuple-element.77.lp.refs_3_, f32[512,256]{1,0:T(8,128)S(1)} %get-tuple-element.78.lm.refs_4_, ...), custom_call_target="tpu_custom_call" | custom-call | flops 3564999936 | bytes 1 | tf_op jit(solution)/shard_map/text_share/pallas_call | solution.py:43
  148.9 0.5 sum.6.refs_0_
  149.6 0.3 collective-permute-start.22
  149.9 3.4 %image_grads.1 = f32[256,1280]{1,0:T(8,128)} custom-call(f32[3]{0:T(128)S(1)} %pad_maximum_fusion.s.refs_0_, f32[8,256]{1,0:T(8,128)S(1)} %merge.1.own.refs_1_, f32[8,256]{1,0:T(8,128)S(1)} %sort.1.refs_2_, f32[512,256]{1,0:T(8,128)S(1)} %get-tuple-element.72.lp.refs_3_, f32[512,256]{1,0:T(8,128)S(1)} %get-tuple-element.73.lm.refs_4_, ...), custom_call_target="tpu_custom_call" | custom-call | flops 4485000192 | bytes 1 | tf_op jit(solution)/shard_map/image_grads/pallas_call | solution.py:43
  153.3 4.1 %collective-permute-done.22.refs_1_ = f32[8,128]{1,0:T(8,128)S(1)} collective-permute-done((f32[8,128]{1,0:T(8,128)S(1)}, f32[8,128]{1,0:T(8,128)S(1)}, u32[]{:S(2)}, u32[]{:S(2)}) %collective-permute-start.22) | collective-permute-done | bytes 4128 | tf_op jit(solution)/shard_map/ppermute | solution.py:35
  157.4 0.5 sum.7.refs_0_
  158.1 3.5 %text_grads.1 = f32[256,1280]{1,0:T(8,128)} custom-call(f32[3]{0:T(128)S(1)} %pad_maximum_fusion.s.refs_0_, f32[8,256]{1,0:T(8,128)S(1)} %merge.1.own.refs_1_, f32[8,256]{1,0:T(8,128)S(1)} %sort.1.refs_2_, f32[512,256]{1,0:T(8,128)S(1)} %get-tuple-element.77.lp.refs_3_, f32[512,256]{1,0:T(8,128)S(1)} %get-tuple-element.78.lm.refs_4_, ...), custom_call_target="tpu_custom_call" | custom-call | flops 4485000192 | bytes 1 | tf_op jit(solution)/shard_map/text_grads/pallas_call | solution.py:43
  161.6 1.0 collective-permute-done.24.refs_1_
  162.6 1.1 last.1
  (31 shorter events, 1.1 us)
Async XLA Ops:
  0.6 11.9 %collective-permute-start = (f32[256,1280]{1,0:T(8,128)}, f32[256,1280]{1,0:T(8,128)}, u32[]{:S(2)}, u32[]{:S(2)}) collective-permute-start(f32[256,1280]{1,0:T(8,128)} %b0.6), channel_id=1, source_target_pairs={{0,1},{1,0},{2,3},{3,2},{4,5},{5,4},{6,7},{7,6},{8,9},{9,8},{10,11... | collective-permute-start | bytes 3932168 | tf_op jit(solution)/shard_map/ppermute | solution.py:35
  0.7 11.9 %collective-permute-start.1 = (f32[256,1280]{1,0:T(8,128)}, f32[256,1280]{1,0:T(8,128)}, u32[]{:S(2)}, u32[]{:S(2)}) collective-permute-start(f32[256,1280]{1,0:T(8,128)} %b0.7), channel_id=1, source_target_pairs={{0,1},{1,0},{2,3},{3,2},{4,5},{5,4},{6,7},{7,6},{8,9},{9,8},{10,11... | collective-permute-start | bytes 3932168 | tf_op jit(solution)/shard_map/ppermute | solution.py:35
  1.2 31.8 %collective-permute-start.4 = (f32[256,1280]{1,0:T(8,128)}, f32[256,1280]{1,0:T(8,128)S(1)}, u32[]{:S(2)}, u32[]{:S(2)}) collective-permute-start(f32[256,1280]{1,0:T(8,128)} %b0.6), channel_id=1, source_target_pairs={{0,2},{1,3},{2,4},{3,5},{4,6},{5,7},{6,8},{7,9},{8,10},{9,11},{10,... | collective-permute-start | bytes 3932168 | tf_op jit(solution)/shard_map/ppermute | solution.py:24
  3.1 32.0 %collective-permute-start.3 = (f32[256,1280]{1,0:T(8,128)}, f32[256,1280]{1,0:T(8,128)}, u32[]{:S(2)}, u32[]{:S(2)}) collective-permute-start(f32[256,1280]{1,0:T(8,128)} %b0.6), channel_id=1, source_target_pairs={{0,254},{1,255},{2,0},{3,1},{4,2},{5,3},{6,4},{7,5},{8,6},{9,7},{1... | collective-permute-start | bytes 3932168 | tf_op jit(solution)/shard_map/ppermute | solution.py:24
  3.3 59.8 %collective-permute-start.2 = (f32[256,1280]{1,0:T(8,128)}, f32[256,1280]{1,0:T(8,128)S(1)}, u32[]{:S(2)}, u32[]{:S(2)}) collective-permute-start(f32[256,1280]{1,0:T(8,128)} %b0.7), channel_id=1, source_target_pairs={{0,254},{1,255},{2,0},{3,1},{4,2},{5,3},{6,4},{7,5},{8,6},{9,7},{1... | collective-permute-start | bytes 3932168 | tf_op jit(solution)/shard_map/ppermute | solution.py:24
  12.6 48.6 %collective-permute-start.6 = (f32[256,1280]{1,0:T(8,128)}, f32[256,1280]{1,0:T(8,128)S(1)}, u32[]{:S(2)}, u32[]{:S(2)}) collective-permute-start(f32[256,1280]{1,0:T(8,128)} %b0.7), channel_id=1, source_target_pairs={{0,2},{1,3},{2,4},{3,5},{4,6},{5,7},{6,8},{7,9},{8,10},{9,11},{10,... | collective-permute-start | bytes 3932168 | tf_op jit(solution)/shard_map/ppermute | solution.py:24
  12.6 1.3 copy-start
  13.9 1.3 copy-start.1
  15.3 3.7 %copy-start.2 = (f32[256,1280]{1,0:T(8,128)S(1)}, f32[256,1280]{1,0:T(8,128)}, u32[]{:S(2)}) copy-start(f32[256,1280]{1,0:T(8,128)} %b0.7) | copy-start | bytes 3932164
  35.1 55.1 %collective-permute-start.8 = (f32[256,1280]{1,0:T(8,128)}, f32[256,1280]{1,0:T(8,128)S(1)}, u32[]{:S(2)}, u32[]{:S(2)}) collective-permute-start(f32[256,1280]{1,0:T(8,128)} %collective-permute-done.3.bm), channel_id=1, source_target_pairs={{0,254},{1,255},{2,0},{3,1},{4,2},{5,3},{6,4},{7,5},{8,6},{9,7},{1... | collective-permute-start | bytes 3932168 | tf_op jit(solution)/shard_map/ppermute | solution.py:24
  41.6 48.6 %collective-permute-start.9 = (f32[256,1280]{1,0:T(8,128)S(1)}, f32[256,1280]{1,0:T(8,128)S(1)}, u32[]{:S(2)}, u32[]{:S(2)}) collective-permute-start(f32[256,1280]{1,0:T(8,128)S(1)} %collective-permute-done.4.bp), channel_id=1, source_target_pairs={{1,3},{3,5},{5,7},{7,9},{9,11},{11,13},{13,15},{15,17},{17,19},{19... | collective-permute-start | bytes 3932168 | tf_op jit(solution)/shard_map/ppermute | solution.py:24
  61.1 38.3 %collective-permute-start.7 = (f32[256,1280]{1,0:T(8,128)S(1)}, f32[256,1280]{1,0:T(8,128)S(1)}, u32[]{:S(2)}, u32[]{:S(2)}) collective-permute-start(f32[256,1280]{1,0:T(8,128)S(1)} %collective-permute-done.6.bp), channel_id=1, source_target_pairs={{0,2},{1,3},{2,4},{3,5},{4,6},{5,7},{6,8},{7,9},{8,10},{9,11},{10,... | collective-permute-start | bytes 3932168 | tf_op jit(solution)/shard_map/ppermute | solution.py:24
  63.1 41.2 %collective-permute-start.5 = (f32[256,1280]{1,0:T(8,128)S(1)}, f32[256,1280]{1,0:T(8,128)S(1)}, u32[]{:S(2)}, u32[]{:S(2)}) collective-permute-start(f32[256,1280]{1,0:T(8,128)S(1)} %collective-permute-done.2.bm), channel_id=1, source_target_pairs={{0,254},{2,0},{4,2},{6,4},{8,6},{10,8},{12,10},{14,12},{16,14},{18... | collective-permute-start | bytes 3932168 | tf_op jit(solution)/shard_map/ppermute | solution.py:24
  106.5 1.5 collective-permute-start.10
  108.7 16.3 %collective-permute-start.11 = (f32[8,256]{1,0:T(8,128)S(1)}, f32[8,256]{1,0:T(8,128)S(1)}, u32[]{:S(2)}, u32[]{:S(2)}) collective-permute-start(f32[8,256]{1,0:T(8,128)S(1)} %merge.1.own.refs_1_), channel_id=1, source_target_pairs={{0,16},{1,17},{2,18},{3,19},{4,20},{5,21},{6,22},{7,23},{8,24},{9,... | collective-permute-start | bytes 24584 | tf_op jit(solution)/shard_map/ppermute | solution.py:35
  110.2 23.5 %collective-permute-start.15 = (f32[8,256]{1,0:T(8,128)S(1)}, f32[8,256]{1,0:T(8,128)S(1)}, u32[]{:S(2)}, u32[]{:S(2)}) collective-permute-start(f32[8,256]{1,0:T(8,128)S(1)} %merge.1.own.refs_1_), channel_id=1, source_target_pairs={{0,2},{1,5},{2,4},{3,7},{4,6},{5,9},{6,8},{7,11},{8,10},{9,13},{10... | collective-permute-start | bytes 24584 | tf_op jit(solution)/shard_map/ppermute | solution.py:30
  113.1 15.6 %collective-permute-start.13 = (f32[8,256]{1,0:T(8,128)S(1)}, f32[8,256]{1,0:T(8,128)S(1)}, u32[]{:S(2)}, u32[]{:S(2)}) collective-permute-start(f32[8,256]{1,0:T(8,128)S(1)} %merge.1.own.refs_1_), channel_id=1, source_target_pairs={{0,254},{1,253},{2,0},{3,255},{4,2},{5,1},{6,4},{7,3},{8,6},{9,5},... | collective-permute-start | bytes 24584 | tf_op jit(solution)/shard_map/ppermute | solution.py:30
  125.5 8.2 %collective-permute-start.12 = (f32[8,128]{1,0:T(8,128)S(1)}, f32[8,128]{1,0:T(8,128)S(1)}, u32[]{:S(2)}, u32[]{:S(2)}) collective-permute-start(f32[8,128]{1,0:T(8,128)S(1)} %pair.1.refs_0_), channel_id=1, source_target_pairs={{0,32},{1,33},{2,34},{3,35},{4,36},{5,37},{6,38},{7,39},{8,40},{9,... | collective-permute-start | bytes 12296 | tf_op jit(solution)/shard_map/ppermute | solution.py:35
  128.7 9.8 %collective-permute-start.14 = (f32[8,256]{1,0:T(8,128)S(1)}, f32[8,256]{1,0:T(8,128)S(1)}, u32[]{:S(2)}, u32[]{:S(2)}) collective-permute-start(f32[8,256]{1,0:T(8,128)S(1)} %collective-permute-done.13.v), channel_id=1, source_target_pairs={{0,1},{1,0},{2,3},{3,2},{4,5},{5,4},{6,7},{7,6},{8,9},{9,8},{10,11... | collective-permute-start | bytes 24584 | tf_op jit(solution)/shard_map/ppermute | solution.py:35
  133.6 4.9 %collective-permute-start.16 = (f32[8,256]{1,0:T(8,128)S(1)}, f32[8,256]{1,0:T(8,128)S(1)}, u32[]{:S(2)}, u32[]{:S(2)}) collective-permute-start(f32[8,256]{1,0:T(8,128)S(1)} %collective-permute-done.15.u), channel_id=1, source_target_pairs={{0,1},{1,0},{2,3},{3,2},{4,5},{5,4},{6,7},{7,6},{8,9},{9,8},{10,11... | collective-permute-start | bytes 24584 | tf_op jit(solution)/shard_map/ppermute | solution.py:35
  134.3 7.3 %collective-permute-start.17 = (f32[8,128]{1,0:T(8,128)S(1)}, f32[8,128]{1,0:T(8,128)S(1)}, u32[]{:S(2)}, u32[]{:S(2)}) collective-permute-start(f32[8,128]{1,0:T(8,128)S(1)} %sum.4.refs_0_), channel_id=1, source_target_pairs={{0,2},{1,3},{2,0},{3,1},{4,6},{5,7},{6,4},{7,5},{8,10},{9,11},{10,... | collective-permute-start | bytes 12296 | tf_op jit(solution)/shard_map/ppermute | solution.py:35
  142.1 7.8 %collective-permute-start.21 = (f32[256,1280]{1,0:T(8,128)S(1)}, f32[256,1280]{1,0:T(8,128)S(1)}, u32[]{:S(2)}, u32[]{:S(2)}) collective-permute-start(f32[256,1280]{1,0:T(8,128)S(1)} %image_share.1), channel_id=1, source_target_pairs={{0,1},{1,0},{2,3},{3,2},{4,5},{5,4},{6,7},{7,6},{8,9},{9,8},{10,11... | collective-permute-start | bytes 3932168 | tf_op jit(solution)/shard_map/ppermute | solution.py:35
  142.2 6.7 %collective-permute-start.20 = (f32[8,128]{1,0:T(8,128)S(1)}, f32[8,128]{1,0:T(8,128)S(1)}, u32[]{:S(2)}, u32[]{:S(2)}) collective-permute-start(f32[8,128]{1,0:T(8,128)S(1)} %sum.5.refs_0_), channel_id=1, source_target_pairs={{0,192},{1,193},{2,194},{3,195},{4,196},{5,197},{6,198},{7,199},{8... | collective-permute-start | bytes 12296 | tf_op jit(solution)/shard_map/ppermute | solution.py:35
  142.3 6.6 %collective-permute-start.19 = (f32[8,128]{1,0:T(8,128)S(1)}, f32[8,128]{1,0:T(8,128)S(1)}, u32[]{:S(2)}, u32[]{:S(2)}) collective-permute-start(f32[8,128]{1,0:T(8,128)S(1)} %sum.5.refs_0_), channel_id=1, source_target_pairs={{0,128},{1,129},{2,130},{3,131},{4,132},{5,133},{6,134},{7,135},{8... | collective-permute-start | bytes 12296 | tf_op jit(solution)/shard_map/ppermute | solution.py:35
  142.4 6.5 %collective-permute-start.18 = (f32[8,128]{1,0:T(8,128)S(1)}, f32[8,128]{1,0:T(8,128)S(1)}, u32[]{:S(2)}, u32[]{:S(2)}) collective-permute-start(f32[8,128]{1,0:T(8,128)S(1)} %sum.5.refs_0_), channel_id=1, source_target_pairs={{0,64},{1,65},{2,66},{3,67},{4,68},{5,69},{6,70},{7,71},{8,72},{9,... | collective-permute-start | bytes 12296 | tf_op jit(solution)/shard_map/ppermute | solution.py:35
  149.5 8.6 %collective-permute-start.23 = (f32[256,1280]{1,0:T(8,128)S(1)}, f32[256,1280]{1,0:T(8,128)S(1)}, u32[]{:S(2)}, u32[]{:S(2)}) collective-permute-start(f32[256,1280]{1,0:T(8,128)S(1)} %text_share.1), channel_id=1, source_target_pairs={{0,1},{1,0},{2,3},{3,2},{4,5},{5,4},{6,7},{7,6},{8,9},{9,8},{10,11... | collective-permute-start | bytes 3932168 | tf_op jit(solution)/shard_map/ppermute | solution.py:35
  149.6 7.8 %collective-permute-start.22 = (f32[8,128]{1,0:T(8,128)S(1)}, f32[8,128]{1,0:T(8,128)S(1)}, u32[]{:S(2)}, u32[]{:S(2)}) collective-permute-start(f32[8,128]{1,0:T(8,128)S(1)} %sum.6.refs_0_), channel_id=1, source_target_pairs={{0,8},{1,9},{2,10},{3,11},{4,12},{5,13},{6,14},{7,15},{8,0},{9,1},... | collective-permute-start | bytes 12296 | tf_op jit(solution)/shard_map/ppermute | solution.py:35
  158.0 4.6 %collective-permute-start.24 = (f32[8,128]{1,0:T(8,128)S(1)}, f32[8,128]{1,0:T(8,128)S(1)}, u32[]{:S(2)}, u32[]{:S(2)}) collective-permute-start(f32[8,128]{1,0:T(8,128)S(1)} %sum.7.refs_0_), channel_id=1, source_target_pairs={{0,4},{1,5},{2,6},{3,7},{4,0},{5,1},{6,2},{7,3},{8,12},{9,13},{10,... | collective-permute-start | bytes 12296 | tf_op jit(solution)/shard_map/ppermute | solution.py:35
